TPU v7x, 256 devices: a whole 4x4x8 slice. The times are simulated.
256 devices in a mesh: sup: 32 (over x, z), tm: 8 (over y, core).
Axes of the slice: x: 4, y: 4, z: 8, core: 2. Of those that a mesh axis runs over, the one named last changes fastest.
Arguments:
- factor: bfloat16 [8192, 8192], P('sup'), may hold values from -6 to 6, as said below
- white_noise: bfloat16 [8192, 16384], P('sup', 'tm'), may hold values from -6 to 6
- site_class: int32 [8192], replicated, may hold values from 0 to 3
- site_decay: float32 [2, 4], replicated, may hold values from 2e-05 to 0.02
- site_angle: float32 [2, 4], replicated, may hold values from 0.05 to 0.8
- site_mix: float32 [4, 4], replicated, may hold values from -3 to 3
Outputs:
- motions: float32 [8192, 16384], P('sup', 'tm')
Inputs may be any that keep to these rules, and one draw needn't show every extreme that they name: factor is zero above the diagonal and one on it.
All inputs are finite; a program needn't handle non-finite values.
Results may differ from a plain program's by a relative error of at most 0.0045.
Values may be sent and summed in bfloat16 or wider, within the bound.
No kernel may reach another device: no remote copies, remote signals or barrier semaphores. Data moves between devices by JAX's collectives and lax.ppermute only.
A program may use at most 128 MiB of HBM per device.

v0:
```python
import functools

import jax
import jax.numpy as jnp
from jax import lax
from jax.experimental import pallas as pl
from jax.experimental.pallas import tpu as pltpu
from jax.sharding import Mesh, PartitionSpec as P

CH = 256
NX, NZ, NY, NCORE = 4, 8, 4, 2
ROWS = 256
SLAB = 512
AWAY = (0, 7, 1, 6, 2, 5, 3)
VMEM_LIMIT = 58 * 1024 * 1024
F32 = jnp.float32
BF16 = jnp.bfloat16
PRECISE = lax.Precision.HIGHEST


def system(site_decay, site_angle, site_mix):
    radius = 1.0 - site_decay
    norm_gain = jnp.sqrt(site_decay * (2.0 - site_decay))
    cos_ground = radius[0] * jnp.cos(site_angle[0])
    sin_ground = radius[0] * jnp.sin(site_angle[0])
    cos_high = radius[1] * jnp.cos(site_angle[1])
    sin_high = radius[1] * jnp.sin(site_angle[1])
    zeros_row = jnp.zeros_like(cos_ground)
    ones_row = jnp.ones_like(cos_ground)
    mix_a, mix_b, out_a, out_b = (site_mix[0], site_mix[1], site_mix[2], site_mix[3])
    row_list = [
        [cos_ground, -sin_ground, zeros_row, zeros_row],
        [sin_ground, cos_ground, zeros_row, zeros_row],
        [
            norm_gain[0] * (mix_a * cos_ground + mix_b * sin_ground),
            norm_gain[0] * (mix_b * cos_ground - mix_a * sin_ground),
            cos_high,
            -sin_high,
        ],
        [zeros_row, zeros_row, sin_high, cos_high],
    ]
    matrix = jnp.stack([jnp.stack(entries, axis=-1) for entries in row_list], axis=1)
    entry_vec = jnp.stack([ones_row, zeros_row, norm_gain[0] * mix_a, zeros_row], axis=-1)
    readout = jnp.stack([zeros_row, zeros_row, norm_gain[1] * out_a, norm_gain[1] * out_b], axis=-1)
    return (matrix, entry_vec, readout)


def tables(site_decay, site_angle, site_mix):
    matrix, entry_vec, readout = system(site_decay, site_angle, site_mix)
    classes = matrix.shape[0]
    powers = matrix[None]
    while powers.shape[0] < CH:
        further = jnp.einsum("kab,jkbc->jkac", powers[-1], powers, precision=PRECISE)
        powers = jnp.concatenate([powers, further], axis=0)
    gains = jnp.einsum("ka,jkab->kbj", readout, powers, precision=PRECISE)
    responses = jnp.einsum("jkab,kb->kja", powers[: CH - 1], entry_vec, precision=PRECISE)
    responses = jnp.concatenate([entry_vec[:, None, :], responses], axis=1)
    impulse = jnp.einsum("ka,kma->km", readout, responses, precision=PRECISE)
    padded_len = 2 * CH
    padded = jnp.concatenate([impulse, jnp.zeros((classes, CH), F32)], axis=1)
    tiled = jnp.tile(padded, (1, CH))[:, : CH * (padded_len - 1)]
    toeplitz = tiled.reshape(classes, CH, padded_len - 1)[:, :, :CH]
    toeplitz = toeplitz.reshape(classes * CH, CH).astype(BF16)
    final = responses[:, ::-1, :].transpose(0, 2, 1).astype(BF16)
    final = jnp.concatenate([final, jnp.zeros_like(final)], axis=1).reshape(classes * 8, CH)
    gains = gains.reshape(classes * 4, CH)
    gains_hi = lax.reduce_precision(gains, 8, 7)
    gains_lo = (gains - gains_hi).astype(BF16)
    gains_hi = gains_hi.astype(BF16)
    gain_stack = jnp.concatenate([gains_hi, gains_lo, gains_hi], axis=0)
    power = powers[-1]
    twice = [power]
    for _ in range(3):
        twice.append(jnp.einsum("kab,kbc->kac", twice[-1], twice[-1], precision=PRECISE))
    return toeplitz, final, gain_stack, power, twice[1], twice[3]


def per_row(power, onehot):
    return jnp.sum(power.transpose(2, 1, 0)[:, :, :, None] * onehot[None, None], axis=2)


def apply_power(table, state):
    out = table[0] * state[0:1]
    for b in range(1, 4):
        out = out + table[b] * state[b : b + 1]
    return out


def load(zs, where, g_ref, noise, held, block, sems):
    waits = []
    for b, z in enumerate(where):
        copies = []
        for q in range(NX):
            columns = pl.ds(pl.multiple_of(q * NZ * CH + zs[z] * CH, CH), CH)
            copies.append(
                pltpu.make_async_copy(
                    g_ref.at[pl.ds(q, NX - q), :, columns], held[q].at[b], sems.at[b, q]
                )
            )
        for j, (ref, first, count, by, to, left) in enumerate(noise[b]):
            owner = lax.rem(zs[0] + NX - by, NX)
            copies.append(
                pltpu.make_async_copy(
                    ref.at[pl.ds(first, count)],
                    block.at[b, owner, pl.ds(to, count), pl.ds(left, CH)],
                    sems.at[b, NX + j],
                )
            )
        for copy in copies:
            copy.start()
        waits.append(copies)
    return waits


def term(held, block, b, s):
    parts = [held[q][b, s - q] for q in range(s + 1)]
    rows = jnp.concatenate(parts, axis=1) if s else parts[0]
    noise = block[b, 0 : s + 1].reshape((s + 1) * ROWS, SLAB)
    return jnp.dot(rows, noise, preferred_element_type=F32)


def product_kernel(zs, g_ref, *refs):
    count = 2 * len(AWAY)
    noise_refs, (out_ref, *held, block, sems) = refs[:count], refs[count:]
    noise = [
        [
            (noise_refs[2 * b + half], d * ROWS, ROWS, d, 0, half * CH)
            for half in range(2)
            for d in range(NX)
        ]
        for b in range(len(AWAY))
    ]
    waits = load(zs, range(1, 8), g_ref, noise, held, block, sems)
    for b in range(len(AWAY)):
        for copy in waits[b]:
            copy.wait()
        for s in range(NX):
            rows = pl.ds(s * ROWS, ROWS)
            value = term(held, block, b, s)
            out_ref[rows, :] = value if b == 0 else out_ref[rows, :] + value


def scratch(blocks):
    return [pltpu.VMEM((blocks, NX - q, ROWS, CH), BF16) for q in range(NX)] + [
        pltpu.VMEM((blocks, NX, ROWS, SLAB), BF16),
        pltpu.SemaphoreType.DMA((blocks, 4 * NX)),
    ]


def whole(a):
    return pl.BlockSpec(a.shape, lambda i, zs: (0,) * len(a.shape))


ANYWHERE = pl.BlockSpec(memory_space=pl.ANY)


def product(scalars, gathered, noise_blocks):
    out = jax.ShapeDtypeStruct((NX * ROWS, SLAB), F32)
    return pl.pallas_call(
        product_kernel,
        grid_spec=pltpu.PrefetchScalarGridSpec(
            num_scalar_prefetch=1,
            grid=(1,),
            in_specs=[ANYWHERE] * (1 + len(noise_blocks)),
            out_specs=whole(out),
            scratch_shapes=scratch(len(AWAY)),
        ),
        out_shape=out,
        compiler_params=pltpu.CompilerParams(vmem_limit_bytes=VMEM_LIMIT),
        cost_estimate=pl.CostEstimate(
            flops=7 * 2 * 10 * ROWS * CH * SLAB, bytes_accessed=19 * 1048576, transcendentals=0
        ),
    )(scalars, gathered, *noise_blocks)


def last_kernel(
    zs, g_ref, up_one, down_one, up_two, down_two, total_ref, final_ref, onehot_ref,
    power_ref, *refs,
):
    piece_refs, (send_ref, local, acc_ref, *held, block, sems) = refs[:NX], refs[NX:]
    noise = []
    for left, up, down in ((0, up_one, down_one), (CH, up_two, down_two)):
        for d in range(NX):
            noise.append(((up, down)[d // 2], d % 2 * ROWS, ROWS, d, 0, left))
    (waits,) = load(zs, (8,), g_ref, [noise], held, block, sems)
    fetch = []
    for s in range(NX):
        rows = pl.ds(s * ROWS, ROWS)
        fetch.append(
            pltpu.make_async_copy(total_ref.at[rows], acc_ref.at[rows], sems.at[0, 3 * NX + s])
        )
        fetch[s].start()
    for copy in waits[NX:]:
        copy.wait()
    for s in range(NX):
        waits[s].wait()
        fetch[s].wait()
        rows = pl.ds(s * ROWS, ROWS)
        local[s] = (acc_ref[rows, :] + term(held, block, 0, s)).astype(BF16)
    for d in range(NX):
        piece_refs[d][...] = local[lax.rem(zs[0] + d, NX)]
    for s in range(NX):
        rows = slice(s * ROWS, (s + 1) * ROWS)
        end = None
        for half in range(2):
            ends = lax.dot_general(
                final_ref[...], local[s, :, half * CH : (half + 1) * CH],
                (((1,), (1,)), ((), ())), preferred_element_type=F32,
            )
            picked = onehot_ref[0:1, rows] * ends[0:4]
            for k in range(1, 4):
                picked = picked + onehot_ref[k : k + 1, rows] * ends[k * 8 : k * 8 + 4]
            end = (
                apply_power([power_ref[b, :, rows] for b in range(4)], end) + picked
                if half
                else picked
            )
        for t in range(s, NY * NCORE * NX, NX):
            send_ref[t] = end


def last_product(scalars, gathered, noise, total, *args):
    out_shape = [jax.ShapeDtypeStruct((ROWS, SLAB), BF16)] * NX
    out_shape.append(jax.ShapeDtypeStruct((NY * NCORE * NX, 4, ROWS), F32))
    return pl.pallas_call(
        last_kernel,
        grid_spec=pltpu.PrefetchScalarGridSpec(
            num_scalar_prefetch=1,
            grid=(1,),
            in_specs=[ANYWHERE] * 6 + [whole(a) for a in args],
            out_specs=[whole(a) for a in out_shape],
            scratch_shapes=[
                pltpu.VMEM((NX, ROWS, SLAB), BF16),
                pltpu.VMEM((NX * ROWS, SLAB), F32),
                *scratch(1),
            ],
        ),
        out_shape=out_shape,
        compiler_params=pltpu.CompilerParams(vmem_limit_bytes=VMEM_LIMIT),
        cost_estimate=pl.CostEstimate(
            flops=2 * 11 * ROWS * CH * SLAB, bytes_accessed=6 * 1048576, transcendentals=0
        ),
    )(scalars, gathered, *noise, total, *args)


def filter_kernel(
    place, own_ref, by_one_ref, by_two_ref, by_three_ref, slabs_ref, mask_ref, onehot_ref,
    one_ref, two_ref, eight_ref, toeplitz_ref, final_ref, gain_ref, out_ref, state_ref, local_ref, spread_ref,
):
    step = pl.program_id(0)

    @pl.when(step == 0)
    def _():
        for d, ref in enumerate((own_ref, by_one_ref, by_two_ref, by_three_ref)):
            local_ref[lax.rem(place[1] + NX - d, NX)] = ref[...]
        for k in range(4):
            spread_ref[k] = jnp.broadcast_to(mask_ref[:, k : k + 1], (ROWS, CH))
        slabs = slabs_ref[...].reshape(NY * NCORE, NX, 4, ROWS)
        ends = slabs[:, 0]
        for s in range(1, NX):
            moved = slabs[:, s]
            for b in range(4):
                moved = moved + two_ref[b][None] * ends[:, b : b + 1, :]
            ends = moved
        eight = [eight_ref[b] for b in range(4)]
        state = jnp.zeros((4, ROWS), F32)
        for t in range(NY * NCORE - 1):
            state = jnp.where(t < place[0], apply_power(eight, state) + ends[t], state)
        state_ref[...] = state

    one = [one_ref[b] for b in range(4)]
    state = state_ref[...]
    for half in range(2):
        local = local_ref[step, :, half * CH : (half + 1) * CH]
        masked = jnp.concatenate([local * spread_ref[k] for k in range(4)], axis=1)
        spread = jnp.concatenate([onehot_ref[k : k + 1, :] * state for k in range(4)], axis=0)
        high = spread.astype(BF16)
        low = (spread - high.astype(F32)).astype(BF16)
        stacked = jnp.concatenate([high, high, low], axis=0)
        carried = lax.dot_general(
            stacked, gain_ref[...], (((0,), (0,)), ((), ())), preferred_element_type=F32
        )
        out_ref[:, half * CH : (half + 1) * CH] = (
            jnp.dot(masked, toeplitz_ref[...], preferred_element_type=F32) + carried
        )
        ends = lax.dot_general(
            final_ref[...], local, (((1,), (1,)), ((), ())), preferred_element_type=F32
        )
        entered = onehot_ref[0:1, :] * ends[0:4]
        for k in range(1, 4):
            entered = entered + onehot_ref[k : k + 1, :] * ends[k * 8 : k * 8 + 4]
        state = apply_power(one, state) + entered
    state_ref[...] = state


def filtered(place, *args):
    return pl.pallas_call(
        filter_kernel,
        grid_spec=pltpu.PrefetchScalarGridSpec(
            num_scalar_prefetch=1,
            grid=(NX,),
            in_specs=[whole(a) for a in args],
            out_specs=pl.BlockSpec((ROWS, SLAB), lambda i, zs: (0, i)),
            scratch_shapes=[
                pltpu.VMEM((4, ROWS), F32),
                pltpu.VMEM((NX, ROWS, SLAB), BF16),
                pltpu.VMEM((4, ROWS, CH), BF16),
            ],
        ),
        out_shape=jax.ShapeDtypeStruct((ROWS, NX * SLAB), F32),
        compiler_params=pltpu.CompilerParams(vmem_limit_bytes=VMEM_LIMIT),
        cost_estimate=pl.CostEstimate(
            flops=8 * 2 * ROWS * CH * 1100, bytes_accessed=4 * 1024 * 1024, transcendentals=0
        ),
    )(place, *args)


def ring(value, by):
    return lax.ppermute(value, "z", [(i, (i + by) % NZ) for i in range(NZ)])


def round_x(value, by):
    return lax.ppermute(value, "x", [(i, (i + by) % NX) for i in range(NX)])


def body(factor, white_noise, site_class, site_decay, site_angle, site_mix):
    x = lax.axis_index("x")
    z = lax.axis_index("z")
    tm = lax.axis_index("y") * NCORE + lax.axis_index("c")

    share = lax.dynamic_slice(factor, (tm * 32, 0), (32, factor.shape[1]))
    gathered = lax.all_gather(share, ("x", "y", "c"), tiled=True)
    gathered = gathered.reshape(NX, ROWS, factor.shape[1])

    def cut(by, half):
        first = lax.rem(x + by, NX) * SLAB + half * CH
        return lax.dynamic_slice(white_noise, (0, first), (ROWS, CH))

    steps = []
    for half in range(2):
        start = jnp.concatenate(
            [cut(0, half)] + [round_x(cut(d, half), d) for d in (1, 2, 3)], axis=0
        )
        blocks = [start, ring(start, 1), ring(start, -1)]
        if half == 0:
            site_class, site_decay, site_angle, site_mix, *blocks[1:] = lax.optimization_barrier(
                (site_class, site_decay, site_angle, site_mix, *blocks[1:])
            )
        for _ in range(2):
            blocks += [ring(blocks[-2], 1), ring(blocks[-1], -1)]
        steps.append(blocks)

    toeplitz, final, gain, one, two, eight = tables(site_decay, site_angle, site_mix)
    by_block = site_class.reshape(NX, NZ, ROWS)
    ids = jnp.arange(4, dtype=jnp.int32)
    tile_class = lax.dynamic_slice(by_block, (0, z, 0), (NX, 1, ROWS)).reshape(1, NX * ROWS)
    tile_hot = (tile_class == ids[:, None]).astype(F32)
    own_class = lax.dynamic_slice(by_block, (x, z, 0), (1, 1, ROWS)).reshape(1, ROWS)
    own_hot = (own_class == ids[:, None]).astype(F32)
    own_mask = (own_class.reshape(ROWS, 1) == ids[None, :]).astype(BF16)
    scalars = jnp.stack([x] + [(z + by) % NZ for by in AWAY + (4,)]).astype(jnp.int32)
    place = jnp.stack([tm, x]).astype(jnp.int32)
    for_last = (final, tile_hot, per_row(one, tile_hot))
    for_filter = (
        own_mask, own_hot, per_row(one, own_hot), per_row(two, own_hot), per_row(eight, own_hot),
        toeplitz, final, gain,
    )
    scalars, place, for_last, for_filter, *steps[1][5:] = lax.optimization_barrier(
        (scalars, place, for_last, for_filter, *steps[1][5:])
    )
    opposite = []
    for blocks in steps:
        opposite += [ring(blocks[5][:512], 1), ring(blocks[6][512:], -1)]

    total = product(scalars, gathered, [n for pair in zip(*steps) for n in pair])
    *pieces, to_send = last_product(scalars, gathered, opposite, total, *for_last)
    excitation = [pieces[0]] + [round_x(pieces[d], d) for d in (1, 2, 3)]
    own_ends = lax.all_to_all(to_send, ("y", "c", "x"), 0, 0, tiled=True)
    return filtered(place, *excitation, own_ends, *for_filter)


def solution(mesh):
    fine = Mesh(mesh.devices.reshape(NX, NZ, NY, NCORE), ("x", "z", "y", "c"))
    rows = ("x", "z")
    in_specs = (P(rows, None), P(rows, ("y", "c")), P(), P(), P(), P())
    return jax.shard_map(
        body, mesh=fine, in_specs=in_specs, out_specs=P(rows, ("y", "c")), check_vma=False
    )
```

profile of v0, /device:TPU:1, one launch (start us, length us, event | category | flops | bytes accessed | tf_op | source)
XLA Modules:
  0.0 163.0 jit_solution(1946194284936897981)
XLA Ops:
  6.5 2.0 %constant_dynamic-slice_fusion = bf16[32,8192]{1,0:T(8,128)(2,1)} fusion(bf16[256,8192]{1,0:T(8,128)(2,1)} %param.6, s32[]{:T(128)S(6)} %select_n.87), kind=kLoop, calls=%fused_computation.57 | loop fusion | bytes 1048580 | tf_op jit(solution)/shard_map/dynamic_slice | solution.py:331
  8.8 2.1 %collective-permute-start = (bf16[256,256]{1,0:T(8,128)(2,1)S(1)}, bf16[256,256]{1,0:T(8,128)(2,1)S(1)}, u32[]{:S(2)}, u32[]{:S(2)}) collective-permute-start(bf16[256,256]{1,0:T(8,128)(2,1)S(1)} %get-tuple-element.70), channel_id=1, source_target_pairs={{0,64},{64,128},{128,192},{192,0},{1,65},{65,129},{129,193},{193,1... | collective-permute-start | bytes 393224 | tf_op jit(solution)/shard_map/ppermute | solution.py:323
  10.9 2.5 %collective-permute-start.1 = (bf16[256,256]{1,0:T(8,128)(2,1)S(1)}, bf16[256,256]{1,0:T(8,128)(2,1)S(1)}, u32[]{:S(2)}, u32[]{:S(2)}) collective-permute-start(bf16[256,256]{1,0:T(8,128)(2,1)S(1)} %get-tuple-element.69), channel_id=1, source_target_pairs={{0,128},{64,192},{128,0},{192,64},{1,129},{65,193},{129,1},{193,65... | collective-permute-start | bytes 393224 | tf_op jit(solution)/shard_map/ppermute | solution.py:323
  13.3 1.2 collective-permute-start.2
  14.5 4.5 %collective-permute-done.1 = bf16[256,256]{1,0:T(8,128)(2,1)S(1)} collective-permute-done((bf16[256,256]{1,0:T(8,128)(2,1)S(1)}, bf16[256,256]{1,0:T(8,128)(2,1)S(1)}, u32[]{:S(2)}, u32[]{:S(2)}) %collective-permute-start.1) | collective-permute-done | bytes 131104 | tf_op jit(solution)/shard_map/ppermute | solution.py:323
  19.1 1.7 %collective-permute-start.3 = (bf16[1024,256]{1,0:T(8,128)(2,1)S(1)}, bf16[1024,256]{1,0:T(8,128)(2,1)S(1)}, u32[]{:S(2)}, u32[]{:S(2)}) collective-permute-start(bf16[1024,256]{1,0:T(8,128)(2,1)S(1)} %pad_maximum_fusion.refs_0_), channel_id=1, source_target_pairs={{0,8},{8,16},{16,24},{24,32},{32,40},{40,48},{48,56},{56,0},{1,9},... | collective-permute-start | bytes 1572872 | tf_op jit(solution)/shard_map/ppermute | solution.py:319
  20.8 4.0 %collective-permute-start.4 = (bf16[1024,256]{1,0:T(8,128)(2,1)S(1)}, bf16[1024,256]{1,0:T(8,128)(2,1)}, u32[]{:S(2)}, u32[]{:S(2)}) collective-permute-start(bf16[1024,256]{1,0:T(8,128)(2,1)S(1)} %pad_maximum_fusion.refs_0_), channel_id=1, source_target_pairs={{0,56},{8,0},{16,8},{24,16},{32,24},{40,32},{48,40},{56,48},{1,57}... | collective-permute-start | bytes 1572872 | tf_op jit(solution)/shard_map/ppermute | solution.py:319
  24.8 1.2 collective-permute-start.5
  26.0 2.2 %collective-permute-start.6 = (bf16[256,256]{1,0:T(8,128)(2,1)S(1)}, bf16[256,256]{1,0:T(8,128)(2,1)S(1)}, u32[]{:S(2)}, u32[]{:S(2)}) collective-permute-start(bf16[256,256]{1,0:T(8,128)(2,1)S(1)} %get-tuple-element.73), channel_id=1, source_target_pairs={{0,128},{64,192},{128,0},{192,64},{1,129},{65,193},{129,1},{193,65... | collective-permute-start | bytes 393224 | tf_op jit(solution)/shard_map/ppermute | solution.py:323
  28.2 0.5 collective-permute-start.7
  28.7 0.6 stack.92.zs
  29.3 0.6 pad_add_fusion.place
  30.2 6.1 %collective-permute-done.6 = bf16[256,256]{1,0:T(8,128)(2,1)S(1)} collective-permute-done((bf16[256,256]{1,0:T(8,128)(2,1)S(1)}, bf16[256,256]{1,0:T(8,128)(2,1)S(1)}, u32[]{:S(2)}, u32[]{:S(2)}) %collective-permute-start.6) | collective-permute-done | bytes 131104 | tf_op jit(solution)/shard_map/ppermute | solution.py:323
  36.3 2.2 %collective-permute-done.7 = bf16[256,256]{1,0:T(8,128)(2,1)S(1)} collective-permute-done((bf16[256,256]{1,0:T(8,128)(2,1)S(1)}, bf16[256,256]{1,0:T(8,128)(2,1)S(1)}, u32[]{:S(2)}, u32[]{:S(2)}) %collective-permute-start.7) | collective-permute-done | bytes 131104 | tf_op jit(solution)/shard_map/ppermute | solution.py:323
  38.6 2.7 %collective-permute-start.11 = (bf16[1024,256]{1,0:T(8,128)(2,1)S(1)}, bf16[1024,256]{1,0:T(8,128)(2,1)}, u32[]{:S(2)}, u32[]{:S(2)}) collective-permute-start(bf16[1024,256]{1,0:T(8,128)(2,1)S(1)} %pad_maximum_fusion.1.refs_1_), channel_id=1, source_target_pairs={{0,56},{8,0},{16,8},{24,16},{32,24},{40,32},{48,40},{56,48},{1,57}... | collective-permute-start | bytes 1572872 | tf_op jit(solution)/shard_map/ppermute | solution.py:319
  42.7 0.3 fusion.24
  44.0 1.0 convolution_bitcast_fusion.4
  48.0 3.4 %fusion.39 = f32[4,1,256,4]{1,2,3,0:T(8,128)S(1)} fusion(f32[256,4,4,4]{0,2,3,1:T(4,128)S(1)} %concatenate.57, f32[4,4,1,1]{1,2,3,0:T(1,128)S(1)} %bitcast.197), kind=kOutput, calls=%fused_computation.101 | convolution fusion | flops 196608 | bytes 81984 | tf_op jit(solution)/shard_map/ka,jkab->kbj/dot_general | solution.py:55
  51.6 0.6 copy.182
  53.1 2.7 %collective-permute-start.17 = (bf16[1024,256]{1,0:T(8,128)(2,1)}, bf16[1024,256]{1,0:T(8,128)(2,1)}, u32[]{:S(2)}, u32[]{:S(2)}) collective-permute-start(bf16[1024,256]{1,0:T(8,128)(2,1)} %collective-permute-done.4.refs_4_), channel_id=1, source_target_pairs={{0,56},{8,0},{16,8},{24,16},{32,24},{40,32},{48,40},{56,48},{1,57}... | collective-permute-start | bytes 1572872 | tf_op jit(solution)/shard_map/ppermute | solution.py:319
  55.8 2.7 %collective-permute-start.12 = (bf16[1024,256]{1,0:T(8,128)(2,1)}, bf16[1024,256]{1,0:T(8,128)(2,1)}, u32[]{:S(2)}, u32[]{:S(2)}) collective-permute-start(bf16[1024,256]{1,0:T(8,128)(2,1)} %collective-permute-done.11.refs_5_), channel_id=1, source_target_pairs={{0,56},{8,0},{16,8},{24,16},{32,24},{40,32},{48,40},{56,48},{1,57}... | collective-permute-start | bytes 1572872 | tf_op jit(solution)/shard_map/ppermute | solution.py:319
  58.5 0.6 pad_maximum_fusion.3.gain_ref
  59.9 16.1 %collective-permute-done.9.refs_7_ = bf16[1024,256]{1,0:T(8,128)(2,1)} collective-permute-done((bf16[1024,256]{1,0:T(8,128)(2,1)}, bf16[1024,256]{1,0:T(8,128)(2,1)}, u32[]{:S(2)}, u32[]{:S(2)}) %collective-permute-start.9) | collective-permute-done | bytes 524320 | tf_op jit(solution)/shard_map/ppermute | solution.py:319
  76.1 2.7 %collective-permute-start.13 = (bf16[1024,256]{1,0:T(8,128)(2,1)}, bf16[1024,256]{1,0:T(8,128)(2,1)S(1)}, u32[]{:S(2)}, u32[]{:S(2)}) collective-permute-start(bf16[1024,256]{1,0:T(8,128)(2,1)} %collective-permute-done.12.refs_9_), channel_id=1, source_target_pairs={{0,56},{8,0},{16,8},{24,16},{32,24},{40,32},{48,40},{56,48},{1,57}... | collective-permute-start | bytes 1572872 | tf_op jit(solution)/shard_map/ppermute | solution.py:319
  78.8 2.7 %collective-permute-start.18 = (bf16[1024,256]{1,0:T(8,128)(2,1)}, bf16[1024,256]{1,0:T(8,128)(2,1)}, u32[]{:S(2)}, u32[]{:S(2)}) collective-permute-start(bf16[1024,256]{1,0:T(8,128)(2,1)} %collective-permute-done.17.refs_8_), channel_id=1, source_target_pairs={{0,56},{8,0},{16,8},{24,16},{32,24},{40,32},{48,40},{56,48},{1,57}... | collective-permute-start | bytes 1572872 | tf_op jit(solution)/shard_map/ppermute | solution.py:319
  81.4 0.6 pad_bitcast_fusion.final_ref
  82.2 0.8 copy.191
  83.1 0.4 slice.113
  83.4 1.8 %reshape.340 = bf16[4,256,511]{2,1,0:T(8,128)(2,1)S(1)} reshape(bf16[4,130816]{1,0:T(4,128)(2,1)S(1)} %slice.113) | data formatting | bytes 2093056 | tf_op jit(solution)/shard_map/reshape | solution.py:62
  85.2 0.8 slice.114
  86.2 0.9 multiply_reduce_fusion.power_ref
  87.1 0.8 multiply_reduce_fusion.1
  87.9 0.7 fusion.mask_ref
  88.8 2.7 %collective-permute-start.21 = (bf16[512,256]{1,0:T(8,128)(2,1)S(1)}, bf16[512,256]{1,0:T(8,128)(2,1)S(1)}, u32[]{:S(2)}, u32[]{:S(2)}) collective-permute-start(bf16[512,256]{1,0:T(8,128)(2,1)S(1)} %slice.104), channel_id=1, source_target_pairs={{0,56},{8,0},{16,8},{24,16},{32,24},{40,32},{48,40},{56,48},{1,57}... | collective-permute-start | bytes 786440 | tf_op jit(solution)/shard_map/ppermute | solution.py:319
  91.5 6.6 %collective-permute-done.15.refs_10_ = bf16[1024,256]{1,0:T(8,128)(2,1)} collective-permute-done((bf16[1024,256]{1,0:T(8,128)(2,1)}, bf16[1024,256]{1,0:T(8,128)(2,1)}, u32[]{:S(2)}, u32[]{:S(2)}) %collective-permute-start.15) | collective-permute-done | bytes 524320 | tf_op jit(solution)/shard_map/ppermute | solution.py:319
  98.1 1.0 slice.115
  99.2 1.0 slice.116
  100.1 2.7 %collective-permute-start.19 = (bf16[512,256]{1,0:T(8,128)(2,1)S(1)}, bf16[512,256]{1,0:T(8,128)(2,1)S(1)}, u32[]{:S(2)}, u32[]{:S(2)}) collective-permute-start(bf16[512,256]{1,0:T(8,128)(2,1)S(1)} %slice.116), channel_id=1, source_target_pairs={{0,56},{8,0},{16,8},{24,16},{32,24},{40,32},{48,40},{56,48},{1,57}... | collective-permute-start | bytes 786440 | tf_op jit(solution)/shard_map/ppermute | solution.py:319
  102.9 9.9 %shard_map.64.total_ref = f32[1024,512]{1,0:T(8,128)} custom-call(s32[9]{0:T(128)} %stack.92.zs, bf16[4,256,8192]{2,1,0:T(8,128)(2,1)} %bitcast.181, bf16[1024,256]{1,0:T(8,128)(2,1)} %copy-done, bf16[1024,256]{1,0:T(8,128)(2,1)} %copy-done.1, bf16[1024,256]{1,0:T(8,128)(2,1)} %copy-done.5, bf16[1024,256]{1,0:T(8,128)(2,1)} %collective-permute-done.8.refs_3_, ...), custom_call_target="tpu_custom_call" | custom-call | flops 4697620480 | bytes 19922944 | tf_op jit(solution)/shard_map/pallas_call | solution.py:159
  112.8 0.6 copy-done.6
  113.7 0.7 copy-done.9
  114.4 5.9 %shard_map.65 = (bf16[256,512]{1,0:T(8,128)(2,1)}, bf16[256,512]{1,0:T(8,128)(2,1)}, bf16[256,512]{1,0:T(8,128)(2,1)}, bf16[256,512]{1,0:T(8,128)(2,1)}, f32[32,4,256]{2,1,0:T(4,128)}) custom-call(s32[9]{0:T(128)} %stack.92.zs, bf16[4,256,8192]{2,1,0:T(8,128)(2,1)} %bitcast.182, bf16[512,256]{1,0:T(8,128)(2,1)} %copy-done.8, bf16[512,256]{1,0:T(8,128)(2,1)} %copy-done.9, ...), custom_call_target="tpu_custom_call" | custom-call | flops 738197504 | bytes 6291456 | tf_op jit(solution)/shard_map/pallas_call | solution.py:225
  120.3 0.7 collective-permute-start.22
  121.0 1.8 %collective-permute-start.23 = (bf16[256,512]{1,0:T(8,128)(2,1)}, bf16[256,512]{1,0:T(8,128)(2,1)S(1)}, u32[]{:S(2)}, u32[]{:S(2)}) collective-permute-start(bf16[256,512]{1,0:T(8,128)(2,1)} %get-tuple-element.46), channel_id=1, source_target_pairs={{0,128},{64,192},{128,0},{192,64},{1,129},{65,193},{129,1},{193,65... | collective-permute-start | bytes 786440 | tf_op jit(solution)/shard_map/ppermute | solution.py:323
  122.9 0.7 collective-permute-start.24
  123.5 25.4 %all_to_all.5.slabs_ref = f32[32,4,256]{2,1,0:T(4,128)} all-to-all(f32[32,4,256]{2,1,0:T(4,128)} %get-tuple-element.48), channel_id=1, replica_groups=mesh['x'=4,'z'=8,'y'=4,'c'=2] {'y','c','x'}, dimensions={0} | all-to-all | bytes 262144 | tf_op jit(solution)/shard_map/all_to_all | solution.py:378
  149.0 0.7 copy-done.16
  149.9 6.3 %shard_map.66 = f32[256,2048]{1,0:T(8,128)} custom-call(s32[2]{0:T(128)} %pad_add_fusion.place, bf16[256,512]{1,0:T(8,128)(2,1)} %get-tuple-element.44.own_ref, bf16[256,512]{1,0:T(8,128)(2,1)} %copy-done.16, bf16[256,512]{1,0:T(8,128)(2,1)} %copy-done.17, bf16[256,512]{1,0:T(8,128)(2,1)} %copy-done.18, f32[32,4,256]{2,1,0:T(4,128)} %all_to_all.5.slabs_ref, ...), custom_call_target="tpu_custom_call" | custom-call | flops 1153433600 | bytes 4194304 | tf_op jit(solution)/shard_map/pallas_call | solution.py:297
  (139 shorter events, 8.8 us)
Async XLA Ops:
  6.5 2.0 %copy-start.4 = (bf16[256,2048]{1,0:T(8,128)(2,1)S(1)}, bf16[256,2048]{1,0:T(8,128)(2,1)}, u32[]{:S(2)}) copy-start(bf16[256,2048]{1,0:T(8,128)(2,1)} %param.7) | copy-start | bytes 3145732
  6.5 96.3 %all-gather.2.cloned.1.call-start = ((), (), s32[]{:S(2)}) async-start(), calls=%async_computation.1 | async-start | bytes 17301504 | tf_op jit(solution)/shard_map/all_gather | solution.py:332
  8.6 32.7 %copy-start.15 = (f32[2,4]{1,0:T(2,128)S(1)}, f32[2,4]{1,0:T(2,128)}, u32[]{:S(2)}) copy-start(f32[2,4]{1,0:T(2,128)} %param.9) | copy-start | bytes 100
  8.6 32.8 %copy-start.14 = (f32[2,4]{1,0:T(2,128)S(1)}, f32[2,4]{1,0:T(2,128)}, u32[]{:S(2)}) copy-start(f32[2,4]{1,0:T(2,128)} %param.10) | copy-start | bytes 100
  8.6 32.9 %copy-start.13 = (f32[4,4]{1,0:T(4,128)S(1)}, f32[4,4]{1,0:T(4,128)}, u32[]{:S(2)}) copy-start(f32[4,4]{1,0:T(4,128)} %param.11) | copy-start | bytes 196
  8.8 5.7 %collective-permute-start = (bf16[256,256]{1,0:T(8,128)(2,1)S(1)}, bf16[256,256]{1,0:T(8,128)(2,1)S(1)}, u32[]{:S(2)}, u32[]{:S(2)}) collective-permute-start(bf16[256,256]{1,0:T(8,128)(2,1)S(1)} %get-tuple-element.70), channel_id=1, source_target_pairs={{0,64},{64,128},{128,192},{192,0},{1,65},{65,129},{129,193},{193,1... | collective-permute-start | bytes 393224 | tf_op jit(solution)/shard_map/ppermute | solution.py:323
  10.9 8.2 %collective-permute-start.1 = (bf16[256,256]{1,0:T(8,128)(2,1)S(1)}, bf16[256,256]{1,0:T(8,128)(2,1)S(1)}, u32[]{:S(2)}, u32[]{:S(2)}) collective-permute-start(bf16[256,256]{1,0:T(8,128)(2,1)S(1)} %get-tuple-element.69), channel_id=1, source_target_pairs={{0,128},{64,192},{128,0},{192,64},{1,129},{65,193},{129,1},{193,65... | collective-permute-start | bytes 393224 | tf_op jit(solution)/shard_map/ppermute | solution.py:323
  13.3 5.7 %collective-permute-start.2 = (bf16[256,256]{1,0:T(8,128)(2,1)S(1)}, bf16[256,256]{1,0:T(8,128)(2,1)S(1)}, u32[]{:S(2)}, u32[]{:S(2)}) collective-permute-start(bf16[256,256]{1,0:T(8,128)(2,1)S(1)} %get-tuple-element.68), channel_id=1, source_target_pairs={{0,192},{64,0},{128,64},{192,128},{1,193},{65,1},{129,65},{193,129... | collective-permute-start | bytes 393224 | tf_op jit(solution)/shard_map/ppermute | solution.py:323
  19.1 32.3 %copy-start = (bf16[1024,256]{1,0:T(8,128)(2,1)}, bf16[1024,256]{1,0:T(8,128)(2,1)S(1)}, u32[]{:S(2)}) copy-start(bf16[1024,256]{1,0:T(8,128)(2,1)S(1)} %pad_maximum_fusion.refs_0_) | copy-start | bytes 1572868
  19.1 22.2 %collective-permute-start.3 = (bf16[1024,256]{1,0:T(8,128)(2,1)S(1)}, bf16[1024,256]{1,0:T(8,128)(2,1)S(1)}, u32[]{:S(2)}, u32[]{:S(2)}) collective-permute-start(bf16[1024,256]{1,0:T(8,128)(2,1)S(1)} %pad_maximum_fusion.refs_0_), channel_id=1, source_target_pairs={{0,8},{8,16},{16,24},{24,32},{32,40},{40,48},{48,56},{56,0},{1,9},... | collective-permute-start | bytes 1572872 | tf_op jit(solution)/shard_map/ppermute | solution.py:319
  20.8 20.5 %collective-permute-start.4 = (bf16[1024,256]{1,0:T(8,128)(2,1)S(1)}, bf16[1024,256]{1,0:T(8,128)(2,1)}, u32[]{:S(2)}, u32[]{:S(2)}) collective-permute-start(bf16[1024,256]{1,0:T(8,128)(2,1)S(1)} %pad_maximum_fusion.refs_0_), channel_id=1, source_target_pairs={{0,56},{8,0},{16,8},{24,16},{32,24},{40,32},{48,40},{56,48},{1,57}... | collective-permute-start | bytes 1572872 | tf_op jit(solution)/shard_map/ppermute | solution.py:319
  24.8 5.3 %collective-permute-start.5 = (bf16[256,256]{1,0:T(8,128)(2,1)S(1)}, bf16[256,256]{1,0:T(8,128)(2,1)S(1)}, u32[]{:S(2)}, u32[]{:S(2)}) collective-permute-start(bf16[256,256]{1,0:T(8,128)(2,1)S(1)} %get-tuple-element.67), channel_id=1, source_target_pairs={{0,64},{64,128},{128,192},{192,0},{1,65},{65,129},{129,193},{193,1... | collective-permute-start | bytes 393224 | tf_op jit(solution)/shard_map/ppermute | solution.py:323
  26.0 10.2 %collective-permute-start.6 = (bf16[256,256]{1,0:T(8,128)(2,1)S(1)}, bf16[256,256]{1,0:T(8,128)(2,1)S(1)}, u32[]{:S(2)}, u32[]{:S(2)}) collective-permute-start(bf16[256,256]{1,0:T(8,128)(2,1)S(1)} %get-tuple-element.73), channel_id=1, source_target_pairs={{0,128},{64,192},{128,0},{192,64},{1,129},{65,193},{129,1},{193,65... | collective-permute-start | bytes 393224 | tf_op jit(solution)/shard_map/ppermute | solution.py:323
  28.2 10.3 %collective-permute-start.7 = (bf16[256,256]{1,0:T(8,128)(2,1)S(1)}, bf16[256,256]{1,0:T(8,128)(2,1)S(1)}, u32[]{:S(2)}, u32[]{:S(2)}) collective-permute-start(bf16[256,256]{1,0:T(8,128)(2,1)S(1)} %get-tuple-element.72), channel_id=1, source_target_pairs={{0,192},{64,0},{128,64},{192,128},{1,193},{65,1},{129,65},{193,129... | collective-permute-start | bytes 393224 | tf_op jit(solution)/shard_map/ppermute | solution.py:323
  38.5 12.9 %copy-start.1 = (bf16[1024,256]{1,0:T(8,128)(2,1)}, bf16[1024,256]{1,0:T(8,128)(2,1)S(1)}, u32[]{:S(2)}) copy-start(bf16[1024,256]{1,0:T(8,128)(2,1)S(1)} %pad_maximum_fusion.1.refs_1_) | copy-start | bytes 1572868
  38.5 17.3 %collective-permute-start.8 = (bf16[1024,256]{1,0:T(8,128)(2,1)S(1)}, bf16[1024,256]{1,0:T(8,128)(2,1)}, u32[]{:S(2)}, u32[]{:S(2)}) collective-permute-start(bf16[1024,256]{1,0:T(8,128)(2,1)S(1)} %pad_maximum_fusion.1.refs_1_), channel_id=1, source_target_pairs={{0,8},{8,16},{16,24},{24,32},{32,40},{40,48},{48,56},{56,0},{1,9},... | collective-permute-start | bytes 1572872 | tf_op jit(solution)/shard_map/ppermute | solution.py:319
  38.6 17.2 %collective-permute-start.11 = (bf16[1024,256]{1,0:T(8,128)(2,1)S(1)}, bf16[1024,256]{1,0:T(8,128)(2,1)}, u32[]{:S(2)}, u32[]{:S(2)}) collective-permute-start(bf16[1024,256]{1,0:T(8,128)(2,1)S(1)} %pad_maximum_fusion.1.refs_1_), channel_id=1, source_target_pairs={{0,56},{8,0},{16,8},{24,16},{32,24},{40,32},{48,40},{56,48},{1,57}... | collective-permute-start | bytes 1572872 | tf_op jit(solution)/shard_map/ppermute | solution.py:319
  41.3 1.1 copy-start.5
  48.0 5.0 %copy-start.11 = (s32[8192]{0:T(1024)S(1)}, s32[8192]{0:T(1024)}, u32[]{:S(2)}) copy-start(s32[8192]{0:T(1024)} %param.8) | copy-start | bytes 98308
  53.1 25.7 %collective-permute-start.14 = (bf16[1024,256]{1,0:T(8,128)(2,1)}, bf16[1024,256]{1,0:T(8,128)(2,1)}, u32[]{:S(2)}, u32[]{:S(2)}) collective-permute-start(bf16[1024,256]{1,0:T(8,128)(2,1)} %copy-done.5), channel_id=1, source_target_pairs={{0,8},{8,16},{16,24},{24,32},{32,40},{40,48},{48,56},{56,0},{1,9},... | collective-permute-start | bytes 1572872 | tf_op jit(solution)/shard_map/ppermute | solution.py:319
  53.1 25.6 %collective-permute-start.17 = (bf16[1024,256]{1,0:T(8,128)(2,1)}, bf16[1024,256]{1,0:T(8,128)(2,1)}, u32[]{:S(2)}, u32[]{:S(2)}) collective-permute-start(bf16[1024,256]{1,0:T(8,128)(2,1)} %collective-permute-done.4.refs_4_), channel_id=1, source_target_pairs={{0,56},{8,0},{16,8},{24,16},{32,24},{40,32},{48,40},{56,48},{1,57}... | collective-permute-start | bytes 1572872 | tf_op jit(solution)/shard_map/ppermute | solution.py:319
  55.8 20.3 %collective-permute-start.9 = (bf16[1024,256]{1,0:T(8,128)(2,1)}, bf16[1024,256]{1,0:T(8,128)(2,1)}, u32[]{:S(2)}, u32[]{:S(2)}) collective-permute-start(bf16[1024,256]{1,0:T(8,128)(2,1)} %collective-permute-done.8.refs_3_), channel_id=1, source_target_pairs={{0,8},{8,16},{16,24},{24,32},{32,40},{40,48},{48,56},{56,0},{1,9},... | collective-permute-start | bytes 1572872 | tf_op jit(solution)/shard_map/ppermute | solution.py:319
  55.8 20.3 %collective-permute-start.12 = (bf16[1024,256]{1,0:T(8,128)(2,1)}, bf16[1024,256]{1,0:T(8,128)(2,1)}, u32[]{:S(2)}, u32[]{:S(2)}) collective-permute-start(bf16[1024,256]{1,0:T(8,128)(2,1)} %collective-permute-done.11.refs_5_), channel_id=1, source_target_pairs={{0,56},{8,0},{16,8},{24,16},{32,24},{40,32},{48,40},{56,48},{1,57}... | collective-permute-start | bytes 1572872 | tf_op jit(solution)/shard_map/ppermute | solution.py:319
  59.1 28.0 %copy-start.12 = (f32[4,256]{1,0:T(4,128)}, f32[4,256]{1,0:T(4,128)S(1)}, u32[]{:S(2)}) copy-start(f32[4,256]{1,0:T(4,128)S(1)} %fusion.21.onehot_ref) | copy-start | bytes 12292
  59.3 26.9 %copy-start.10 = (f32[4,1024]{1,0:T(4,128)}, f32[4,1024]{1,0:T(4,128)S(1)}, u32[]{:S(2)}) copy-start(f32[4,1024]{1,0:T(4,128)S(1)} %fusion.13.onehot_ref) | copy-start | bytes 49156
  76.1 12.5 %collective-permute-start.10 = (bf16[1024,256]{1,0:T(8,128)(2,1)}, bf16[1024,256]{1,0:T(8,128)(2,1)S(1)}, u32[]{:S(2)}, u32[]{:S(2)}) collective-permute-start(bf16[1024,256]{1,0:T(8,128)(2,1)} %collective-permute-done.9.refs_7_), channel_id=1, source_target_pairs={{0,8},{8,16},{16,24},{24,32},{32,40},{40,48},{48,56},{56,0},{1,9},... | collective-permute-start | bytes 1572872 | tf_op jit(solution)/shard_map/ppermute | solution.py:319
  76.1 12.5 %collective-permute-start.13 = (bf16[1024,256]{1,0:T(8,128)(2,1)}, bf16[1024,256]{1,0:T(8,128)(2,1)S(1)}, u32[]{:S(2)}, u32[]{:S(2)}) collective-permute-start(bf16[1024,256]{1,0:T(8,128)(2,1)} %collective-permute-done.12.refs_9_), channel_id=1, source_target_pairs={{0,56},{8,0},{16,8},{24,16},{32,24},{40,32},{48,40},{56,48},{1,57}... | collective-permute-start | bytes 1572872 | tf_op jit(solution)/shard_map/ppermute | solution.py:319
  78.8 19.3 %collective-permute-start.15 = (bf16[1024,256]{1,0:T(8,128)(2,1)}, bf16[1024,256]{1,0:T(8,128)(2,1)}, u32[]{:S(2)}, u32[]{:S(2)}) collective-permute-start(bf16[1024,256]{1,0:T(8,128)(2,1)} %collective-permute-done.14.refs_6_), channel_id=1, source_target_pairs={{0,8},{8,16},{16,24},{24,32},{32,40},{40,48},{48,56},{56,0},{1,9},... | collective-permute-start | bytes 1572872 | tf_op jit(solution)/shard_map/ppermute | solution.py:319
  78.8 20.4 %collective-permute-start.18 = (bf16[1024,256]{1,0:T(8,128)(2,1)}, bf16[1024,256]{1,0:T(8,128)(2,1)}, u32[]{:S(2)}, u32[]{:S(2)}) collective-permute-start(bf16[1024,256]{1,0:T(8,128)(2,1)} %collective-permute-done.17.refs_8_), channel_id=1, source_target_pairs={{0,56},{8,0},{16,8},{24,16},{32,24},{40,32},{48,40},{56,48},{1,57}... | collective-permute-start | bytes 1572872 | tf_op jit(solution)/shard_map/ppermute | solution.py:319
  88.6 14.2 %copy-start.2 = (bf16[1024,256]{1,0:T(8,128)(2,1)}, bf16[1024,256]{1,0:T(8,128)(2,1)S(1)}, u32[]{:S(2)}) copy-start(bf16[1024,256]{1,0:T(8,128)(2,1)S(1)} %collective-permute-done.10.refs_11_) | copy-start | bytes 1572868
  88.6 14.2 %copy-start.3 = (bf16[1024,256]{1,0:T(8,128)(2,1)}, bf16[1024,256]{1,0:T(8,128)(2,1)S(1)}, u32[]{:S(2)}) copy-start(bf16[1024,256]{1,0:T(8,128)(2,1)S(1)} %collective-permute-done.13.refs_13_) | copy-start | bytes 1572868
  88.7 24.1 %collective-permute-start.20 = (bf16[512,256]{1,0:T(8,128)(2,1)S(1)}, bf16[512,256]{1,0:T(8,128)(2,1)S(1)}, u32[]{:S(2)}, u32[]{:S(2)}) collective-permute-start(bf16[512,256]{1,0:T(8,128)(2,1)S(1)} %slice.103), channel_id=1, source_target_pairs={{0,8},{8,16},{16,24},{24,32},{32,40},{40,48},{48,56},{56,0},{1,9},... | collective-permute-start | bytes 786440 | tf_op jit(solution)/shard_map/ppermute | solution.py:319
  88.8 24.0 %collective-permute-start.21 = (bf16[512,256]{1,0:T(8,128)(2,1)S(1)}, bf16[512,256]{1,0:T(8,128)(2,1)S(1)}, u32[]{:S(2)}, u32[]{:S(2)}) collective-permute-start(bf16[512,256]{1,0:T(8,128)(2,1)S(1)} %slice.104), channel_id=1, source_target_pairs={{0,56},{8,0},{16,8},{24,16},{32,24},{40,32},{48,40},{56,48},{1,57}... | collective-permute-start | bytes 786440 | tf_op jit(solution)/shard_map/ppermute | solution.py:319
  99.1 13.7 %collective-permute-start.16 = (bf16[512,256]{1,0:T(8,128)(2,1)S(1)}, bf16[512,256]{1,0:T(8,128)(2,1)S(1)}, u32[]{:S(2)}, u32[]{:S(2)}) collective-permute-start(bf16[512,256]{1,0:T(8,128)(2,1)S(1)} %slice.115), channel_id=1, source_target_pairs={{0,8},{8,16},{16,24},{24,32},{32,40},{40,48},{48,56},{56,0},{1,9},... | collective-permute-start | bytes 786440 | tf_op jit(solution)/shard_map/ppermute | solution.py:319
  100.1 12.7 %collective-permute-start.19 = (bf16[512,256]{1,0:T(8,128)(2,1)S(1)}, bf16[512,256]{1,0:T(8,128)(2,1)S(1)}, u32[]{:S(2)}, u32[]{:S(2)}) collective-permute-start(bf16[512,256]{1,0:T(8,128)(2,1)S(1)} %slice.116), channel_id=1, source_target_pairs={{0,56},{8,0},{16,8},{24,16},{32,24},{40,32},{48,40},{56,48},{1,57}... | collective-permute-start | bytes 786440 | tf_op jit(solution)/shard_map/ppermute | solution.py:319
  112.8 0.7 copy-start.6
  112.8 0.8 copy-start.7
  112.8 0.9 copy-start.8
  113.7 0.7 copy-start.9
  120.3 28.6 %collective-permute-start.22 = (bf16[256,512]{1,0:T(8,128)(2,1)}, bf16[256,512]{1,0:T(8,128)(2,1)S(1)}, u32[]{:S(2)}, u32[]{:S(2)}) collective-permute-start(bf16[256,512]{1,0:T(8,128)(2,1)} %get-tuple-element.45), channel_id=1, source_target_pairs={{0,64},{64,128},{128,192},{192,0},{1,65},{65,129},{129,193},{193,1... | collective-permute-start | bytes 786440 | tf_op jit(solution)/shard_map/ppermute | solution.py:323
  121.0 27.9 %collective-permute-start.23 = (bf16[256,512]{1,0:T(8,128)(2,1)}, bf16[256,512]{1,0:T(8,128)(2,1)S(1)}, u32[]{:S(2)}, u32[]{:S(2)}) collective-permute-start(bf16[256,512]{1,0:T(8,128)(2,1)} %get-tuple-element.46), channel_id=1, source_target_pairs={{0,128},{64,192},{128,0},{192,64},{1,129},{65,193},{129,1},{193,65... | collective-permute-start | bytes 786440 | tf_op jit(solution)/shard_map/ppermute | solution.py:323
  122.9 26.1 %collective-permute-start.24 = (bf16[256,512]{1,0:T(8,128)(2,1)}, bf16[256,512]{1,0:T(8,128)(2,1)S(1)}, u32[]{:S(2)}, u32[]{:S(2)}) collective-permute-start(bf16[256,512]{1,0:T(8,128)(2,1)} %get-tuple-element.47), channel_id=1, source_target_pairs={{0,192},{64,0},{128,64},{192,128},{1,193},{65,1},{129,65},{193,129... | collective-permute-start | bytes 786440 | tf_op jit(solution)/shard_map/ppermute | solution.py:323
  149.0 0.7 copy-start.16
  149.0 0.8 copy-start.17
  149.0 0.9 copy-start.18
Sparse Core Ops, SparseCore 0:
  9.9 84.2 all-gather.1
where the time goes:
time: 163 us
  starting transfers between devices  37.7 us (23%)
  waiting for transfers between devices  35.9 us (22%)
  blocking collectives  25.4 us (16%)
  Pallas kernels  22.1 us (14%)
  local copies, waits for them, and re-layouts  17.3 us (11%)
  between operations  14 us (9%)
  matrix products  6.44 us (4%)
  other arithmetic  4.21 us (3%)
    all_to_all x1, blocking collectives, body(): own_ends = lax.all_to_all(to_send, ('y', 'c', 'x'), 0, 0, tiled=True)  25.4 us
    ppermute x16, starting transfers between devices, ring(): return lax.ppermute(value, 'z', [(i, (i + by) % NZ) for i in range(NZ)])  24.9 us
    ppermute x16, waiting for transfers between devices, ring(): return lax.ppermute(value, 'z', [(i, (i + by) % NZ) for i in range(NZ)])  22.7 us
    ppermute x9, waiting for transfers between devices, round_x(): return lax.ppermute(value, 'x', [(i, (i + by) % NX) for i in range(NX)])  13.1 us
    ppermute x9, starting transfers between devices, round_x(): return lax.ppermute(value, 'x', [(i, (i + by) % NX) for i in range(NX)])  12.8 us
    pallas_call x1, Pallas kernels, product(): pl.pallas_call(product_kernel, grid_spec=pltpu.PrefetchScalarGridSpec(num...  9.88 us
    pallas_call x1, Pallas kernels, filtered(): pl.pallas_call(filter_kernel, grid_spec=pltpu.PrefetchScalarGridSpec(num_...  6.26 us
    pallas_call x1, Pallas kernels, last_product(): pl.pallas_call(last_kernel, grid_spec=pltpu.PrefetchScalarGridSpec(num_sc...  5.93 us
  transfers between devices with their start and end apart: 26, of which 6 were waited for; matrix products, arithmetic and copies ran while one was open for 14% of the time, Pallas kernels for 6%

commit v1 on v0

--- a/solution.py
+++ b/solution.py
@@ -12,6 +12,7 @@
 ROWS = 256
 SLAB = 512
 AWAY = (0, 7, 1, 6, 2, 5, 3)
+AHEAD = 3
 VMEM_LIMIT = 58 * 1024 * 1024
 F32 = jnp.float32
 BF16 = jnp.bfloat16
@@ -87,7 +88,7 @@
 
 
 def load(zs, where, g_ref, noise, held, block, sems):
-    waits = []
+    every = []
     for b, z in enumerate(where):
         copies = []
         for q in range(NX):
@@ -106,10 +107,8 @@
                     sems.at[b, NX + j],
                 )
             )
-        for copy in copies:
-            copy.start()
-        waits.append(copies)
-    return waits
+        every.append(copies)
+    return every
 
 
 def term(held, block, b, s):
@@ -130,10 +129,16 @@
         ]
         for b in range(len(AWAY))
     ]
-    waits = load(zs, range(1, 8), g_ref, noise, held, block, sems)
+    copies = load(zs, range(1, 8), g_ref, noise, held, block, sems)
+    for b in range(AHEAD):
+        for copy in copies[b]:
+            copy.start()
     for b in range(len(AWAY)):
-        for copy in waits[b]:
+        for copy in copies[b]:
             copy.wait()
+        if b + AHEAD < len(AWAY):
+            for copy in copies[b + AHEAD]:
+                copy.start()
         for s in range(NX):
             rows = pl.ds(s * ROWS, ROWS)
             value = term(held, block, b, s)
@@ -183,6 +188,8 @@
         for d in range(NX):
             noise.append(((up, down)[d // 2], d % 2 * ROWS, ROWS, d, 0, left))
     (waits,) = load(zs, (8,), g_ref, [noise], held, block, sems)
+    for copy in waits[NX:] + waits[:NX]:
+        copy.start()
     fetch = []
     for s in range(NX):
         rows = pl.ds(s * ROWS, ROWS)
@@ -323,6 +330,10 @@
     return lax.ppermute(value, "x", [(i, (i + by) % NX) for i in range(NX)])
 
 
+def together(*lists):
+    return lax.optimization_barrier(lists)
+
+
 def body(factor, white_noise, site_class, site_decay, site_angle, site_mix):
     x = lax.axis_index("x")
     z = lax.axis_index("z")
@@ -341,14 +352,16 @@
         start = jnp.concatenate(
             [cut(0, half)] + [round_x(cut(d, half), d) for d in (1, 2, 3)], axis=0
         )
-        blocks = [start, ring(start, 1), ring(start, -1)]
-        if half == 0:
-            site_class, site_decay, site_angle, site_mix, *blocks[1:] = lax.optimization_barrier(
-                (site_class, site_decay, site_angle, site_mix, *blocks[1:])
-            )
-        for _ in range(2):
-            blocks += [ring(blocks[-2], 1), ring(blocks[-1], -1)]
-        steps.append(blocks)
+        steps.append([start, ring(start, 1), ring(start, -1)])
+    first, second = steps
+    site_class, site_decay, site_angle, site_mix, *first[1:] = lax.optimization_barrier(
+        (site_class, site_decay, site_angle, site_mix, *first[1:])
+    )
+    for _ in range(2):
+        first += [ring(first[-2], 1), ring(first[-1], -1)]
+        second[-2:], first[-4:-2] = together(second[-2:], first[-4:-2])
+        second += [ring(second[-2], 1), ring(second[-1], -1)]
+        first[-2:], second[-4:-2] = together(first[-2:], second[-4:-2])
 
     toeplitz, final, gain, one, two, eight = tables(site_decay, site_angle, site_mix)
     by_block = site_class.reshape(NX, NZ, ROWS)
@@ -365,9 +378,10 @@
         own_mask, own_hot, per_row(one, own_hot), per_row(two, own_hot), per_row(eight, own_hot),
         toeplitz, final, gain,
     )
-    scalars, place, for_last, for_filter, *steps[1][5:] = lax.optimization_barrier(
-        (scalars, place, for_last, for_filter, *steps[1][5:])
+    scalars, place, for_last, for_filter, *first[5:] = lax.optimization_barrier(
+        (scalars, place, for_last, for_filter, *first[5:])
     )
+    second[5:], _ = together(second[5:], first[5:])
     opposite = []
     for blocks in steps:
         opposite += [ring(blocks[5][:512], 1), ring(blocks[6][512:], -1)]

time: 163 us -> 158 us (0.969)
  blocking collectives: 25.4 us -> 19.3 us
    all_to_all x1, blocking collectives: 25.4 us -> 19.3 us  [body(): own_ends = lax.all_to_all(to_send, ('y', 'c', 'x'), 0, 0, tiled=True)]
    unnamed x41 -> x39, local copies, waits for them, and re-layouts: 3.47 us -> 3.49 us
  transfers between devices with their start and end apart: 26 -> 26, of which waited for: 6 -> 8; matrix products, arithmetic and copies ran while one was open for 14% -> 15% of each run, Pallas kernels for 6% -> 6%
where the time goes in v1:
time: 158 us
  starting transfers between devices  37.3 us (24%)
  waiting for transfers between devices  37.2 us (24%)
  Pallas kernels  22.3 us (14%)
  blocking collectives  19.3 us (12%)
  local copies, waits for them, and re-layouts  17.3 us (11%)
  between operations  14 us (9%)
  matrix products  6.44 us (4%)
  other arithmetic  4.27 us (3%)
    ppermute x16, starting transfers between devices, ring(): return lax.ppermute(value, 'z', [(i, (i + by) % NZ) for i in range(NZ)])  25 us
    ppermute x16, waiting for transfers between devices, ring(): return lax.ppermute(value, 'z', [(i, (i + by) % NZ) for i in range(NZ)])  24.1 us
    all_to_all x1, blocking collectives, body(): own_ends = lax.all_to_all(to_send, ('y', 'c', 'x'), 0, 0, tiled=True)  19.3 us
    ppermute x9, waiting for transfers between devices, round_x(): return lax.ppermute(value, 'x', [(i, (i + by) % NX) for i in range(NX)])  13 us
    ppermute x9, starting transfers between devices, round_x(): return lax.ppermute(value, 'x', [(i, (i + by) % NX) for i in range(NX)])  12.4 us
    pallas_call x1, Pallas kernels, product(): pl.pallas_call(product_kernel, grid_spec=pltpu.PrefetchScalarGridSpec(num...  10 us
    pallas_call x1, Pallas kernels, filtered(): pl.pallas_call(filter_kernel, grid_spec=pltpu.PrefetchScalarGridSpec(num_...  6.26 us
    pallas_call x1, Pallas kernels, last_product(): pl.pallas_call(last_kernel, grid_spec=pltpu.PrefetchScalarGridSpec(num_sc...  6.04 us
  transfers between devices with their start and end apart: 26, of which 8 were waited for; matrix products, arithmetic and copies ran while one was open for 15% of the time, Pallas kernels for 6%

profile of v1, /device:TPU:1, one launch (start us, length us, event | category | flops | bytes accessed | tf_op | source)
XLA Modules:
  0.0 158.1 jit_solution(15675327040121299522)
XLA Ops:
  6.5 2.0 %constant_dynamic-slice_fusion = bf16[32,8192]{1,0:T(8,128)(2,1)} fusion(bf16[256,8192]{1,0:T(8,128)(2,1)} %param.6, s32[]{:T(128)S(6)} %select_n.87), kind=kLoop, calls=%fused_computation.57 | loop fusion | bytes 1048580 | tf_op jit(solution)/shard_map/dynamic_slice | solution.py:342
  8.8 2.1 %collective-permute-start = (bf16[256,256]{1,0:T(8,128)(2,1)S(1)}, bf16[256,256]{1,0:T(8,128)(2,1)S(1)}, u32[]{:S(2)}, u32[]{:S(2)}) collective-permute-start(bf16[256,256]{1,0:T(8,128)(2,1)S(1)} %get-tuple-element.106), channel_id=1, source_target_pairs={{0,64},{64,128},{128,192},{192,0},{1,65},{65,129},{129,193},{193,1... | collective-permute-start | bytes 393224 | tf_op jit(solution)/shard_map/ppermute | solution.py:330
  10.9 2.5 %collective-permute-start.1 = (bf16[256,256]{1,0:T(8,128)(2,1)S(1)}, bf16[256,256]{1,0:T(8,128)(2,1)S(1)}, u32[]{:S(2)}, u32[]{:S(2)}) collective-permute-start(bf16[256,256]{1,0:T(8,128)(2,1)S(1)} %get-tuple-element.105), channel_id=1, source_target_pairs={{0,128},{64,192},{128,0},{192,64},{1,129},{65,193},{129,1},{193,65... | collective-permute-start | bytes 393224 | tf_op jit(solution)/shard_map/ppermute | solution.py:330
  13.3 1.2 collective-permute-start.2
  14.5 4.5 %collective-permute-done.1 = bf16[256,256]{1,0:T(8,128)(2,1)S(1)} collective-permute-done((bf16[256,256]{1,0:T(8,128)(2,1)S(1)}, bf16[256,256]{1,0:T(8,128)(2,1)S(1)}, u32[]{:S(2)}, u32[]{:S(2)}) %collective-permute-start.1) | collective-permute-done | bytes 131104 | tf_op jit(solution)/shard_map/ppermute | solution.py:330
  19.1 1.7 %collective-permute-start.3 = (bf16[1024,256]{1,0:T(8,128)(2,1)S(1)}, bf16[1024,256]{1,0:T(8,128)(2,1)}, u32[]{:S(2)}, u32[]{:S(2)}) collective-permute-start(bf16[1024,256]{1,0:T(8,128)(2,1)S(1)} %pad_maximum_fusion.refs_0_), channel_id=1, source_target_pairs={{0,8},{8,16},{16,24},{24,32},{32,40},{40,48},{48,56},{56,0},{1,9},... | collective-permute-start | bytes 1572872 | tf_op jit(solution)/shard_map/ppermute | solution.py:326
  20.8 4.0 %collective-permute-start.4 = (bf16[1024,256]{1,0:T(8,128)(2,1)S(1)}, bf16[1024,256]{1,0:T(8,128)(2,1)}, u32[]{:S(2)}, u32[]{:S(2)}) collective-permute-start(bf16[1024,256]{1,0:T(8,128)(2,1)S(1)} %pad_maximum_fusion.refs_0_), channel_id=1, source_target_pairs={{0,56},{8,0},{16,8},{24,16},{32,24},{40,32},{48,40},{56,48},{1,57}... | collective-permute-start | bytes 1572872 | tf_op jit(solution)/shard_map/ppermute | solution.py:326
  24.8 1.2 collective-permute-start.7
  26.0 2.2 %collective-permute-start.8 = (bf16[256,256]{1,0:T(8,128)(2,1)S(1)}, bf16[256,256]{1,0:T(8,128)(2,1)S(1)}, u32[]{:S(2)}, u32[]{:S(2)}) collective-permute-start(bf16[256,256]{1,0:T(8,128)(2,1)S(1)} %get-tuple-element.109), channel_id=1, source_target_pairs={{0,128},{64,192},{128,0},{192,64},{1,129},{65,193},{129,1},{193,65... | collective-permute-start | bytes 393224 | tf_op jit(solution)/shard_map/ppermute | solution.py:330
  28.2 0.5 collective-permute-start.9
  28.7 0.6 stack.92.zs
  29.4 0.7 pad_add_fusion.place
  30.3 6.0 %collective-permute-done.8 = bf16[256,256]{1,0:T(8,128)(2,1)S(1)} collective-permute-done((bf16[256,256]{1,0:T(8,128)(2,1)S(1)}, bf16[256,256]{1,0:T(8,128)(2,1)S(1)}, u32[]{:S(2)}, u32[]{:S(2)}) %collective-permute-start.8) | collective-permute-done | bytes 131104 | tf_op jit(solution)/shard_map/ppermute | solution.py:330
  36.3 2.2 %collective-permute-done.9 = bf16[256,256]{1,0:T(8,128)(2,1)S(1)} collective-permute-done((bf16[256,256]{1,0:T(8,128)(2,1)S(1)}, bf16[256,256]{1,0:T(8,128)(2,1)S(1)}, u32[]{:S(2)}, u32[]{:S(2)}) %collective-permute-start.9) | collective-permute-done | bytes 131104 | tf_op jit(solution)/shard_map/ppermute | solution.py:330
  38.6 2.7 %collective-permute-start.11 = (bf16[1024,256]{1,0:T(8,128)(2,1)S(1)}, bf16[1024,256]{1,0:T(8,128)(2,1)}, u32[]{:S(2)}, u32[]{:S(2)}) collective-permute-start(bf16[1024,256]{1,0:T(8,128)(2,1)S(1)} %pad_maximum_fusion.1.refs_1_), channel_id=1, source_target_pairs={{0,56},{8,0},{16,8},{24,16},{32,24},{40,32},{48,40},{56,48},{1,57}... | collective-permute-start | bytes 1572872 | tf_op jit(solution)/shard_map/ppermute | solution.py:326
  44.0 1.0 convolution_bitcast_fusion.4
  48.1 2.7 %collective-permute-start.6 = (bf16[1024,256]{1,0:T(8,128)(2,1)}, bf16[1024,256]{1,0:T(8,128)(2,1)}, u32[]{:S(2)}, u32[]{:S(2)}) collective-permute-start(bf16[1024,256]{1,0:T(8,128)(2,1)} %collective-permute-done.4.refs_4_), channel_id=1, source_target_pairs={{0,56},{8,0},{16,8},{24,16},{32,24},{40,32},{48,40},{56,48},{1,57}... | collective-permute-start | bytes 1572872 | tf_op jit(solution)/shard_map/ppermute | solution.py:326
  50.8 2.7 %collective-permute-start.15 = (bf16[1024,256]{1,0:T(8,128)(2,1)}, bf16[1024,256]{1,0:T(8,128)(2,1)}, u32[]{:S(2)}, u32[]{:S(2)}) collective-permute-start(bf16[1024,256]{1,0:T(8,128)(2,1)} %collective-permute-done.11.refs_5_), channel_id=1, source_target_pairs={{0,56},{8,0},{16,8},{24,16},{32,24},{40,32},{48,40},{56,48},{1,57}... | collective-permute-start | bytes 1572872 | tf_op jit(solution)/shard_map/ppermute | solution.py:326
  53.5 3.4 %fusion.39 = f32[4,1,256,4]{1,2,3,0:T(8,128)S(1)} fusion(f32[256,4,4,4]{0,2,3,1:T(4,128)S(1)} %concatenate.57, f32[4,4,1,1]{1,2,3,0:T(1,128)S(1)} %bitcast.197), kind=kOutput, calls=%fused_computation.101 | convolution fusion | flops 196608 | bytes 81984 | tf_op jit(solution)/shard_map/ka,jkab->kbj/dot_general | solution.py:56
  56.9 0.6 copy.182
  58.5 0.6 pad_maximum_fusion.3.gain_ref
  59.9 3.0 %collective-permute-done.5.refs_6_ = bf16[1024,256]{1,0:T(8,128)(2,1)} collective-permute-done((bf16[1024,256]{1,0:T(8,128)(2,1)}, bf16[1024,256]{1,0:T(8,128)(2,1)}, u32[]{:S(2)}, u32[]{:S(2)}) %collective-permute-start.5) | collective-permute-done | bytes 524320 | tf_op jit(solution)/shard_map/ppermute | solution.py:326
  62.9 2.7 %collective-permute-start.13 = (bf16[1024,256]{1,0:T(8,128)(2,1)}, bf16[1024,256]{1,0:T(8,128)(2,1)S(1)}, u32[]{:S(2)}, u32[]{:S(2)}) collective-permute-start(bf16[1024,256]{1,0:T(8,128)(2,1)} %collective-permute-done.6.refs_8_), channel_id=1, source_target_pairs={{0,56},{8,0},{16,8},{24,16},{32,24},{40,32},{48,40},{56,48},{1,57}... | collective-permute-start | bytes 1572872 | tf_op jit(solution)/shard_map/ppermute | solution.py:326
  65.6 8.6 %collective-permute-done.14.refs_7_ = bf16[1024,256]{1,0:T(8,128)(2,1)} collective-permute-done((bf16[1024,256]{1,0:T(8,128)(2,1)}, bf16[1024,256]{1,0:T(8,128)(2,1)}, u32[]{:S(2)}, u32[]{:S(2)}) %collective-permute-start.14) | collective-permute-done | bytes 524320 | tf_op jit(solution)/shard_map/ppermute | solution.py:326
  74.1 2.7 %collective-permute-start.19 = (bf16[1024,256]{1,0:T(8,128)(2,1)}, bf16[1024,256]{1,0:T(8,128)(2,1)}, u32[]{:S(2)}, u32[]{:S(2)}) collective-permute-start(bf16[1024,256]{1,0:T(8,128)(2,1)} %collective-permute-done.15.refs_9_), channel_id=1, source_target_pairs={{0,56},{8,0},{16,8},{24,16},{32,24},{40,32},{48,40},{56,48},{1,57}... | collective-permute-start | bytes 1572872 | tf_op jit(solution)/shard_map/ppermute | solution.py:326
  76.8 0.6 pad_bitcast_fusion.final_ref
  77.6 0.8 copy.191
  78.4 0.4 slice.113
  78.8 1.8 %reshape.340 = bf16[4,256,511]{2,1,0:T(8,128)(2,1)S(1)} reshape(bf16[4,130816]{1,0:T(4,128)(2,1)S(1)} %slice.113) | data formatting | bytes 2093056 | tf_op jit(solution)/shard_map/reshape | solution.py:63
  80.6 0.8 slice.114
  81.6 0.9 multiply_reduce_fusion.power_ref
  82.5 0.8 multiply_reduce_fusion.1
  83.3 0.7 fusion.mask_ref
  84.0 1.4 collective-permute-done.12.refs_10_
  85.4 11.2 %collective-permute-done.18.refs_11_ = bf16[1024,256]{1,0:T(8,128)(2,1)} collective-permute-done((bf16[1024,256]{1,0:T(8,128)(2,1)}, bf16[1024,256]{1,0:T(8,128)(2,1)}, u32[]{:S(2)}, u32[]{:S(2)}) %collective-permute-start.18) | collective-permute-done | bytes 524320 | tf_op jit(solution)/shard_map/ppermute | solution.py:326
  96.6 1.0 slice.103
  97.9 1.0 slice.104
  98.9 2.7 %collective-permute-start.21 = (bf16[512,256]{1,0:T(8,128)(2,1)S(1)}, bf16[512,256]{1,0:T(8,128)(2,1)S(1)}, u32[]{:S(2)}, u32[]{:S(2)}) collective-permute-start(bf16[512,256]{1,0:T(8,128)(2,1)S(1)} %slice.104), channel_id=1, source_target_pairs={{0,56},{8,0},{16,8},{24,16},{32,24},{40,32},{48,40},{56,48},{1,57}... | collective-permute-start | bytes 786440 | tf_op jit(solution)/shard_map/ppermute | solution.py:326
  101.6 2.7 %collective-permute-start.17 = (bf16[512,256]{1,0:T(8,128)(2,1)S(1)}, bf16[512,256]{1,0:T(8,128)(2,1)S(1)}, u32[]{:S(2)}, u32[]{:S(2)}) collective-permute-start(bf16[512,256]{1,0:T(8,128)(2,1)S(1)} %slice.102), channel_id=1, source_target_pairs={{0,56},{8,0},{16,8},{24,16},{32,24},{40,32},{48,40},{56,48},{1,57}... | collective-permute-start | bytes 786440 | tf_op jit(solution)/shard_map/ppermute | solution.py:326
  104.3 10.0 %shard_map.64.total_ref = f32[1024,512]{1,0:T(8,128)} custom-call(s32[9]{0:T(128)} %stack.92.zs, bf16[4,256,8192]{2,1,0:T(8,128)(2,1)} %bitcast.181, bf16[1024,256]{1,0:T(8,128)(2,1)} %copy-done, bf16[1024,256]{1,0:T(8,128)(2,1)} %copy-done.1, bf16[1024,256]{1,0:T(8,128)(2,1)} %collective-permute-done.3.refs_2_, ...), custom_call_target="tpu_custom_call" | custom-call | flops 4697620480 | bytes 19922944 | tf_op jit(solution)/shard_map/pallas_call | solution.py:164
  114.4 0.7 copy-done.5
  115.2 0.7 copy-done.8
  115.9 6.0 %shard_map.65 = (bf16[256,512]{1,0:T(8,128)(2,1)}, bf16[256,512]{1,0:T(8,128)(2,1)}, bf16[256,512]{1,0:T(8,128)(2,1)}, bf16[256,512]{1,0:T(8,128)(2,1)}, f32[32,4,256]{2,1,0:T(4,128)}) custom-call(s32[9]{0:T(128)} %stack.92.zs, bf16[4,256,8192]{2,1,0:T(8,128)(2,1)} %bitcast.182, bf16[512,256]{1,0:T(8,128)(2,1)} %copy-done.7, bf16[512,256]{1,0:T(8,128)(2,1)} %copy-done.8, ...), custom_call_target="tpu_custom_call" | custom-call | flops 738197504 | bytes 6291456 | tf_op jit(solution)/shard_map/pallas_call | solution.py:232
  122.3 2.2 %collective-permute-start.23 = (bf16[256,512]{1,0:T(8,128)(2,1)}, bf16[256,512]{1,0:T(8,128)(2,1)S(1)}, u32[]{:S(2)}, u32[]{:S(2)}) collective-permute-start(bf16[256,512]{1,0:T(8,128)(2,1)} %get-tuple-element.82), channel_id=1, source_target_pairs={{0,128},{64,192},{128,0},{192,64},{1,129},{65,193},{129,1},{193,65... | collective-permute-start | bytes 786440 | tf_op jit(solution)/shard_map/ppermute | solution.py:330
  124.4 0.3 collective-permute-start.24
  124.8 19.3 %all_to_all.5.slabs_ref = f32[32,4,256]{2,1,0:T(4,128)} all-to-all(f32[32,4,256]{2,1,0:T(4,128)} %get-tuple-element.84), channel_id=1, replica_groups=mesh['x'=4,'z'=8,'y'=4,'c'=2] {'y','c','x'}, dimensions={0} | all-to-all | bytes 262144 | tf_op jit(solution)/shard_map/all_to_all | solution.py:392
  144.1 0.7 copy-done.15
  145.0 6.3 %shard_map.66 = f32[256,2048]{1,0:T(8,128)} custom-call(s32[2]{0:T(128)} %pad_add_fusion.place, bf16[256,512]{1,0:T(8,128)(2,1)} %get-tuple-element.80.own_ref, bf16[256,512]{1,0:T(8,128)(2,1)} %copy-done.15, bf16[256,512]{1,0:T(8,128)(2,1)} %copy-done.16, bf16[256,512]{1,0:T(8,128)(2,1)} %copy-done.17, f32[32,4,256]{2,1,0:T(4,128)} %all_to_all.5.slabs_ref, ...), custom_call_target="tpu_custom_call" | custom-call | flops 1153433600 | bytes 4194304 | tf_op jit(solution)/shard_map/pallas_call | solution.py:304
  (137 shorter events, 9.5 us)
Async XLA Ops:
  6.5 2.0 %copy-start.4 = (bf16[256,2048]{1,0:T(8,128)(2,1)S(1)}, bf16[256,2048]{1,0:T(8,128)(2,1)}, u32[]{:S(2)}) copy-start(bf16[256,2048]{1,0:T(8,128)(2,1)} %param.7) | copy-start | bytes 3145732
  6.5 97.7 %all-gather.2.cloned.1.call-start = ((), (), s32[]{:S(2)}) async-start(), calls=%async_computation.1 | async-start | bytes 17301504 | tf_op jit(solution)/shard_map/all_gather | solution.py:343
  8.6 32.7 %copy-start.14 = (f32[2,4]{1,0:T(2,128)S(1)}, f32[2,4]{1,0:T(2,128)}, u32[]{:S(2)}) copy-start(f32[2,4]{1,0:T(2,128)} %param.9) | copy-start | bytes 100
  8.6 32.7 %copy-start.13 = (f32[2,4]{1,0:T(2,128)S(1)}, f32[2,4]{1,0:T(2,128)}, u32[]{:S(2)}) copy-start(f32[2,4]{1,0:T(2,128)} %param.10) | copy-start | bytes 100
  8.6 32.9 %copy-start.12 = (f32[4,4]{1,0:T(4,128)S(1)}, f32[4,4]{1,0:T(4,128)}, u32[]{:S(2)}) copy-start(f32[4,4]{1,0:T(4,128)} %param.11) | copy-start | bytes 196
  8.8 5.7 %collective-permute-start = (bf16[256,256]{1,0:T(8,128)(2,1)S(1)}, bf16[256,256]{1,0:T(8,128)(2,1)S(1)}, u32[]{:S(2)}, u32[]{:S(2)}) collective-permute-start(bf16[256,256]{1,0:T(8,128)(2,1)S(1)} %get-tuple-element.106), channel_id=1, source_target_pairs={{0,64},{64,128},{128,192},{192,0},{1,65},{65,129},{129,193},{193,1... | collective-permute-start | bytes 393224 | tf_op jit(solution)/shard_map/ppermute | solution.py:330
  10.9 8.2 %collective-permute-start.1 = (bf16[256,256]{1,0:T(8,128)(2,1)S(1)}, bf16[256,256]{1,0:T(8,128)(2,1)S(1)}, u32[]{:S(2)}, u32[]{:S(2)}) collective-permute-start(bf16[256,256]{1,0:T(8,128)(2,1)S(1)} %get-tuple-element.105), channel_id=1, source_target_pairs={{0,128},{64,192},{128,0},{192,64},{1,129},{65,193},{129,1},{193,65... | collective-permute-start | bytes 393224 | tf_op jit(solution)/shard_map/ppermute | solution.py:330
  13.3 5.7 %collective-permute-start.2 = (bf16[256,256]{1,0:T(8,128)(2,1)S(1)}, bf16[256,256]{1,0:T(8,128)(2,1)S(1)}, u32[]{:S(2)}, u32[]{:S(2)}) collective-permute-start(bf16[256,256]{1,0:T(8,128)(2,1)S(1)} %get-tuple-element.104), channel_id=1, source_target_pairs={{0,192},{64,0},{128,64},{192,128},{1,193},{65,1},{129,65},{193,129... | collective-permute-start | bytes 393224 | tf_op jit(solution)/shard_map/ppermute | solution.py:330
  19.1 37.8 %copy-start = (bf16[1024,256]{1,0:T(8,128)(2,1)}, bf16[1024,256]{1,0:T(8,128)(2,1)S(1)}, u32[]{:S(2)}) copy-start(bf16[1024,256]{1,0:T(8,128)(2,1)S(1)} %pad_maximum_fusion.refs_0_) | copy-start | bytes 1572868
  19.1 22.2 %collective-permute-start.3 = (bf16[1024,256]{1,0:T(8,128)(2,1)S(1)}, bf16[1024,256]{1,0:T(8,128)(2,1)}, u32[]{:S(2)}, u32[]{:S(2)}) collective-permute-start(bf16[1024,256]{1,0:T(8,128)(2,1)S(1)} %pad_maximum_fusion.refs_0_), channel_id=1, source_target_pairs={{0,8},{8,16},{16,24},{24,32},{32,40},{40,48},{48,56},{56,0},{1,9},... | collective-permute-start | bytes 1572872 | tf_op jit(solution)/shard_map/ppermute | solution.py:326
  20.8 20.5 %collective-permute-start.4 = (bf16[1024,256]{1,0:T(8,128)(2,1)S(1)}, bf16[1024,256]{1,0:T(8,128)(2,1)}, u32[]{:S(2)}, u32[]{:S(2)}) collective-permute-start(bf16[1024,256]{1,0:T(8,128)(2,1)S(1)} %pad_maximum_fusion.refs_0_), channel_id=1, source_target_pairs={{0,56},{8,0},{16,8},{24,16},{32,24},{40,32},{48,40},{56,48},{1,57}... | collective-permute-start | bytes 1572872 | tf_op jit(solution)/shard_map/ppermute | solution.py:326
  24.8 5.4 %collective-permute-start.7 = (bf16[256,256]{1,0:T(8,128)(2,1)S(1)}, bf16[256,256]{1,0:T(8,128)(2,1)S(1)}, u32[]{:S(2)}, u32[]{:S(2)}) collective-permute-start(bf16[256,256]{1,0:T(8,128)(2,1)S(1)} %get-tuple-element.103), channel_id=1, source_target_pairs={{0,64},{64,128},{128,192},{192,0},{1,65},{65,129},{129,193},{193,1... | collective-permute-start | bytes 393224 | tf_op jit(solution)/shard_map/ppermute | solution.py:330
  26.0 10.3 %collective-permute-start.8 = (bf16[256,256]{1,0:T(8,128)(2,1)S(1)}, bf16[256,256]{1,0:T(8,128)(2,1)S(1)}, u32[]{:S(2)}, u32[]{:S(2)}) collective-permute-start(bf16[256,256]{1,0:T(8,128)(2,1)S(1)} %get-tuple-element.109), channel_id=1, source_target_pairs={{0,128},{64,192},{128,0},{192,64},{1,129},{65,193},{129,1},{193,65... | collective-permute-start | bytes 393224 | tf_op jit(solution)/shard_map/ppermute | solution.py:330
  28.2 10.3 %collective-permute-start.9 = (bf16[256,256]{1,0:T(8,128)(2,1)S(1)}, bf16[256,256]{1,0:T(8,128)(2,1)S(1)}, u32[]{:S(2)}, u32[]{:S(2)}) collective-permute-start(bf16[256,256]{1,0:T(8,128)(2,1)S(1)} %get-tuple-element.108), channel_id=1, source_target_pairs={{0,192},{64,0},{128,64},{192,128},{1,193},{65,1},{129,65},{193,129... | collective-permute-start | bytes 393224 | tf_op jit(solution)/shard_map/ppermute | solution.py:330
  38.5 18.4 %copy-start.1 = (bf16[1024,256]{1,0:T(8,128)(2,1)}, bf16[1024,256]{1,0:T(8,128)(2,1)S(1)}, u32[]{:S(2)}) copy-start(bf16[1024,256]{1,0:T(8,128)(2,1)S(1)} %pad_maximum_fusion.1.refs_1_) | copy-start | bytes 1572868
  38.5 12.2 %collective-permute-start.10 = (bf16[1024,256]{1,0:T(8,128)(2,1)S(1)}, bf16[1024,256]{1,0:T(8,128)(2,1)}, u32[]{:S(2)}, u32[]{:S(2)}) collective-permute-start(bf16[1024,256]{1,0:T(8,128)(2,1)S(1)} %pad_maximum_fusion.1.refs_1_), channel_id=1, source_target_pairs={{0,8},{8,16},{16,24},{24,32},{32,40},{40,48},{48,56},{56,0},{1,9},... | collective-permute-start | bytes 1572872 | tf_op jit(solution)/shard_map/ppermute | solution.py:326
  38.6 12.1 %collective-permute-start.11 = (bf16[1024,256]{1,0:T(8,128)(2,1)S(1)}, bf16[1024,256]{1,0:T(8,128)(2,1)}, u32[]{:S(2)}, u32[]{:S(2)}) collective-permute-start(bf16[1024,256]{1,0:T(8,128)(2,1)S(1)} %pad_maximum_fusion.1.refs_1_), channel_id=1, source_target_pairs={{0,56},{8,0},{16,8},{24,16},{32,24},{40,32},{48,40},{56,48},{1,57}... | collective-permute-start | bytes 1572872 | tf_op jit(solution)/shard_map/ppermute | solution.py:326
  48.0 14.8 %collective-permute-start.5 = (bf16[1024,256]{1,0:T(8,128)(2,1)}, bf16[1024,256]{1,0:T(8,128)(2,1)}, u32[]{:S(2)}, u32[]{:S(2)}) collective-permute-start(bf16[1024,256]{1,0:T(8,128)(2,1)} %collective-permute-done.3.refs_2_), channel_id=1, source_target_pairs={{0,8},{8,16},{16,24},{24,32},{32,40},{40,48},{48,56},{56,0},{1,9},... | collective-permute-start | bytes 1572872 | tf_op jit(solution)/shard_map/ppermute | solution.py:326
  48.1 14.8 %collective-permute-start.6 = (bf16[1024,256]{1,0:T(8,128)(2,1)}, bf16[1024,256]{1,0:T(8,128)(2,1)}, u32[]{:S(2)}, u32[]{:S(2)}) collective-permute-start(bf16[1024,256]{1,0:T(8,128)(2,1)} %collective-permute-done.4.refs_4_), channel_id=1, source_target_pairs={{0,56},{8,0},{16,8},{24,16},{32,24},{40,32},{48,40},{56,48},{1,57}... | collective-permute-start | bytes 1572872 | tf_op jit(solution)/shard_map/ppermute | solution.py:326
  50.8 23.3 %collective-permute-start.14 = (bf16[1024,256]{1,0:T(8,128)(2,1)}, bf16[1024,256]{1,0:T(8,128)(2,1)}, u32[]{:S(2)}, u32[]{:S(2)}) collective-permute-start(bf16[1024,256]{1,0:T(8,128)(2,1)} %collective-permute-done.10.refs_3_), channel_id=1, source_target_pairs={{0,8},{8,16},{16,24},{24,32},{32,40},{40,48},{48,56},{56,0},{1,9},... | collective-permute-start | bytes 1572872 | tf_op jit(solution)/shard_map/ppermute | solution.py:326
  50.8 23.3 %collective-permute-start.15 = (bf16[1024,256]{1,0:T(8,128)(2,1)}, bf16[1024,256]{1,0:T(8,128)(2,1)}, u32[]{:S(2)}, u32[]{:S(2)}) collective-permute-start(bf16[1024,256]{1,0:T(8,128)(2,1)} %collective-permute-done.11.refs_5_), channel_id=1, source_target_pairs={{0,56},{8,0},{16,8},{24,16},{32,24},{40,32},{48,40},{56,48},{1,57}... | collective-permute-start | bytes 1572872 | tf_op jit(solution)/shard_map/ppermute | solution.py:326
  53.5 4.9 %copy-start.10 = (s32[8192]{0:T(1024)S(1)}, s32[8192]{0:T(1024)}, u32[]{:S(2)}) copy-start(s32[8192]{0:T(1024)} %param.8) | copy-start | bytes 98308
  59.1 23.4 %copy-start.11 = (f32[4,256]{1,0:T(4,128)}, f32[4,256]{1,0:T(4,128)S(1)}, u32[]{:S(2)}) copy-start(f32[4,256]{1,0:T(4,128)S(1)} %fusion.21.onehot_ref) | copy-start | bytes 12292
  59.3 22.3 %copy-start.9 = (f32[4,1024]{1,0:T(4,128)}, f32[4,1024]{1,0:T(4,128)S(1)}, u32[]{:S(2)}) copy-start(f32[4,1024]{1,0:T(4,128)S(1)} %fusion.13.onehot_ref) | copy-start | bytes 49156
  62.9 22.5 %collective-permute-start.12 = (bf16[1024,256]{1,0:T(8,128)(2,1)}, bf16[1024,256]{1,0:T(8,128)(2,1)S(1)}, u32[]{:S(2)}, u32[]{:S(2)}) collective-permute-start(bf16[1024,256]{1,0:T(8,128)(2,1)} %collective-permute-done.5.refs_6_), channel_id=1, source_target_pairs={{0,8},{8,16},{16,24},{24,32},{32,40},{40,48},{48,56},{56,0},{1,9},... | collective-permute-start | bytes 1572872 | tf_op jit(solution)/shard_map/ppermute | solution.py:326
  62.9 22.5 %collective-permute-start.13 = (bf16[1024,256]{1,0:T(8,128)(2,1)}, bf16[1024,256]{1,0:T(8,128)(2,1)S(1)}, u32[]{:S(2)}, u32[]{:S(2)}) collective-permute-start(bf16[1024,256]{1,0:T(8,128)(2,1)} %collective-permute-done.6.refs_8_), channel_id=1, source_target_pairs={{0,56},{8,0},{16,8},{24,16},{32,24},{40,32},{48,40},{56,48},{1,57}... | collective-permute-start | bytes 1572872 | tf_op jit(solution)/shard_map/ppermute | solution.py:326
  74.1 22.5 %collective-permute-start.18 = (bf16[1024,256]{1,0:T(8,128)(2,1)}, bf16[1024,256]{1,0:T(8,128)(2,1)}, u32[]{:S(2)}, u32[]{:S(2)}) collective-permute-start(bf16[1024,256]{1,0:T(8,128)(2,1)} %collective-permute-done.14.refs_7_), channel_id=1, source_target_pairs={{0,8},{8,16},{16,24},{24,32},{32,40},{40,48},{48,56},{56,0},{1,9},... | collective-permute-start | bytes 1572872 | tf_op jit(solution)/shard_map/ppermute | solution.py:326
  74.1 22.5 %collective-permute-start.19 = (bf16[1024,256]{1,0:T(8,128)(2,1)}, bf16[1024,256]{1,0:T(8,128)(2,1)}, u32[]{:S(2)}, u32[]{:S(2)}) collective-permute-start(bf16[1024,256]{1,0:T(8,128)(2,1)} %collective-permute-done.15.refs_9_), channel_id=1, source_target_pairs={{0,56},{8,0},{16,8},{24,16},{32,24},{40,32},{48,40},{56,48},{1,57}... | collective-permute-start | bytes 1572872 | tf_op jit(solution)/shard_map/ppermute | solution.py:326
  85.4 18.9 %copy-start.2 = (bf16[1024,256]{1,0:T(8,128)(2,1)}, bf16[1024,256]{1,0:T(8,128)(2,1)S(1)}, u32[]{:S(2)}) copy-start(bf16[1024,256]{1,0:T(8,128)(2,1)S(1)} %collective-permute-done.12.refs_10_) | copy-start | bytes 1572868
  85.4 18.9 %copy-start.3 = (bf16[1024,256]{1,0:T(8,128)(2,1)}, bf16[1024,256]{1,0:T(8,128)(2,1)S(1)}, u32[]{:S(2)}) copy-start(bf16[1024,256]{1,0:T(8,128)(2,1)S(1)} %collective-permute-done.13.refs_12_) | copy-start | bytes 1572868
  97.6 16.7 %collective-permute-start.20 = (bf16[512,256]{1,0:T(8,128)(2,1)S(1)}, bf16[512,256]{1,0:T(8,128)(2,1)S(1)}, u32[]{:S(2)}, u32[]{:S(2)}) collective-permute-start(bf16[512,256]{1,0:T(8,128)(2,1)S(1)} %slice.103), channel_id=1, source_target_pairs={{0,8},{8,16},{16,24},{24,32},{32,40},{40,48},{48,56},{56,0},{1,9},... | collective-permute-start | bytes 786440 | tf_op jit(solution)/shard_map/ppermute | solution.py:326
  98.9 15.5 %collective-permute-start.21 = (bf16[512,256]{1,0:T(8,128)(2,1)S(1)}, bf16[512,256]{1,0:T(8,128)(2,1)S(1)}, u32[]{:S(2)}, u32[]{:S(2)}) collective-permute-start(bf16[512,256]{1,0:T(8,128)(2,1)S(1)} %slice.104), channel_id=1, source_target_pairs={{0,56},{8,0},{16,8},{24,16},{32,24},{40,32},{48,40},{56,48},{1,57}... | collective-permute-start | bytes 786440 | tf_op jit(solution)/shard_map/ppermute | solution.py:326
  101.6 12.7 %collective-permute-start.16 = (bf16[512,256]{1,0:T(8,128)(2,1)S(1)}, bf16[512,256]{1,0:T(8,128)(2,1)S(1)}, u32[]{:S(2)}, u32[]{:S(2)}) collective-permute-start(bf16[512,256]{1,0:T(8,128)(2,1)S(1)} %slice.101), channel_id=1, source_target_pairs={{0,8},{8,16},{16,24},{24,32},{32,40},{40,48},{48,56},{56,0},{1,9},... | collective-permute-start | bytes 786440 | tf_op jit(solution)/shard_map/ppermute | solution.py:326
  101.6 12.8 %collective-permute-start.17 = (bf16[512,256]{1,0:T(8,128)(2,1)S(1)}, bf16[512,256]{1,0:T(8,128)(2,1)S(1)}, u32[]{:S(2)}, u32[]{:S(2)}) collective-permute-start(bf16[512,256]{1,0:T(8,128)(2,1)S(1)} %slice.102), channel_id=1, source_target_pairs={{0,56},{8,0},{16,8},{24,16},{32,24},{40,32},{48,40},{56,48},{1,57}... | collective-permute-start | bytes 786440 | tf_op jit(solution)/shard_map/ppermute | solution.py:326
  114.3 0.7 copy-start.5
  114.3 0.8 copy-start.6
  114.3 0.9 copy-start.7
  115.2 0.7 copy-start.8
  122.0 22.1 %collective-permute-start.22 = (bf16[256,512]{1,0:T(8,128)(2,1)}, bf16[256,512]{1,0:T(8,128)(2,1)S(1)}, u32[]{:S(2)}, u32[]{:S(2)}) collective-permute-start(bf16[256,512]{1,0:T(8,128)(2,1)} %get-tuple-element.81), channel_id=1, source_target_pairs={{0,64},{64,128},{128,192},{192,0},{1,65},{65,129},{129,193},{193,1... | collective-permute-start | bytes 786440 | tf_op jit(solution)/shard_map/ppermute | solution.py:330
  122.3 21.8 %collective-permute-start.23 = (bf16[256,512]{1,0:T(8,128)(2,1)}, bf16[256,512]{1,0:T(8,128)(2,1)S(1)}, u32[]{:S(2)}, u32[]{:S(2)}) collective-permute-start(bf16[256,512]{1,0:T(8,128)(2,1)} %get-tuple-element.82), channel_id=1, source_target_pairs={{0,128},{64,192},{128,0},{192,64},{1,129},{65,193},{129,1},{193,65... | collective-permute-start | bytes 786440 | tf_op jit(solution)/shard_map/ppermute | solution.py:330
  124.4 19.7 %collective-permute-start.24 = (bf16[256,512]{1,0:T(8,128)(2,1)}, bf16[256,512]{1,0:T(8,128)(2,1)S(1)}, u32[]{:S(2)}, u32[]{:S(2)}) collective-permute-start(bf16[256,512]{1,0:T(8,128)(2,1)} %get-tuple-element.83), channel_id=1, source_target_pairs={{0,192},{64,0},{128,64},{192,128},{1,193},{65,1},{129,65},{193,129... | collective-permute-start | bytes 786440 | tf_op jit(solution)/shard_map/ppermute | solution.py:330
  144.1 0.7 copy-start.15
  144.1 0.8 copy-start.16
  144.1 0.9 copy-start.17
Sparse Core Ops, SparseCore 0:
  9.9 84.2 all-gather.1

commit v2 on v1

--- a/solution.py
+++ b/solution.py
@@ -92,10 +92,11 @@
     for b, z in enumerate(where):
         copies = []
         for q in range(NX):
-            columns = pl.ds(pl.multiple_of(q * NZ * CH + zs[z] * CH, CH), CH)
             copies.append(
                 pltpu.make_async_copy(
-                    g_ref.at[pl.ds(q, NX - q), :, columns], held[q].at[b], sems.at[b, q]
+                    g_ref.at[pl.ds(8 * q, 8 * (NX - q)), q * NZ + zs[z]],
+                    held[q].at[b],
+                    sems.at[b, q],
                 )
             )
         for j, (ref, first, count, by, to, left) in enumerate(noise[b]):
@@ -112,7 +113,9 @@
 
 
 def term(held, block, b, s):
-    parts = [held[q][b, s - q] for q in range(s + 1)]
+    parts = [
+        held[q][b, 8 * (s - q) : 8 * (s - q + 1)].reshape(ROWS, CH) for q in range(s + 1)
+    ]
     rows = jnp.concatenate(parts, axis=1) if s else parts[0]
     noise = block[b, 0 : s + 1].reshape((s + 1) * ROWS, SLAB)
     return jnp.dot(rows, noise, preferred_element_type=F32)
@@ -146,7 +149,7 @@
 
 
 def scratch(blocks):
-    return [pltpu.VMEM((blocks, NX - q, ROWS, CH), BF16) for q in range(NX)] + [
+    return [pltpu.VMEM((blocks, 8 * (NX - q), 32, CH), BF16) for q in range(NX)] + [
         pltpu.VMEM((blocks, NX, ROWS, SLAB), BF16),
         pltpu.SemaphoreType.DMA((blocks, 4 * NX)),
     ]
@@ -179,14 +182,15 @@
 
 
 def last_kernel(
-    zs, g_ref, up_one, down_one, up_two, down_two, total_ref, final_ref, onehot_ref,
+    zs, g_ref, first_ref, second_ref, total_ref, final_ref, onehot_ref,
     power_ref, *refs,
 ):
     piece_refs, (send_ref, local, acc_ref, *held, block, sems) = refs[:NX], refs[NX:]
-    noise = []
-    for left, up, down in ((0, up_one, down_one), (CH, up_two, down_two)):
-        for d in range(NX):
-            noise.append(((up, down)[d // 2], d % 2 * ROWS, ROWS, d, 0, left))
+    noise = [
+        (ref, d * ROWS, ROWS, d, 0, left)
+        for left, ref in ((0, first_ref), (CH, second_ref))
+        for d in range(NX)
+    ]
     (waits,) = load(zs, (8,), g_ref, [noise], held, block, sems)
     for copy in waits[NX:] + waits[:NX]:
         copy.start()
@@ -234,7 +238,7 @@
         grid_spec=pltpu.PrefetchScalarGridSpec(
             num_scalar_prefetch=1,
             grid=(1,),
-            in_specs=[ANYWHERE] * 6 + [whole(a) for a in args],
+            in_specs=[ANYWHERE] * 4 + [whole(a) for a in args],
             out_specs=[whole(a) for a in out_shape],
             scratch_shapes=[
                 pltpu.VMEM((NX, ROWS, SLAB), BF16),
@@ -340,18 +344,18 @@
     tm = lax.axis_index("y") * NCORE + lax.axis_index("c")
 
     share = lax.dynamic_slice(factor, (tm * 32, 0), (32, factor.shape[1]))
+    share = jnp.concatenate([share[:, b * CH : (b + 1) * CH] for b in range(NX * NZ)], axis=0)
     gathered = lax.all_gather(share, ("x", "y", "c"), tiled=True)
-    gathered = gathered.reshape(NX, ROWS, factor.shape[1])
-
-    def cut(by, half):
-        first = lax.rem(x + by, NX) * SLAB + half * CH
-        return lax.dynamic_slice(white_noise, (0, first), (ROWS, CH))
-
+    gathered = gathered.reshape(32, NX * NZ, 32, CH)
+
+    def cut(by):
+        first = lax.rem(x + by, NX) * SLAB
+        return lax.dynamic_slice(white_noise, (0, first), (ROWS, SLAB))
+
+    parts = [cut(0)] + [round_x(cut(d), d) for d in (1, 2, 3)]
     steps = []
     for half in range(2):
-        start = jnp.concatenate(
-            [cut(0, half)] + [round_x(cut(d, half), d) for d in (1, 2, 3)], axis=0
-        )
+        start = jnp.concatenate([p[:, half * CH : (half + 1) * CH] for p in parts], axis=0)
         steps.append([start, ring(start, 1), ring(start, -1)])
     first, second = steps
     site_class, site_decay, site_angle, site_mix, *first[1:] = lax.optimization_barrier(
@@ -378,13 +382,11 @@
         own_mask, own_hot, per_row(one, own_hot), per_row(two, own_hot), per_row(eight, own_hot),
         toeplitz, final, gain,
     )
-    scalars, place, for_last, for_filter, *first[5:] = lax.optimization_barrier(
-        (scalars, place, for_last, for_filter, *first[5:])
+    scalars, place, for_last, for_filter, first[5] = lax.optimization_barrier(
+        (scalars, place, for_last, for_filter, first[5])
     )
-    second[5:], _ = together(second[5:], first[5:])
-    opposite = []
-    for blocks in steps:
-        opposite += [ring(blocks[5][:512], 1), ring(blocks[6][512:], -1)]
+    second[6], _ = together(second[6], first[5])
+    opposite = [ring(first[5], 1), ring(second[6], -1)]
 
     total = product(scalars, gathered, [n for pair in zip(*steps) for n in pair])
     *pieces, to_send = last_product(scalars, gathered, opposite, total, *for_last)

time: 158 us -> 181 us (1.15); the launches traced: 158 us -> 179 us
  local copies, waits for them, and re-layouts: 17.3 us -> 40 us
  starting transfers between devices: 37.3 us -> 35 us
    unnamed x39 -> x68, local copies, waits for them, and re-layouts: 3.49 us -> 27.3 us
    ppermute x16 -> x14, waiting for transfers between devices: 24.1 us -> 29.8 us  [ring(): return lax.ppermute(value, 'z', [(i, (i + by) % NZ) for i in range(NZ)])]
    ppermute x9 -> x6, waiting for transfers between devices: 13 us -> 9.13 us  [round_x(): return lax.ppermute(value, 'x', [(i, (i + by) % NX) for i in range(NX)])]
    ppermute x16 -> x14, starting transfers between devices: 25 us -> 23.3 us  [ring(): return lax.ppermute(value, 'z', [(i, (i + by) % NZ) for i in range(NZ)])]
    ppermute x9 -> x6, starting transfers between devices: 12.4 us -> 11.7 us  [round_x(): return lax.ppermute(value, 'x', [(i, (i + by) % NX) for i in range(NX)])]
  transfers between devices with their start and end apart: 26 -> 21, of which waited for: 8 -> 9; matrix products, arithmetic and copies ran while one was open for 15% -> 13% of each run, Pallas kernels for 6% -> 6%
where the time goes in v2:
time: 181 us; the launch traced here: 179 us
  local copies, waits for them, and re-layouts  40 us (22%)
  waiting for transfers between devices  39 us (22%)
  starting transfers between devices  35 us (19%)
  Pallas kernels  22.2 us (12%)
  blocking collectives  18.4 us (10%)
  between operations  13.9 us (8%)
  matrix products  6.45 us (4%)
  other arithmetic  4.22 us (2%)
    ppermute x14, waiting for transfers between devices, ring(): return lax.ppermute(value, 'z', [(i, (i + by) % NZ) for i in range(NZ)])  29.8 us
    unnamed x68, local copies, waits for them, and re-layouts  27.3 us
    ppermute x14, starting transfers between devices, ring(): return lax.ppermute(value, 'z', [(i, (i + by) % NZ) for i in range(NZ)])  23.3 us
    all_to_all x1, blocking collectives, body(): own_ends = lax.all_to_all(to_send, ('y', 'c', 'x'), 0, 0, tiled=True)  18.4 us
    ppermute x6, starting transfers between devices, round_x(): return lax.ppermute(value, 'x', [(i, (i + by) % NX) for i in range(NX)])  11.7 us
    pallas_call x1, Pallas kernels, product(): pl.pallas_call(product_kernel, grid_spec=pltpu.PrefetchScalarGridSpec(num...  9.94 us
    ppermute x6, waiting for transfers between devices, round_x(): return lax.ppermute(value, 'x', [(i, (i + by) % NX) for i in range(NX)])  9.13 us
    pallas_call x1, Pallas kernels, filtered(): pl.pallas_call(filter_kernel, grid_spec=pltpu.PrefetchScalarGridSpec(num_...  6.26 us
  transfers between devices with their start and end apart: 21, of which 9 were waited for; matrix products, arithmetic and copies ran while one was open for 13% of the time, Pallas kernels for 6%

profile of v2, /device:TPU:1, one launch (start us, length us, event | category | flops | bytes accessed | tf_op | source)
XLA Modules:
  0.0 179.3 jit_solution(2644789421857959671)
XLA Ops:
  6.5 0.7 constant_dynamic-update-slice_fusion.31
  7.3 0.7 constant_dynamic-update-slice_fusion.30
  8.0 0.7 constant_dynamic-update-slice_fusion.29
  8.7 0.7 constant_dynamic-update-slice_fusion.28
  9.5 0.7 constant_dynamic-update-slice_fusion.27
  10.2 0.7 constant_dynamic-update-slice_fusion.26
  10.9 0.7 constant_dynamic-update-slice_fusion.25
  13.8 0.7 constant_dynamic-update-slice_fusion.21
  23.8 0.7 constant_dynamic-update-slice_fusion.7
  26.7 0.7 constant_dynamic-update-slice_fusion.3
  29.6 0.8 copy-done.2
  30.4 1.2 constant_dynamic-slice_fusion.5
  31.6 2.1 %collective-permute-start = (bf16[256,512]{1,0:T(8,128)(2,1)S(1)}, bf16[256,512]{1,0:T(8,128)(2,1)S(1)}, u32[]{:S(2)}, u32[]{:S(2)}) collective-permute-start(bf16[256,512]{1,0:T(8,128)(2,1)S(1)} %get-tuple-element.100), channel_id=1, source_target_pairs={{0,64},{64,128},{128,192},{192,0},{1,65},{65,129},{129,193},{193,1... | collective-permute-start | bytes 786440 | tf_op jit(solution)/shard_map/ppermute | solution.py:334
  33.7 2.5 %collective-permute-start.1 = (bf16[256,512]{1,0:T(8,128)(2,1)S(1)}, bf16[256,512]{1,0:T(8,128)(2,1)S(1)}, u32[]{:S(2)}, u32[]{:S(2)}) collective-permute-start(bf16[256,512]{1,0:T(8,128)(2,1)S(1)} %get-tuple-element.102), channel_id=1, source_target_pairs={{0,128},{64,192},{128,0},{192,64},{1,129},{65,193},{129,1},{193,65... | collective-permute-start | bytes 786440 | tf_op jit(solution)/shard_map/ppermute | solution.py:334
  36.2 1.2 collective-permute-start.2
  37.3 1.0 constant_dynamic-slice_fusion.6
  38.8 8.7 %collective-permute-done.1 = bf16[256,512]{1,0:T(8,128)(2,1)S(1)} collective-permute-done((bf16[256,512]{1,0:T(8,128)(2,1)S(1)}, bf16[256,512]{1,0:T(8,128)(2,1)S(1)}, u32[]{:S(2)}, u32[]{:S(2)}) %collective-permute-start.1) | collective-permute-done | bytes 262176 | tf_op jit(solution)/shard_map/ppermute | solution.py:334
  47.6 1.7 collective-permute-start.3
  49.3 5.1 %collective-permute-start.4 = (bf16[1024,256]{1,0:T(8,128)(2,1)S(1)}, bf16[1024,256]{1,0:T(8,128)(2,1)}, u32[]{:S(2)}, u32[]{:S(2)}) collective-permute-start(bf16[1024,256]{1,0:T(8,128)(2,1)S(1)} %pad_maximum_fusion.refs_0_), channel_id=1, source_target_pairs={{0,56},{8,0},{16,8},{24,16},{32,24},{40,32},{48,40},{56,48},{1,57}... | collective-permute-start | bytes 1572872 | tf_op jit(solution)/shard_map/ppermute | solution.py:330
  55.8 2.7 %collective-permute-start.8 = (bf16[1024,256]{1,0:T(8,128)(2,1)S(1)}, bf16[1024,256]{1,0:T(8,128)(2,1)}, u32[]{:S(2)}, u32[]{:S(2)}) collective-permute-start(bf16[1024,256]{1,0:T(8,128)(2,1)S(1)} %pad_maximum_fusion.1.refs_1_), channel_id=1, source_target_pairs={{0,56},{8,0},{16,8},{24,16},{32,24},{40,32},{48,40},{56,48},{1,57}... | collective-permute-start | bytes 1572872 | tf_op jit(solution)/shard_map/ppermute | solution.py:330
  58.5 6.6 %collective-permute-done.3.refs_2_ = bf16[1024,256]{1,0:T(8,128)(2,1)} collective-permute-done((bf16[1024,256]{1,0:T(8,128)(2,1)S(1)}, bf16[1024,256]{1,0:T(8,128)(2,1)}, u32[]{:S(2)}, u32[]{:S(2)}) %collective-permute-start.3) | collective-permute-done | bytes 524320 | tf_op jit(solution)/shard_map/ppermute | solution.py:330
  67.7 1.0 convolution_bitcast_fusion.4
  72.3 2.7 %collective-permute-start.6 = (bf16[1024,256]{1,0:T(8,128)(2,1)}, bf16[1024,256]{1,0:T(8,128)(2,1)}, u32[]{:S(2)}, u32[]{:S(2)}) collective-permute-start(bf16[1024,256]{1,0:T(8,128)(2,1)} %collective-permute-done.4.refs_4_), channel_id=1, source_target_pairs={{0,56},{8,0},{16,8},{24,16},{32,24},{40,32},{48,40},{56,48},{1,57}... | collective-permute-start | bytes 1572872 | tf_op jit(solution)/shard_map/ppermute | solution.py:330
  74.9 1.3 collective-permute-done.7.refs_3_
  76.3 2.7 %collective-permute-start.12 = (bf16[1024,256]{1,0:T(8,128)(2,1)}, bf16[1024,256]{1,0:T(8,128)(2,1)}, u32[]{:S(2)}, u32[]{:S(2)}) collective-permute-start(bf16[1024,256]{1,0:T(8,128)(2,1)} %collective-permute-done.8.refs_5_), channel_id=1, source_target_pairs={{0,56},{8,0},{16,8},{24,16},{32,24},{40,32},{48,40},{56,48},{1,57}... | collective-permute-start | bytes 1572872 | tf_op jit(solution)/shard_map/ppermute | solution.py:330
  79.7 0.9 multiply_reduce_fusion.power_ref
  81.1 3.4 %fusion.42 = f32[4,1,256,4]{1,2,3,0:T(8,128)S(1)} fusion(f32[256,4,4,4]{0,2,3,1:T(4,128)S(1)} %concatenate.60, f32[4,4,1,1]{1,2,3,0:T(1,128)S(1)} %bitcast.198), kind=kOutput, calls=%fused_computation.132 | convolution fusion | flops 196608 | bytes 81984 | tf_op jit(solution)/shard_map/ka,jkab->kbj/dot_general | solution.py:56
  85.3 1.0 collective-permute-done.5.refs_6_
  86.3 2.5 %collective-permute-start.10 = (bf16[1024,256]{1,0:T(8,128)(2,1)}, bf16[1024,256]{1,0:T(8,128)(2,1)S(1)}, u32[]{:S(2)}, u32[]{:S(2)}) collective-permute-start(bf16[1024,256]{1,0:T(8,128)(2,1)} %collective-permute-done.6.refs_8_), channel_id=1, source_target_pairs={{0,56},{8,0},{16,8},{24,16},{32,24},{40,32},{48,40},{56,48},{1,57}... | collective-permute-start | bytes 1572872 | tf_op jit(solution)/shard_map/ppermute | solution.py:330
  88.8 8.8 %collective-permute-done.11.refs_7_ = bf16[1024,256]{1,0:T(8,128)(2,1)} collective-permute-done((bf16[1024,256]{1,0:T(8,128)(2,1)}, bf16[1024,256]{1,0:T(8,128)(2,1)}, u32[]{:S(2)}, u32[]{:S(2)}) %collective-permute-start.11) | collective-permute-done | bytes 524320 | tf_op jit(solution)/shard_map/ppermute | solution.py:330
  97.5 2.5 %collective-permute-start.14 = (bf16[1024,256]{1,0:T(8,128)(2,1)}, bf16[1024,256]{1,0:T(8,128)(2,1)}, u32[]{:S(2)}, u32[]{:S(2)}) collective-permute-start(bf16[1024,256]{1,0:T(8,128)(2,1)} %collective-permute-done.12.refs_9_), channel_id=1, source_target_pairs={{0,56},{8,0},{16,8},{24,16},{32,24},{40,32},{48,40},{56,48},{1,57}... | collective-permute-start | bytes 1572872 | tf_op jit(solution)/shard_map/ppermute | solution.py:330
  100.8 0.8 copy.191
  102.0 1.8 reshape.340
  103.8 0.8 slice.261
  105.4 0.8 multiply_reduce_fusion.1
  106.3 0.7 fusion.mask_ref
  107.0 0.9 collective-permute-done.10.refs_12_
  107.8 0.9 collective-permute-done.9.refs_10_
  108.8 10.3 %collective-permute-done.14.refs_13_ = bf16[1024,256]{1,0:T(8,128)(2,1)} collective-permute-done((bf16[1024,256]{1,0:T(8,128)(2,1)}, bf16[1024,256]{1,0:T(8,128)(2,1)}, u32[]{:S(2)}, u32[]{:S(2)}) %collective-permute-start.14) | collective-permute-done | bytes 524320 | tf_op jit(solution)/shard_map/ppermute | solution.py:330
  119.1 3.4 %collective-permute-start.15 = (bf16[1024,256]{1,0:T(8,128)(2,1)}, bf16[1024,256]{1,0:T(8,128)(2,1)S(1)}, u32[]{:S(2)}, u32[]{:S(2)}) collective-permute-start(bf16[1024,256]{1,0:T(8,128)(2,1)} %collective-permute-done.14.refs_13_), channel_id=1, source_target_pairs={{0,56},{8,0},{16,8},{24,16},{32,24},{40,32},{48,40},{56,48},{1,57}... | collective-permute-start | bytes 1572872 | tf_op jit(solution)/shard_map/ppermute | solution.py:330
  122.6 0.7 copy-done.5
  123.3 9.9 %shard_map.64.total_ref = f32[1024,512]{1,0:T(8,128)} custom-call(s32[9]{0:T(128)} %stack.92.zs, bf16[32,32,32,256]{3,2,1,0:T(8,128)(2,1)} %bitcast.181, bf16[1024,256]{1,0:T(8,128)(2,1)} %copy-done, bf16[1024,256]{1,0:T(8,128)(2,1)} %copy-done.1, bf16[1024,256]{1,0:T(8,128)(2,1)} %collective-permute-done.3.refs_2_, ...), custom_call_target="tpu_custom_call" | custom-call | flops 4697620480 | bytes 19922944 | tf_op jit(solution)/shard_map/pallas_call | solution.py:167
  133.3 0.8 copy-done.6
  134.0 0.8 copy-done.7
  134.8 6.0 %shard_map.65 = (bf16[256,512]{1,0:T(8,128)(2,1)}, bf16[256,512]{1,0:T(8,128)(2,1)}, bf16[256,512]{1,0:T(8,128)(2,1)}, bf16[256,512]{1,0:T(8,128)(2,1)}, f32[32,4,256]{2,1,0:T(4,128)}) custom-call(s32[9]{0:T(128)} %stack.92.zs, bf16[32,32,32,256]{3,2,1,0:T(8,128)(2,1)} %bitcast.182, bf16[1024,256]{1,0:T(8,128)(2,1)} %copy-done.7, ...), custom_call_target="tpu_custom_call" | custom-call | flops 738197504 | bytes 6291456 | tf_op jit(solution)/shard_map/pallas_call | solution.py:236
  140.9 5.9 %collective-permute-start.18 = (bf16[256,512]{1,0:T(8,128)(2,1)}, bf16[256,512]{1,0:T(8,128)(2,1)S(1)}, u32[]{:S(2)}, u32[]{:S(2)}) collective-permute-start(bf16[256,512]{1,0:T(8,128)(2,1)} %get-tuple-element.78), channel_id=1, source_target_pairs={{0,128},{64,192},{128,0},{192,64},{1,129},{65,193},{129,1},{193,65... | collective-permute-start | bytes 786440 | tf_op jit(solution)/shard_map/ppermute | solution.py:334
  146.8 18.4 %all_to_all.5.slabs_ref = f32[32,4,256]{2,1,0:T(4,128)} all-to-all(f32[32,4,256]{2,1,0:T(4,128)} %get-tuple-element.80), channel_id=1, replica_groups=mesh['x'=4,'z'=8,'y'=4,'c'=2] {'y','c','x'}, dimensions={0} | all-to-all | bytes 262144 | tf_op jit(solution)/shard_map/all_to_all | solution.py:394
  166.2 6.3 %shard_map.66 = f32[256,2048]{1,0:T(8,128)} custom-call(s32[2]{0:T(128)} %pad_add_fusion.place, bf16[256,512]{1,0:T(8,128)(2,1)} %get-tuple-element.76.own_ref, bf16[256,512]{1,0:T(8,128)(2,1)} %copy-done.14, bf16[256,512]{1,0:T(8,128)(2,1)} %copy-done.15, bf16[256,512]{1,0:T(8,128)(2,1)} %copy-done.16, f32[32,4,256]{2,1,0:T(4,128)} %all_to_all.5.slabs_ref, ...), custom_call_target="tpu_custom_call" | custom-call | flops 1153433600 | bytes 4194304 | tf_op jit(solution)/shard_map/pallas_call | solution.py:308
  (156 shorter events, 28.8 us)
Async XLA Ops:
  6.5 58.5 %copy-start.12 = (f32[2,4]{1,0:T(2,128)S(1)}, f32[2,4]{1,0:T(2,128)}, u32[]{:S(2)}) copy-start(f32[2,4]{1,0:T(2,128)} %param.10) | copy-start | bytes 100
  6.5 58.7 %copy-start.11 = (f32[4,4]{1,0:T(4,128)S(1)}, f32[4,4]{1,0:T(4,128)}, u32[]{:S(2)}) copy-start(f32[4,4]{1,0:T(4,128)} %param.11) | copy-start | bytes 196
  6.5 58.5 %copy-start.13 = (f32[2,4]{1,0:T(2,128)S(1)}, f32[2,4]{1,0:T(2,128)}, u32[]{:S(2)}) copy-start(f32[2,4]{1,0:T(2,128)} %param.9) | copy-start | bytes 100
  6.5 116.0 %all-gather.2.cloned.1.call-start = ((), (), s32[]{:S(2)}) async-start(), calls=%async_computation.1 | async-start | bytes 17301504 | tf_op jit(solution)/shard_map/all_gather | solution.py:348
  29.6 0.8 copy-start.2
  30.4 49.2 %copy-start.9 = (s32[8192]{0:T(1024)S(1)}, s32[8192]{0:T(1024)}, u32[]{:S(2)}) copy-start(s32[8192]{0:T(1024)} %param.8) | copy-start | bytes 98308
  31.6 7.1 %collective-permute-start = (bf16[256,512]{1,0:T(8,128)(2,1)S(1)}, bf16[256,512]{1,0:T(8,128)(2,1)S(1)}, u32[]{:S(2)}, u32[]{:S(2)}) collective-permute-start(bf16[256,512]{1,0:T(8,128)(2,1)S(1)} %get-tuple-element.100), channel_id=1, source_target_pairs={{0,64},{64,128},{128,192},{192,0},{1,65},{65,129},{129,193},{193,1... | collective-permute-start | bytes 786440 | tf_op jit(solution)/shard_map/ppermute | solution.py:334
  33.7 13.7 %collective-permute-start.1 = (bf16[256,512]{1,0:T(8,128)(2,1)S(1)}, bf16[256,512]{1,0:T(8,128)(2,1)S(1)}, u32[]{:S(2)}, u32[]{:S(2)}) collective-permute-start(bf16[256,512]{1,0:T(8,128)(2,1)S(1)} %get-tuple-element.102), channel_id=1, source_target_pairs={{0,128},{64,192},{128,0},{192,64},{1,129},{65,193},{129,1},{193,65... | collective-permute-start | bytes 786440 | tf_op jit(solution)/shard_map/ppermute | solution.py:334
  36.2 11.3 %collective-permute-start.2 = (bf16[256,512]{1,0:T(8,128)(2,1)S(1)}, bf16[256,512]{1,0:T(8,128)(2,1)S(1)}, u32[]{:S(2)}, u32[]{:S(2)}) collective-permute-start(bf16[256,512]{1,0:T(8,128)(2,1)S(1)} %get-tuple-element.101), channel_id=1, source_target_pairs={{0,192},{64,0},{128,64},{192,128},{1,193},{65,1},{129,65},{193,129... | collective-permute-start | bytes 786440 | tf_op jit(solution)/shard_map/ppermute | solution.py:334
  47.6 37.6 %copy-start = (bf16[1024,256]{1,0:T(8,128)(2,1)}, bf16[1024,256]{1,0:T(8,128)(2,1)S(1)}, u32[]{:S(2)}) copy-start(bf16[1024,256]{1,0:T(8,128)(2,1)S(1)} %pad_maximum_fusion.refs_0_) | copy-start | bytes 1572868
  47.6 17.5 %collective-permute-start.3 = (bf16[1024,256]{1,0:T(8,128)(2,1)S(1)}, bf16[1024,256]{1,0:T(8,128)(2,1)}, u32[]{:S(2)}, u32[]{:S(2)}) collective-permute-start(bf16[1024,256]{1,0:T(8,128)(2,1)S(1)} %pad_maximum_fusion.refs_0_), channel_id=1, source_target_pairs={{0,8},{8,16},{16,24},{24,32},{32,40},{40,48},{48,56},{56,0},{1,9},... | collective-permute-start | bytes 1572872 | tf_op jit(solution)/shard_map/ppermute | solution.py:330
  49.3 15.8 %collective-permute-start.4 = (bf16[1024,256]{1,0:T(8,128)(2,1)S(1)}, bf16[1024,256]{1,0:T(8,128)(2,1)}, u32[]{:S(2)}, u32[]{:S(2)}) collective-permute-start(bf16[1024,256]{1,0:T(8,128)(2,1)S(1)} %pad_maximum_fusion.refs_0_), channel_id=1, source_target_pairs={{0,56},{8,0},{16,8},{24,16},{32,24},{40,32},{48,40},{56,48},{1,57}... | collective-permute-start | bytes 1572872 | tf_op jit(solution)/shard_map/ppermute | solution.py:330
  55.7 29.6 %copy-start.1 = (bf16[1024,256]{1,0:T(8,128)(2,1)}, bf16[1024,256]{1,0:T(8,128)(2,1)S(1)}, u32[]{:S(2)}) copy-start(bf16[1024,256]{1,0:T(8,128)(2,1)S(1)} %pad_maximum_fusion.1.refs_1_) | copy-start | bytes 1572868
  55.7 20.6 %collective-permute-start.7 = (bf16[1024,256]{1,0:T(8,128)(2,1)S(1)}, bf16[1024,256]{1,0:T(8,128)(2,1)}, u32[]{:S(2)}, u32[]{:S(2)}) collective-permute-start(bf16[1024,256]{1,0:T(8,128)(2,1)S(1)} %pad_maximum_fusion.1.refs_1_), channel_id=1, source_target_pairs={{0,8},{8,16},{16,24},{24,32},{32,40},{40,48},{48,56},{56,0},{1,9},... | collective-permute-start | bytes 1572872 | tf_op jit(solution)/shard_map/ppermute | solution.py:330
  55.8 20.5 %collective-permute-start.8 = (bf16[1024,256]{1,0:T(8,128)(2,1)S(1)}, bf16[1024,256]{1,0:T(8,128)(2,1)}, u32[]{:S(2)}, u32[]{:S(2)}) collective-permute-start(bf16[1024,256]{1,0:T(8,128)(2,1)S(1)} %pad_maximum_fusion.1.refs_1_), channel_id=1, source_target_pairs={{0,56},{8,0},{16,8},{24,16},{32,24},{40,32},{48,40},{56,48},{1,57}... | collective-permute-start | bytes 1572872 | tf_op jit(solution)/shard_map/ppermute | solution.py:330
  72.2 14.1 %collective-permute-start.5 = (bf16[1024,256]{1,0:T(8,128)(2,1)}, bf16[1024,256]{1,0:T(8,128)(2,1)}, u32[]{:S(2)}, u32[]{:S(2)}) collective-permute-start(bf16[1024,256]{1,0:T(8,128)(2,1)} %collective-permute-done.3.refs_2_), channel_id=1, source_target_pairs={{0,8},{8,16},{16,24},{24,32},{32,40},{40,48},{48,56},{56,0},{1,9},... | collective-permute-start | bytes 1572872 | tf_op jit(solution)/shard_map/ppermute | solution.py:330
  72.3 14.0 %collective-permute-start.6 = (bf16[1024,256]{1,0:T(8,128)(2,1)}, bf16[1024,256]{1,0:T(8,128)(2,1)}, u32[]{:S(2)}, u32[]{:S(2)}) collective-permute-start(bf16[1024,256]{1,0:T(8,128)(2,1)} %collective-permute-done.4.refs_4_), channel_id=1, source_target_pairs={{0,56},{8,0},{16,8},{24,16},{32,24},{40,32},{48,40},{56,48},{1,57}... | collective-permute-start | bytes 1572872 | tf_op jit(solution)/shard_map/ppermute | solution.py:330
  76.3 21.3 %collective-permute-start.11 = (bf16[1024,256]{1,0:T(8,128)(2,1)}, bf16[1024,256]{1,0:T(8,128)(2,1)}, u32[]{:S(2)}, u32[]{:S(2)}) collective-permute-start(bf16[1024,256]{1,0:T(8,128)(2,1)} %collective-permute-done.7.refs_3_), channel_id=1, source_target_pairs={{0,8},{8,16},{16,24},{24,32},{32,40},{40,48},{48,56},{56,0},{1,9},... | collective-permute-start | bytes 1572872 | tf_op jit(solution)/shard_map/ppermute | solution.py:330
  76.3 21.3 %collective-permute-start.12 = (bf16[1024,256]{1,0:T(8,128)(2,1)}, bf16[1024,256]{1,0:T(8,128)(2,1)}, u32[]{:S(2)}, u32[]{:S(2)}) collective-permute-start(bf16[1024,256]{1,0:T(8,128)(2,1)} %collective-permute-done.8.refs_5_), channel_id=1, source_target_pairs={{0,56},{8,0},{16,8},{24,16},{32,24},{40,32},{48,40},{56,48},{1,57}... | collective-permute-start | bytes 1572872 | tf_op jit(solution)/shard_map/ppermute | solution.py:330
  79.7 22.3 %copy-start.8 = (f32[4,1024]{1,0:T(4,128)}, f32[4,1024]{1,0:T(4,128)S(1)}, u32[]{:S(2)}) copy-start(f32[4,1024]{1,0:T(4,128)S(1)} %fusion.13.onehot_ref) | copy-start | bytes 49156
  80.6 24.9 %copy-start.10 = (f32[4,256]{1,0:T(4,128)}, f32[4,256]{1,0:T(4,128)S(1)}, u32[]{:S(2)}) copy-start(f32[4,256]{1,0:T(4,128)S(1)} %fusion.21.onehot_ref) | copy-start | bytes 12292
  86.3 21.5 %collective-permute-start.10 = (bf16[1024,256]{1,0:T(8,128)(2,1)}, bf16[1024,256]{1,0:T(8,128)(2,1)S(1)}, u32[]{:S(2)}, u32[]{:S(2)}) collective-permute-start(bf16[1024,256]{1,0:T(8,128)(2,1)} %collective-permute-done.6.refs_8_), channel_id=1, source_target_pairs={{0,56},{8,0},{16,8},{24,16},{32,24},{40,32},{48,40},{56,48},{1,57}... | collective-permute-start | bytes 1572872 | tf_op jit(solution)/shard_map/ppermute | solution.py:330
  88.8 20.0 %collective-permute-start.9 = (bf16[1024,256]{1,0:T(8,128)(2,1)}, bf16[1024,256]{1,0:T(8,128)(2,1)S(1)}, u32[]{:S(2)}, u32[]{:S(2)}) collective-permute-start(bf16[1024,256]{1,0:T(8,128)(2,1)} %collective-permute-done.5.refs_6_), channel_id=1, source_target_pairs={{0,8},{8,16},{16,24},{24,32},{32,40},{40,48},{48,56},{56,0},{1,9},... | collective-permute-start | bytes 1572872 | tf_op jit(solution)/shard_map/ppermute | solution.py:330
  97.5 21.5 %collective-permute-start.14 = (bf16[1024,256]{1,0:T(8,128)(2,1)}, bf16[1024,256]{1,0:T(8,128)(2,1)}, u32[]{:S(2)}, u32[]{:S(2)}) collective-permute-start(bf16[1024,256]{1,0:T(8,128)(2,1)} %collective-permute-done.12.refs_9_), channel_id=1, source_target_pairs={{0,56},{8,0},{16,8},{24,16},{32,24},{40,32},{48,40},{56,48},{1,57}... | collective-permute-start | bytes 1572872 | tf_op jit(solution)/shard_map/ppermute | solution.py:330
  104.8 17.7 %collective-permute-start.16 = (bf16[1024,256]{1,0:T(8,128)(2,1)}, bf16[1024,256]{1,0:T(8,128)(2,1)S(1)}, u32[]{:S(2)}, u32[]{:S(2)}) collective-permute-start(bf16[1024,256]{1,0:T(8,128)(2,1)} %collective-permute-done.11.refs_7_), channel_id=1, source_target_pairs={{0,8},{8,16},{16,24},{24,32},{32,40},{40,48},{48,56},{56,0},{1,9},... | collective-permute-start | bytes 1572872 | tf_op jit(solution)/shard_map/ppermute | solution.py:330
  107.8 14.7 %copy-start.4 = (bf16[1024,256]{1,0:T(8,128)(2,1)}, bf16[1024,256]{1,0:T(8,128)(2,1)S(1)}, u32[]{:S(2)}) copy-start(bf16[1024,256]{1,0:T(8,128)(2,1)S(1)} %collective-permute-done.10.refs_12_) | copy-start | bytes 1572868
  108.8 13.8 %copy-start.3 = (bf16[1024,256]{1,0:T(8,128)(2,1)}, bf16[1024,256]{1,0:T(8,128)(2,1)S(1)}, u32[]{:S(2)}) copy-start(bf16[1024,256]{1,0:T(8,128)(2,1)S(1)} %collective-permute-done.9.refs_10_) | copy-start | bytes 1572868
  119.1 14.2 %collective-permute-start.15 = (bf16[1024,256]{1,0:T(8,128)(2,1)}, bf16[1024,256]{1,0:T(8,128)(2,1)S(1)}, u32[]{:S(2)}, u32[]{:S(2)}) collective-permute-start(bf16[1024,256]{1,0:T(8,128)(2,1)} %collective-permute-done.14.refs_13_), channel_id=1, source_target_pairs={{0,56},{8,0},{16,8},{24,16},{32,24},{40,32},{48,40},{56,48},{1,57}... | collective-permute-start | bytes 1572872 | tf_op jit(solution)/shard_map/ppermute | solution.py:330
  122.5 10.8 %collective-permute-start.13 = (bf16[1024,256]{1,0:T(8,128)(2,1)S(1)}, bf16[1024,256]{1,0:T(8,128)(2,1)S(1)}, u32[]{:S(2)}, u32[]{:S(2)}) collective-permute-start(bf16[1024,256]{1,0:T(8,128)(2,1)S(1)} %collective-permute-done.9.refs_10_), channel_id=1, source_target_pairs={{0,8},{8,16},{16,24},{24,32},{32,40},{40,48},{48,56},{56,0},{1,9},... | collective-permute-start | bytes 1572872 | tf_op jit(solution)/shard_map/ppermute | solution.py:330
  122.5 0.8 copy-start.5
  133.2 0.8 copy-start.6
  134.0 0.8 copy-start.7
  140.8 24.4 %collective-permute-start.17 = (bf16[256,512]{1,0:T(8,128)(2,1)}, bf16[256,512]{1,0:T(8,128)(2,1)S(1)}, u32[]{:S(2)}, u32[]{:S(2)}) collective-permute-start(bf16[256,512]{1,0:T(8,128)(2,1)} %get-tuple-element.77), channel_id=1, source_target_pairs={{0,64},{64,128},{128,192},{192,0},{1,65},{65,129},{129,193},{193,1... | collective-permute-start | bytes 786440 | tf_op jit(solution)/shard_map/ppermute | solution.py:334
  140.9 24.3 %collective-permute-start.18 = (bf16[256,512]{1,0:T(8,128)(2,1)}, bf16[256,512]{1,0:T(8,128)(2,1)S(1)}, u32[]{:S(2)}, u32[]{:S(2)}) collective-permute-start(bf16[256,512]{1,0:T(8,128)(2,1)} %get-tuple-element.78), channel_id=1, source_target_pairs={{0,128},{64,192},{128,0},{192,64},{1,129},{65,193},{129,1},{193,65... | collective-permute-start | bytes 786440 | tf_op jit(solution)/shard_map/ppermute | solution.py:334
  146.8 18.4 %collective-permute-start.19 = (bf16[256,512]{1,0:T(8,128)(2,1)}, bf16[256,512]{1,0:T(8,128)(2,1)S(1)}, u32[]{:S(2)}, u32[]{:S(2)}) collective-permute-start(bf16[256,512]{1,0:T(8,128)(2,1)} %get-tuple-element.79), channel_id=1, source_target_pairs={{0,192},{64,0},{128,64},{192,128},{1,193},{65,1},{129,65},{193,129... | collective-permute-start | bytes 786440 | tf_op jit(solution)/shard_map/ppermute | solution.py:334
  165.2 0.7 copy-start.14
  165.2 0.8 copy-start.15
  165.3 0.9 copy-start.16
Sparse Core Ops, SparseCore 0:
  30.5 82.2 all-gather.1

commit v3 on v2

--- a/solution.py
+++ b/solution.py
@@ -92,47 +92,40 @@
     for b, z in enumerate(where):
         copies = []
         for q in range(NX):
+            columns = pl.ds(pl.multiple_of(q * NZ * CH + zs[z] * CH, CH), CH)
             copies.append(
                 pltpu.make_async_copy(
-                    g_ref.at[pl.ds(8 * q, 8 * (NX - q)), q * NZ + zs[z]],
-                    held[q].at[b],
-                    sems.at[b, q],
+                    g_ref.at[pl.ds(q, NX - q), :, columns], held[q].at[b], sems.at[b, q]
                 )
             )
-        for j, (ref, first, count, by, to, left) in enumerate(noise[b]):
-            owner = lax.rem(zs[0] + NX - by, NX)
+        for half in range(2):
             copies.append(
                 pltpu.make_async_copy(
-                    ref.at[pl.ds(first, count)],
-                    block.at[b, owner, pl.ds(to, count), pl.ds(left, CH)],
-                    sems.at[b, NX + j],
+                    noise[2 * b + half], block.at[b, half], sems.at[b, NX + half]
                 )
             )
         every.append(copies)
     return every
 
 
-def term(held, block, b, s):
-    parts = [
-        held[q][b, 8 * (s - q) : 8 * (s - q + 1)].reshape(ROWS, CH) for q in range(s + 1)
-    ]
+def term(zs, held, block, b, s):
+    parts = [held[q][b, s - q] for q in range(s + 1)]
     rows = jnp.concatenate(parts, axis=1) if s else parts[0]
-    noise = block[b, 0 : s + 1].reshape((s + 1) * ROWS, SLAB)
+    turns = [pl.multiple_of(lax.rem(zs[0] + NX - q, NX) * ROWS, ROWS) for q in range(s + 1)]
+    noise = jnp.concatenate(
+        [
+            jnp.concatenate([block[b, half, pl.ds(t, ROWS), :] for half in range(2)], axis=1)
+            for t in turns
+        ],
+        axis=0,
+    )
     return jnp.dot(rows, noise, preferred_element_type=F32)
 
 
 def product_kernel(zs, g_ref, *refs):
     count = 2 * len(AWAY)
     noise_refs, (out_ref, *held, block, sems) = refs[:count], refs[count:]
-    noise = [
-        [
-            (noise_refs[2 * b + half], d * ROWS, ROWS, d, 0, half * CH)
-            for half in range(2)
-            for d in range(NX)
-        ]
-        for b in range(len(AWAY))
-    ]
-    copies = load(zs, range(1, 8), g_ref, noise, held, block, sems)
+    copies = load(zs, range(1, 8), g_ref, noise_refs, held, block, sems)
     for b in range(AHEAD):
         for copy in copies[b]:
             copy.start()
@@ -144,14 +137,14 @@
                 copy.start()
         for s in range(NX):
             rows = pl.ds(s * ROWS, ROWS)
-            value = term(held, block, b, s)
+            value = term(zs, held, block, b, s)
             out_ref[rows, :] = value if b == 0 else out_ref[rows, :] + value
 
 
 def scratch(blocks):
-    return [pltpu.VMEM((blocks, 8 * (NX - q), 32, CH), BF16) for q in range(NX)] + [
-        pltpu.VMEM((blocks, NX, ROWS, SLAB), BF16),
-        pltpu.SemaphoreType.DMA((blocks, 4 * NX)),
+    return [pltpu.VMEM((blocks, NX - q, ROWS, CH), BF16) for q in range(NX)] + [
+        pltpu.VMEM((blocks, 2, NX * ROWS, CH), BF16),
+        pltpu.SemaphoreType.DMA((blocks, 3 * NX)),
     ]
 
 
@@ -186,19 +179,14 @@
     power_ref, *refs,
 ):
     piece_refs, (send_ref, local, acc_ref, *held, block, sems) = refs[:NX], refs[NX:]
-    noise = [
-        (ref, d * ROWS, ROWS, d, 0, left)
-        for left, ref in ((0, first_ref), (CH, second_ref))
-        for d in range(NX)
-    ]
-    (waits,) = load(zs, (8,), g_ref, [noise], held, block, sems)
+    (waits,) = load(zs, (8,), g_ref, (first_ref, second_ref), held, block, sems)
     for copy in waits[NX:] + waits[:NX]:
         copy.start()
     fetch = []
     for s in range(NX):
         rows = pl.ds(s * ROWS, ROWS)
         fetch.append(
-            pltpu.make_async_copy(total_ref.at[rows], acc_ref.at[rows], sems.at[0, 3 * NX + s])
+            pltpu.make_async_copy(total_ref.at[rows], acc_ref.at[rows], sems.at[0, 2 * NX + s])
         )
         fetch[s].start()
     for copy in waits[NX:]:
@@ -207,7 +195,7 @@
         waits[s].wait()
         fetch[s].wait()
         rows = pl.ds(s * ROWS, ROWS)
-        local[s] = (acc_ref[rows, :] + term(held, block, 0, s)).astype(BF16)
+        local[s] = (acc_ref[rows, :] + term(zs, held, block, 0, s)).astype(BF16)
     for d in range(NX):
         piece_refs[d][...] = local[lax.rem(zs[0] + d, NX)]
     for s in range(NX):
@@ -344,9 +332,8 @@
     tm = lax.axis_index("y") * NCORE + lax.axis_index("c")
 
     share = lax.dynamic_slice(factor, (tm * 32, 0), (32, factor.shape[1]))
-    share = jnp.concatenate([share[:, b * CH : (b + 1) * CH] for b in range(NX * NZ)], axis=0)
     gathered = lax.all_gather(share, ("x", "y", "c"), tiled=True)
-    gathered = gathered.reshape(32, NX * NZ, 32, CH)
+    gathered = gathered.reshape(NX, ROWS, factor.shape[1])
 
     def cut(by):
         first = lax.rem(x + by, NX) * SLAB

time: 181 us -> 155 us (0.86)
  local copies, waits for them, and re-layouts: 40 us -> 16.2 us
    unnamed x68 -> x37, local copies, waits for them, and re-layouts: 27.3 us -> 4.3 us
    dynamic_slice x0 -> x1, local copies, waits for them, and re-layouts: none -> 1.96 us  [body(): share = lax.dynamic_slice(factor, (tm * 32, 0), (32, factor.shape[1]))]
  transfers between devices with their start and end apart: 21 -> 21, of which waited for: 9 -> 9; matrix products, arithmetic and copies ran while one was open for 13% -> 14% of each run, Pallas kernels for 6% -> 6%
where the time goes in v3:
time: 155 us
  waiting for transfers between devices  40 us (26%)
  starting transfers between devices  33.8 us (22%)
  Pallas kernels  21.9 us (14%)
  blocking collectives  18.1 us (12%)
  local copies, waits for them, and re-layouts  16.2 us (10%)
  between operations  13.9 us (9%)
  matrix products  6.45 us (4%)
  other arithmetic  4.22 us (3%)
    ppermute x14, waiting for transfers between devices, ring(): return lax.ppermute(value, 'z', [(i, (i + by) % NZ) for i in range(NZ)])  29.8 us
    ppermute x14, starting transfers between devices, ring(): return lax.ppermute(value, 'z', [(i, (i + by) % NZ) for i in range(NZ)])  22.3 us
    all_to_all x1, blocking collectives, body(): own_ends = lax.all_to_all(to_send, ('y', 'c', 'x'), 0, 0, tiled=True)  18.1 us
    ppermute x6, starting transfers between devices, round_x(): return lax.ppermute(value, 'x', [(i, (i + by) % NX) for i in range(NX)])  11.5 us
    ppermute x6, waiting for transfers between devices, round_x(): return lax.ppermute(value, 'x', [(i, (i + by) % NX) for i in range(NX)])  10.1 us
    pallas_call x1, Pallas kernels, product(): pl.pallas_call(product_kernel, grid_spec=pltpu.PrefetchScalarGridSpec(num...  9.77 us
    pallas_call x1, Pallas kernels, filtered(): pl.pallas_call(filter_kernel, grid_spec=pltpu.PrefetchScalarGridSpec(num_...  6.26 us
    pallas_call x1, Pallas kernels, last_product(): pl.pallas_call(last_kernel, grid_spec=pltpu.PrefetchScalarGridSpec(num_sc...  5.88 us
  transfers between devices with their start and end apart: 21, of which 9 were waited for; matrix products, arithmetic and copies ran while one was open for 14% of the time, Pallas kernels for 6%

profile of v3, /device:TPU:1, one launch (start us, length us, event | category | flops | bytes accessed | tf_op | source)
XLA Modules:
  0.0 154.6 jit_solution(6740562760405553788)
XLA Ops:
  6.5 2.0 %constant_dynamic-slice_fusion.1 = bf16[32,8192]{1,0:T(8,128)(2,1)} fusion(bf16[256,8192]{1,0:T(8,128)(2,1)} %param.6, s32[]{:T(128)S(6)} %select_n.71), kind=kLoop, calls=%fused_computation.62 | loop fusion | bytes 1048580 | tf_op jit(solution)/shard_map/dynamic_slice | solution.py:334
  8.6 2.1 %collective-permute-start = (bf16[256,512]{1,0:T(8,128)(2,1)S(1)}, bf16[256,512]{1,0:T(8,128)(2,1)S(1)}, u32[]{:S(2)}, u32[]{:S(2)}) collective-permute-start(bf16[256,512]{1,0:T(8,128)(2,1)S(1)} %get-tuple-element.100), channel_id=1, source_target_pairs={{0,64},{64,128},{128,192},{192,0},{1,65},{65,129},{129,193},{193,1... | collective-permute-start | bytes 786440 | tf_op jit(solution)/shard_map/ppermute | solution.py:322
  10.8 2.5 %collective-permute-start.1 = (bf16[256,512]{1,0:T(8,128)(2,1)S(1)}, bf16[256,512]{1,0:T(8,128)(2,1)S(1)}, u32[]{:S(2)}, u32[]{:S(2)}) collective-permute-start(bf16[256,512]{1,0:T(8,128)(2,1)S(1)} %get-tuple-element.102), channel_id=1, source_target_pairs={{0,128},{64,192},{128,0},{192,64},{1,129},{65,193},{129,1},{193,65... | collective-permute-start | bytes 786440 | tf_op jit(solution)/shard_map/ppermute | solution.py:322
  13.2 1.2 collective-permute-start.2
  14.4 1.4 collective-permute-done
  15.8 8.7 %collective-permute-done.1 = bf16[256,512]{1,0:T(8,128)(2,1)S(1)} collective-permute-done((bf16[256,512]{1,0:T(8,128)(2,1)S(1)}, bf16[256,512]{1,0:T(8,128)(2,1)S(1)}, u32[]{:S(2)}, u32[]{:S(2)}) %collective-permute-start.1) | collective-permute-done | bytes 262176 | tf_op jit(solution)/shard_map/ppermute | solution.py:322
  24.6 1.7 %collective-permute-start.3 = (bf16[1024,256]{1,0:T(8,128)(2,1)S(1)}, bf16[1024,256]{1,0:T(8,128)(2,1)}, u32[]{:S(2)}, u32[]{:S(2)}) collective-permute-start(bf16[1024,256]{1,0:T(8,128)(2,1)S(1)} %pad_maximum_fusion.refs_0_), channel_id=1, source_target_pairs={{0,8},{8,16},{16,24},{24,32},{32,40},{40,48},{48,56},{56,0},{1,9},... | collective-permute-start | bytes 1572872 | tf_op jit(solution)/shard_map/ppermute | solution.py:318
  26.4 4.0 %collective-permute-start.4 = (bf16[1024,256]{1,0:T(8,128)(2,1)S(1)}, bf16[1024,256]{1,0:T(8,128)(2,1)}, u32[]{:S(2)}, u32[]{:S(2)}) collective-permute-start(bf16[1024,256]{1,0:T(8,128)(2,1)S(1)} %pad_maximum_fusion.refs_0_), channel_id=1, source_target_pairs={{0,56},{8,0},{16,8},{24,16},{32,24},{40,32},{48,40},{56,48},{1,57}... | collective-permute-start | bytes 1572872 | tf_op jit(solution)/shard_map/ppermute | solution.py:318
  30.4 0.7 stack.92.zs
  31.1 0.6 pad_add_fusion.place
  31.8 2.7 %collective-permute-start.8 = (bf16[1024,256]{1,0:T(8,128)(2,1)S(1)}, bf16[1024,256]{1,0:T(8,128)(2,1)}, u32[]{:S(2)}, u32[]{:S(2)}) collective-permute-start(bf16[1024,256]{1,0:T(8,128)(2,1)S(1)} %pad_maximum_fusion.1.refs_1_), channel_id=1, source_target_pairs={{0,56},{8,0},{16,8},{24,16},{32,24},{40,32},{48,40},{56,48},{1,57}... | collective-permute-start | bytes 1572872 | tf_op jit(solution)/shard_map/ppermute | solution.py:318
  34.5 6.6 %collective-permute-done.3.refs_2_ = bf16[1024,256]{1,0:T(8,128)(2,1)} collective-permute-done((bf16[1024,256]{1,0:T(8,128)(2,1)S(1)}, bf16[1024,256]{1,0:T(8,128)(2,1)}, u32[]{:S(2)}, u32[]{:S(2)}) %collective-permute-start.3) | collective-permute-done | bytes 524320 | tf_op jit(solution)/shard_map/ppermute | solution.py:318
  42.5 0.2 fusion.24
  43.7 1.0 convolution_bitcast_fusion.4
  46.9 0.2 concatenate.56
  47.5 0.2 concatenate.57
  48.3 2.7 %collective-permute-start.6 = (bf16[1024,256]{1,0:T(8,128)(2,1)}, bf16[1024,256]{1,0:T(8,128)(2,1)S(1)}, u32[]{:S(2)}, u32[]{:S(2)}) collective-permute-start(bf16[1024,256]{1,0:T(8,128)(2,1)} %collective-permute-done.4.refs_4_), channel_id=1, source_target_pairs={{0,56},{8,0},{16,8},{24,16},{32,24},{40,32},{48,40},{56,48},{1,57}... | collective-permute-start | bytes 1572872 | tf_op jit(solution)/shard_map/ppermute | solution.py:318
  51.0 1.3 collective-permute-done.7.refs_3_
  52.3 2.7 %collective-permute-start.12 = (bf16[1024,256]{1,0:T(8,128)(2,1)}, bf16[1024,256]{1,0:T(8,128)(2,1)}, u32[]{:S(2)}, u32[]{:S(2)}) collective-permute-start(bf16[1024,256]{1,0:T(8,128)(2,1)} %collective-permute-done.8.refs_5_), channel_id=1, source_target_pairs={{0,56},{8,0},{16,8},{24,16},{32,24},{40,32},{48,40},{56,48},{1,57}... | collective-permute-start | bytes 1572872 | tf_op jit(solution)/shard_map/ppermute | solution.py:318
  55.7 0.9 multiply_reduce_fusion.power_ref
  57.1 3.4 %fusion.42 = f32[4,1,256,4]{1,2,3,0:T(8,128)S(1)} fusion(f32[256,4,4,4]{0,2,3,1:T(4,128)S(1)} %concatenate.57, f32[4,4,1,1]{1,2,3,0:T(1,128)S(1)} %bitcast.198), kind=kOutput, calls=%fused_computation.101 | convolution fusion | flops 196608 | bytes 81984 | tf_op jit(solution)/shard_map/ka,jkab->kbj/dot_general | solution.py:56
  60.6 0.6 copy.182
  61.3 1.0 collective-permute-done.5.refs_6_
  62.3 2.5 %collective-permute-start.10 = (bf16[1024,256]{1,0:T(8,128)(2,1)S(1)}, bf16[1024,256]{1,0:T(8,128)(2,1)}, u32[]{:S(2)}, u32[]{:S(2)}) collective-permute-start(bf16[1024,256]{1,0:T(8,128)(2,1)S(1)} %collective-permute-done.6.refs_8_), channel_id=1, source_target_pairs={{0,56},{8,0},{16,8},{24,16},{32,24},{40,32},{48,40},{56,48},{1,57}... | collective-permute-start | bytes 1572872 | tf_op jit(solution)/shard_map/ppermute | solution.py:318
  64.8 8.7 %collective-permute-done.11.refs_7_ = bf16[1024,256]{1,0:T(8,128)(2,1)} collective-permute-done((bf16[1024,256]{1,0:T(8,128)(2,1)}, bf16[1024,256]{1,0:T(8,128)(2,1)}, u32[]{:S(2)}, u32[]{:S(2)}) %collective-permute-start.11) | collective-permute-done | bytes 524320 | tf_op jit(solution)/shard_map/ppermute | solution.py:318
  73.6 2.5 %collective-permute-start.14 = (bf16[1024,256]{1,0:T(8,128)(2,1)}, bf16[1024,256]{1,0:T(8,128)(2,1)}, u32[]{:S(2)}, u32[]{:S(2)}) collective-permute-start(bf16[1024,256]{1,0:T(8,128)(2,1)} %collective-permute-done.12.refs_9_), channel_id=1, source_target_pairs={{0,56},{8,0},{16,8},{24,16},{32,24},{40,32},{48,40},{56,48},{1,57}... | collective-permute-start | bytes 1572872 | tf_op jit(solution)/shard_map/ppermute | solution.py:318
  76.1 0.6 pad_maximum_fusion.3.gain_ref
  76.9 0.8 copy.191
  77.7 0.4 slice.132
  78.0 1.8 %reshape.340 = bf16[4,256,511]{2,1,0:T(8,128)(2,1)S(1)} reshape(bf16[4,130816]{1,0:T(4,128)(2,1)S(1)} %slice.132) | data formatting | bytes 2093056 | tf_op jit(solution)/shard_map/reshape | solution.py:63
  79.8 0.8 slice.133
  80.9 0.6 pad_bitcast_fusion.final_ref
  81.5 0.8 multiply_reduce_fusion.1
  82.3 0.7 fusion.mask_ref
  83.0 0.8 collective-permute-done.10.refs_12_
  83.8 1.0 collective-permute-done.9.refs_10_
  84.8 10.3 %collective-permute-done.14.refs_13_ = bf16[1024,256]{1,0:T(8,128)(2,1)} collective-permute-done((bf16[1024,256]{1,0:T(8,128)(2,1)}, bf16[1024,256]{1,0:T(8,128)(2,1)}, u32[]{:S(2)}, u32[]{:S(2)}) %collective-permute-start.14) | collective-permute-done | bytes 524320 | tf_op jit(solution)/shard_map/ppermute | solution.py:318
  95.1 3.4 %collective-permute-start.15 = (bf16[1024,256]{1,0:T(8,128)(2,1)}, bf16[1024,256]{1,0:T(8,128)(2,1)S(1)}, u32[]{:S(2)}, u32[]{:S(2)}) collective-permute-start(bf16[1024,256]{1,0:T(8,128)(2,1)} %collective-permute-done.14.refs_13_), channel_id=1, source_target_pairs={{0,56},{8,0},{16,8},{24,16},{32,24},{40,32},{48,40},{56,48},{1,57}... | collective-permute-start | bytes 1572872 | tf_op jit(solution)/shard_map/ppermute | solution.py:318
  98.6 0.8 copy-done.5
  99.4 9.8 %shard_map.64.total_ref = f32[1024,512]{1,0:T(8,128)} custom-call(s32[9]{0:T(128)} %stack.92.zs, bf16[4,256,8192]{2,1,0:T(8,128)(2,1)} %bitcast.181, bf16[1024,256]{1,0:T(8,128)(2,1)} %copy-done, bf16[1024,256]{1,0:T(8,128)(2,1)} %copy-done.1, bf16[1024,256]{1,0:T(8,128)(2,1)} %collective-permute-done.3.refs_2_, ...), custom_call_target="tpu_custom_call" | custom-call | flops 4697620480 | bytes 19922944 | tf_op jit(solution)/shard_map/pallas_call | solution.py:160
  109.2 0.8 copy-done.6
  110.0 0.8 copy-done.7
  110.8 5.9 %shard_map.65 = (bf16[256,512]{1,0:T(8,128)(2,1)}, bf16[256,512]{1,0:T(8,128)(2,1)}, bf16[256,512]{1,0:T(8,128)(2,1)}, bf16[256,512]{1,0:T(8,128)(2,1)}, f32[32,4,256]{2,1,0:T(4,128)}) custom-call(s32[9]{0:T(128)} %stack.92.zs, bf16[4,256,8192]{2,1,0:T(8,128)(2,1)} %bitcast.182, bf16[1024,256]{1,0:T(8,128)(2,1)} %copy-done.7, bf16[1024,256]{1,0:T(8,128)(2,1)} %copy-done.6, ...), custom_call_target="tpu_custom_call" | custom-call | flops 738197504 | bytes 6291456 | tf_op jit(solution)/shard_map/pallas_call | solution.py:224
  116.7 1.7 %collective-permute-start.17 = (bf16[256,512]{1,0:T(8,128)(2,1)}, bf16[256,512]{1,0:T(8,128)(2,1)S(1)}, u32[]{:S(2)}, u32[]{:S(2)}) collective-permute-start(bf16[256,512]{1,0:T(8,128)(2,1)} %get-tuple-element.77), channel_id=1, source_target_pairs={{0,64},{64,128},{128,192},{192,0},{1,65},{65,129},{129,193},{193,1... | collective-permute-start | bytes 786440 | tf_op jit(solution)/shard_map/ppermute | solution.py:322
  118.4 4.0 %collective-permute-start.18 = (bf16[256,512]{1,0:T(8,128)(2,1)}, bf16[256,512]{1,0:T(8,128)(2,1)S(1)}, u32[]{:S(2)}, u32[]{:S(2)}) collective-permute-start(bf16[256,512]{1,0:T(8,128)(2,1)} %get-tuple-element.78), channel_id=1, source_target_pairs={{0,128},{64,192},{128,0},{192,64},{1,129},{65,193},{129,1},{193,65... | collective-permute-start | bytes 786440 | tf_op jit(solution)/shard_map/ppermute | solution.py:322
  122.4 18.1 %all_to_all.5.slabs_ref = f32[32,4,256]{2,1,0:T(4,128)} all-to-all(f32[32,4,256]{2,1,0:T(4,128)} %get-tuple-element.80), channel_id=1, replica_groups=mesh['x'=4,'z'=8,'y'=4,'c'=2] {'y','c','x'}, dimensions={0} | all-to-all | bytes 262144 | tf_op jit(solution)/shard_map/all_to_all | solution.py:381
  140.6 0.7 copy-done.14
  141.5 6.3 %shard_map.66 = f32[256,2048]{1,0:T(8,128)} custom-call(s32[2]{0:T(128)} %pad_add_fusion.place, bf16[256,512]{1,0:T(8,128)(2,1)} %get-tuple-element.76.own_ref, bf16[256,512]{1,0:T(8,128)(2,1)} %copy-done.14, bf16[256,512]{1,0:T(8,128)(2,1)} %copy-done.15, bf16[256,512]{1,0:T(8,128)(2,1)} %copy-done.16, f32[32,4,256]{2,1,0:T(4,128)} %all_to_all.5.slabs_ref, ...), custom_call_target="tpu_custom_call" | custom-call | flops 1153433600 | bytes 4194304 | tf_op jit(solution)/shard_map/pallas_call | solution.py:296
  (125 shorter events, 7.7 us)
Async XLA Ops:
  6.5 2.0 %copy-start.2 = (bf16[256,2048]{1,0:T(8,128)(2,1)S(1)}, bf16[256,2048]{1,0:T(8,128)(2,1)}, u32[]{:S(2)}) copy-start(bf16[256,2048]{1,0:T(8,128)(2,1)} %param.7) | copy-start | bytes 3145732
  6.5 92.0 %all-gather.2.cloned.1.call-start = ((), (), s32[]{:S(2)}) async-start(), calls=%async_computation.1 | async-start | bytes 17301504 | tf_op jit(solution)/shard_map/all_gather | solution.py:335
  8.6 7.1 %collective-permute-start = (bf16[256,512]{1,0:T(8,128)(2,1)S(1)}, bf16[256,512]{1,0:T(8,128)(2,1)S(1)}, u32[]{:S(2)}, u32[]{:S(2)}) collective-permute-start(bf16[256,512]{1,0:T(8,128)(2,1)S(1)} %get-tuple-element.100), channel_id=1, source_target_pairs={{0,64},{64,128},{128,192},{192,0},{1,65},{65,129},{129,193},{193,1... | collective-permute-start | bytes 786440 | tf_op jit(solution)/shard_map/ppermute | solution.py:322
  10.8 13.8 %collective-permute-start.1 = (bf16[256,512]{1,0:T(8,128)(2,1)S(1)}, bf16[256,512]{1,0:T(8,128)(2,1)S(1)}, u32[]{:S(2)}, u32[]{:S(2)}) collective-permute-start(bf16[256,512]{1,0:T(8,128)(2,1)S(1)} %get-tuple-element.102), channel_id=1, source_target_pairs={{0,128},{64,192},{128,0},{192,64},{1,129},{65,193},{129,1},{193,65... | collective-permute-start | bytes 786440 | tf_op jit(solution)/shard_map/ppermute | solution.py:322
  13.2 11.3 %collective-permute-start.2 = (bf16[256,512]{1,0:T(8,128)(2,1)S(1)}, bf16[256,512]{1,0:T(8,128)(2,1)S(1)}, u32[]{:S(2)}, u32[]{:S(2)}) collective-permute-start(bf16[256,512]{1,0:T(8,128)(2,1)S(1)} %get-tuple-element.101), channel_id=1, source_target_pairs={{0,192},{64,0},{128,64},{192,128},{1,193},{65,1},{129,65},{193,129... | collective-permute-start | bytes 786440 | tf_op jit(solution)/shard_map/ppermute | solution.py:322
  14.4 26.7 %copy-start.13 = (f32[2,4]{1,0:T(2,128)S(1)}, f32[2,4]{1,0:T(2,128)}, u32[]{:S(2)}) copy-start(f32[2,4]{1,0:T(2,128)} %param.9) | copy-start | bytes 100
  14.4 26.8 %copy-start.12 = (f32[2,4]{1,0:T(2,128)S(1)}, f32[2,4]{1,0:T(2,128)}, u32[]{:S(2)}) copy-start(f32[2,4]{1,0:T(2,128)} %param.10) | copy-start | bytes 100
  14.4 26.9 %copy-start.11 = (f32[4,4]{1,0:T(4,128)S(1)}, f32[4,4]{1,0:T(4,128)}, u32[]{:S(2)}) copy-start(f32[4,4]{1,0:T(4,128)} %param.11) | copy-start | bytes 196
  24.6 23.6 %copy-start = (bf16[1024,256]{1,0:T(8,128)(2,1)}, bf16[1024,256]{1,0:T(8,128)(2,1)S(1)}, u32[]{:S(2)}) copy-start(bf16[1024,256]{1,0:T(8,128)(2,1)S(1)} %pad_maximum_fusion.refs_0_) | copy-start | bytes 1572868
  24.6 16.4 %collective-permute-start.3 = (bf16[1024,256]{1,0:T(8,128)(2,1)S(1)}, bf16[1024,256]{1,0:T(8,128)(2,1)}, u32[]{:S(2)}, u32[]{:S(2)}) collective-permute-start(bf16[1024,256]{1,0:T(8,128)(2,1)S(1)} %pad_maximum_fusion.refs_0_), channel_id=1, source_target_pairs={{0,8},{8,16},{16,24},{24,32},{32,40},{40,48},{48,56},{56,0},{1,9},... | collective-permute-start | bytes 1572872 | tf_op jit(solution)/shard_map/ppermute | solution.py:318
  26.4 14.7 %collective-permute-start.4 = (bf16[1024,256]{1,0:T(8,128)(2,1)S(1)}, bf16[1024,256]{1,0:T(8,128)(2,1)}, u32[]{:S(2)}, u32[]{:S(2)}) collective-permute-start(bf16[1024,256]{1,0:T(8,128)(2,1)S(1)} %pad_maximum_fusion.refs_0_), channel_id=1, source_target_pairs={{0,56},{8,0},{16,8},{24,16},{32,24},{40,32},{48,40},{56,48},{1,57}... | collective-permute-start | bytes 1572872 | tf_op jit(solution)/shard_map/ppermute | solution.py:318
  30.4 25.3 %copy-start.9 = (s32[8192]{0:T(1024)S(1)}, s32[8192]{0:T(1024)}, u32[]{:S(2)}) copy-start(s32[8192]{0:T(1024)} %param.8) | copy-start | bytes 98308
  31.7 28.8 %copy-start.1 = (bf16[1024,256]{1,0:T(8,128)(2,1)}, bf16[1024,256]{1,0:T(8,128)(2,1)S(1)}, u32[]{:S(2)}) copy-start(bf16[1024,256]{1,0:T(8,128)(2,1)S(1)} %pad_maximum_fusion.1.refs_1_) | copy-start | bytes 1572868
  31.7 20.6 %collective-permute-start.7 = (bf16[1024,256]{1,0:T(8,128)(2,1)S(1)}, bf16[1024,256]{1,0:T(8,128)(2,1)}, u32[]{:S(2)}, u32[]{:S(2)}) collective-permute-start(bf16[1024,256]{1,0:T(8,128)(2,1)S(1)} %pad_maximum_fusion.1.refs_1_), channel_id=1, source_target_pairs={{0,8},{8,16},{16,24},{24,32},{32,40},{40,48},{48,56},{56,0},{1,9},... | collective-permute-start | bytes 1572872 | tf_op jit(solution)/shard_map/ppermute | solution.py:318
  31.8 20.5 %collective-permute-start.8 = (bf16[1024,256]{1,0:T(8,128)(2,1)S(1)}, bf16[1024,256]{1,0:T(8,128)(2,1)}, u32[]{:S(2)}, u32[]{:S(2)}) collective-permute-start(bf16[1024,256]{1,0:T(8,128)(2,1)S(1)} %pad_maximum_fusion.1.refs_1_), channel_id=1, source_target_pairs={{0,56},{8,0},{16,8},{24,16},{32,24},{40,32},{48,40},{56,48},{1,57}... | collective-permute-start | bytes 1572872 | tf_op jit(solution)/shard_map/ppermute | solution.py:318
  48.2 14.1 %collective-permute-start.5 = (bf16[1024,256]{1,0:T(8,128)(2,1)}, bf16[1024,256]{1,0:T(8,128)(2,1)}, u32[]{:S(2)}, u32[]{:S(2)}) collective-permute-start(bf16[1024,256]{1,0:T(8,128)(2,1)} %collective-permute-done.3.refs_2_), channel_id=1, source_target_pairs={{0,8},{8,16},{16,24},{24,32},{32,40},{40,48},{48,56},{56,0},{1,9},... | collective-permute-start | bytes 1572872 | tf_op jit(solution)/shard_map/ppermute | solution.py:318
  48.3 14.0 %collective-permute-start.6 = (bf16[1024,256]{1,0:T(8,128)(2,1)}, bf16[1024,256]{1,0:T(8,128)(2,1)S(1)}, u32[]{:S(2)}, u32[]{:S(2)}) collective-permute-start(bf16[1024,256]{1,0:T(8,128)(2,1)} %collective-permute-done.4.refs_4_), channel_id=1, source_target_pairs={{0,56},{8,0},{16,8},{24,16},{32,24},{40,32},{48,40},{56,48},{1,57}... | collective-permute-start | bytes 1572872 | tf_op jit(solution)/shard_map/ppermute | solution.py:318
  52.3 21.2 %collective-permute-start.11 = (bf16[1024,256]{1,0:T(8,128)(2,1)}, bf16[1024,256]{1,0:T(8,128)(2,1)}, u32[]{:S(2)}, u32[]{:S(2)}) collective-permute-start(bf16[1024,256]{1,0:T(8,128)(2,1)} %collective-permute-done.7.refs_3_), channel_id=1, source_target_pairs={{0,8},{8,16},{16,24},{24,32},{32,40},{40,48},{48,56},{56,0},{1,9},... | collective-permute-start | bytes 1572872 | tf_op jit(solution)/shard_map/ppermute | solution.py:318
  52.3 21.2 %collective-permute-start.12 = (bf16[1024,256]{1,0:T(8,128)(2,1)}, bf16[1024,256]{1,0:T(8,128)(2,1)}, u32[]{:S(2)}, u32[]{:S(2)}) collective-permute-start(bf16[1024,256]{1,0:T(8,128)(2,1)} %collective-permute-done.8.refs_5_), channel_id=1, source_target_pairs={{0,56},{8,0},{16,8},{24,16},{32,24},{40,32},{48,40},{56,48},{1,57}... | collective-permute-start | bytes 1572872 | tf_op jit(solution)/shard_map/ppermute | solution.py:318
  55.7 5.5 %copy-start.8 = (f32[4,1024]{1,0:T(4,128)}, f32[4,1024]{1,0:T(4,128)S(1)}, u32[]{:S(2)}) copy-start(f32[4,1024]{1,0:T(4,128)S(1)} %fusion.13.onehot_ref) | copy-start | bytes 49156
  56.6 24.9 %copy-start.10 = (f32[4,256]{1,0:T(4,128)}, f32[4,256]{1,0:T(4,128)S(1)}, u32[]{:S(2)}) copy-start(f32[4,256]{1,0:T(4,128)S(1)} %fusion.21.onehot_ref) | copy-start | bytes 12292
  62.3 15.7 %copy-start.3 = (bf16[1024,256]{1,0:T(8,128)(2,1)}, bf16[1024,256]{1,0:T(8,128)(2,1)S(1)}, u32[]{:S(2)}) copy-start(bf16[1024,256]{1,0:T(8,128)(2,1)S(1)} %collective-permute-done.6.refs_8_) | copy-start | bytes 1572868
  62.3 21.4 %collective-permute-start.10 = (bf16[1024,256]{1,0:T(8,128)(2,1)S(1)}, bf16[1024,256]{1,0:T(8,128)(2,1)}, u32[]{:S(2)}, u32[]{:S(2)}) collective-permute-start(bf16[1024,256]{1,0:T(8,128)(2,1)S(1)} %collective-permute-done.6.refs_8_), channel_id=1, source_target_pairs={{0,56},{8,0},{16,8},{24,16},{32,24},{40,32},{48,40},{56,48},{1,57}... | collective-permute-start | bytes 1572872 | tf_op jit(solution)/shard_map/ppermute | solution.py:318
  64.8 20.0 %collective-permute-start.9 = (bf16[1024,256]{1,0:T(8,128)(2,1)}, bf16[1024,256]{1,0:T(8,128)(2,1)S(1)}, u32[]{:S(2)}, u32[]{:S(2)}) collective-permute-start(bf16[1024,256]{1,0:T(8,128)(2,1)} %collective-permute-done.5.refs_6_), channel_id=1, source_target_pairs={{0,8},{8,16},{16,24},{24,32},{32,40},{40,48},{48,56},{56,0},{1,9},... | collective-permute-start | bytes 1572872 | tf_op jit(solution)/shard_map/ppermute | solution.py:318
  73.6 21.5 %collective-permute-start.14 = (bf16[1024,256]{1,0:T(8,128)(2,1)}, bf16[1024,256]{1,0:T(8,128)(2,1)}, u32[]{:S(2)}, u32[]{:S(2)}) collective-permute-start(bf16[1024,256]{1,0:T(8,128)(2,1)} %collective-permute-done.12.refs_9_), channel_id=1, source_target_pairs={{0,56},{8,0},{16,8},{24,16},{32,24},{40,32},{48,40},{56,48},{1,57}... | collective-permute-start | bytes 1572872 | tf_op jit(solution)/shard_map/ppermute | solution.py:318
  80.9 17.7 %collective-permute-start.16 = (bf16[1024,256]{1,0:T(8,128)(2,1)}, bf16[1024,256]{1,0:T(8,128)(2,1)S(1)}, u32[]{:S(2)}, u32[]{:S(2)}) collective-permute-start(bf16[1024,256]{1,0:T(8,128)(2,1)} %collective-permute-done.11.refs_7_), channel_id=1, source_target_pairs={{0,8},{8,16},{16,24},{24,32},{32,40},{40,48},{48,56},{56,0},{1,9},... | collective-permute-start | bytes 1572872 | tf_op jit(solution)/shard_map/ppermute | solution.py:318
  84.8 13.8 %copy-start.4 = (bf16[1024,256]{1,0:T(8,128)(2,1)}, bf16[1024,256]{1,0:T(8,128)(2,1)S(1)}, u32[]{:S(2)}) copy-start(bf16[1024,256]{1,0:T(8,128)(2,1)S(1)} %collective-permute-done.9.refs_10_) | copy-start | bytes 1572868
  95.1 14.1 %collective-permute-start.15 = (bf16[1024,256]{1,0:T(8,128)(2,1)}, bf16[1024,256]{1,0:T(8,128)(2,1)S(1)}, u32[]{:S(2)}, u32[]{:S(2)}) collective-permute-start(bf16[1024,256]{1,0:T(8,128)(2,1)} %collective-permute-done.14.refs_13_), channel_id=1, source_target_pairs={{0,56},{8,0},{16,8},{24,16},{32,24},{40,32},{48,40},{56,48},{1,57}... | collective-permute-start | bytes 1572872 | tf_op jit(solution)/shard_map/ppermute | solution.py:318
  98.5 10.7 %collective-permute-start.13 = (bf16[1024,256]{1,0:T(8,128)(2,1)S(1)}, bf16[1024,256]{1,0:T(8,128)(2,1)S(1)}, u32[]{:S(2)}, u32[]{:S(2)}) collective-permute-start(bf16[1024,256]{1,0:T(8,128)(2,1)S(1)} %collective-permute-done.9.refs_10_), channel_id=1, source_target_pairs={{0,8},{8,16},{16,24},{24,32},{32,40},{40,48},{48,56},{56,0},{1,9},... | collective-permute-start | bytes 1572872 | tf_op jit(solution)/shard_map/ppermute | solution.py:318
  98.5 0.9 copy-start.5
  109.2 0.8 copy-start.6
  110.0 0.8 copy-start.7
  116.7 23.9 %collective-permute-start.17 = (bf16[256,512]{1,0:T(8,128)(2,1)}, bf16[256,512]{1,0:T(8,128)(2,1)S(1)}, u32[]{:S(2)}, u32[]{:S(2)}) collective-permute-start(bf16[256,512]{1,0:T(8,128)(2,1)} %get-tuple-element.77), channel_id=1, source_target_pairs={{0,64},{64,128},{128,192},{192,0},{1,65},{65,129},{129,193},{193,1... | collective-permute-start | bytes 786440 | tf_op jit(solution)/shard_map/ppermute | solution.py:322
  118.4 22.2 %collective-permute-start.18 = (bf16[256,512]{1,0:T(8,128)(2,1)}, bf16[256,512]{1,0:T(8,128)(2,1)S(1)}, u32[]{:S(2)}, u32[]{:S(2)}) collective-permute-start(bf16[256,512]{1,0:T(8,128)(2,1)} %get-tuple-element.78), channel_id=1, source_target_pairs={{0,128},{64,192},{128,0},{192,64},{1,129},{65,193},{129,1},{193,65... | collective-permute-start | bytes 786440 | tf_op jit(solution)/shard_map/ppermute | solution.py:322
  122.4 18.2 %collective-permute-start.19 = (bf16[256,512]{1,0:T(8,128)(2,1)}, bf16[256,512]{1,0:T(8,128)(2,1)S(1)}, u32[]{:S(2)}, u32[]{:S(2)}) collective-permute-start(bf16[256,512]{1,0:T(8,128)(2,1)} %get-tuple-element.79), channel_id=1, source_target_pairs={{0,192},{64,0},{128,64},{192,128},{1,193},{65,1},{129,65},{193,129... | collective-permute-start | bytes 786440 | tf_op jit(solution)/shard_map/ppermute | solution.py:322
  140.6 0.7 copy-start.14
  140.6 0.8 copy-start.15
  140.6 0.9 copy-start.16
Sparse Core Ops, SparseCore 0:
  9.9 81.7 all-gather.1

commit v4 on v3

--- a/solution.py
+++ b/solution.py
@@ -98,11 +98,9 @@
                     g_ref.at[pl.ds(q, NX - q), :, columns], held[q].at[b], sems.at[b, q]
                 )
             )
-        for half in range(2):
+        for half, ref in enumerate(noise[2 * b : 2 * b + 2]):
             copies.append(
-                pltpu.make_async_copy(
-                    noise[2 * b + half], block.at[b, half], sems.at[b, NX + half]
-                )
+                pltpu.make_async_copy(ref, block.at[b, half], sems.at[b, NX + half])
             )
         every.append(copies)
     return every
@@ -122,23 +120,32 @@
     return jnp.dot(rows, noise, preferred_element_type=F32)
 
 
-def product_kernel(zs, g_ref, *refs):
-    count = 2 * len(AWAY)
-    noise_refs, (out_ref, *held, block, sems) = refs[:count], refs[count:]
-    copies = load(zs, range(1, 8), g_ref, noise_refs, held, block, sems)
-    for b in range(AHEAD):
+def product_kernel(blocks, has_acc, zs, g_ref, *refs):
+    count = 2 * blocks
+    noise_refs, refs = refs[:count], refs[count:]
+    acc_ref, refs = (refs[0], refs[1:]) if has_acc else (None, refs)
+    out_ref, *held, block, sems = refs
+    if has_acc:
+        fetch = pltpu.make_async_copy(acc_ref, out_ref, sems.at[0, 2 * NX])
+        fetch.start()
+    copies = load(zs, range(1, 1 + blocks), g_ref, noise_refs, held, block, sems)
+    ahead = min(AHEAD, blocks)
+    for b in range(ahead):
         for copy in copies[b]:
             copy.start()
-    for b in range(len(AWAY)):
+    if has_acc:
+        fetch.wait()
+    for b in range(blocks):
         for copy in copies[b]:
             copy.wait()
-        if b + AHEAD < len(AWAY):
-            for copy in copies[b + AHEAD]:
+        if b + ahead < blocks:
+            for copy in copies[b + ahead]:
                 copy.start()
         for s in range(NX):
             rows = pl.ds(s * ROWS, ROWS)
             value = term(zs, held, block, b, s)
-            out_ref[rows, :] = value if b == 0 else out_ref[rows, :] + value
+            first = b == 0 and not has_acc
+            out_ref[rows, :] = value if first else out_ref[rows, :] + value
 
 
 def scratch(blocks):
@@ -155,31 +162,42 @@
 ANYWHERE = pl.BlockSpec(memory_space=pl.ANY)
 
 
-def product(scalars, gathered, noise_blocks):
+def product(where_z, gathered, noise_blocks, acc=None):
+    blocks = len(noise_blocks) // 2
     out = jax.ShapeDtypeStruct((NX * ROWS, SLAB), F32)
+    args = [*noise_blocks] + ([] if acc is None else [acc])
     return pl.pallas_call(
-        product_kernel,
+        functools.partial(product_kernel, blocks, acc is not None),
         grid_spec=pltpu.PrefetchScalarGridSpec(
             num_scalar_prefetch=1,
             grid=(1,),
-            in_specs=[ANYWHERE] * (1 + len(noise_blocks)),
+            in_specs=[ANYWHERE] * (1 + len(args)),
             out_specs=whole(out),
-            scratch_shapes=scratch(len(AWAY)),
+            scratch_shapes=scratch(blocks),
         ),
         out_shape=out,
         compiler_params=pltpu.CompilerParams(vmem_limit_bytes=VMEM_LIMIT),
         cost_estimate=pl.CostEstimate(
-            flops=7 * 2 * 10 * ROWS * CH * SLAB, bytes_accessed=19 * 1048576, transcendentals=0
-        ),
-    )(scalars, gathered, *noise_blocks)
+            flops=blocks * 2 * 10 * ROWS * CH * SLAB,
+            bytes_accessed=(3 * blocks + 2) * 1048576,
+            transcendentals=0,
+        ),
+    )(where_z, gathered, *args)
 
 
 def last_kernel(
-    zs, g_ref, first_ref, second_ref, total_ref, final_ref, onehot_ref,
+    zs, g_ref, first_ref, up_ref, down_ref, total_ref, final_ref, onehot_ref,
     power_ref, *refs,
 ):
     piece_refs, (send_ref, local, acc_ref, *held, block, sems) = refs[:NX], refs[NX:]
-    (waits,) = load(zs, (8,), g_ref, (first_ref, second_ref), held, block, sems)
+    (waits,) = load(zs, (1,), g_ref, (first_ref,), held, block, sems)
+    half = NX * ROWS // 2
+    waits.append(
+        pltpu.make_async_copy(up_ref, block.at[0, 1, pl.ds(0, half)], sems.at[0, NX + 1])
+    )
+    waits.append(
+        pltpu.make_async_copy(down_ref, block.at[0, 1, pl.ds(half, half)], sems.at[0, NX + 2])
+    )
     for copy in waits[NX:] + waits[:NX]:
         copy.start()
     fetch = []
@@ -226,7 +244,7 @@
         grid_spec=pltpu.PrefetchScalarGridSpec(
             num_scalar_prefetch=1,
             grid=(1,),
-            in_specs=[ANYWHERE] * 4 + [whole(a) for a in args],
+            in_specs=[ANYWHERE] * 5 + [whole(a) for a in args],
             out_specs=[whole(a) for a in out_shape],
             scratch_shapes=[
                 pltpu.VMEM((NX, ROWS, SLAB), BF16),
@@ -362,7 +380,10 @@
     own_class = lax.dynamic_slice(by_block, (x, z, 0), (1, 1, ROWS)).reshape(1, ROWS)
     own_hot = (own_class == ids[:, None]).astype(F32)
     own_mask = (own_class.reshape(ROWS, 1) == ids[None, :]).astype(BF16)
-    scalars = jnp.stack([x] + [(z + by) % NZ for by in AWAY + (4,)]).astype(jnp.int32)
+    scalars = [
+        jnp.stack([x] + [(z + by) % NZ for by in away]).astype(jnp.int32)
+        for away in (AWAY[:5], AWAY[5:], (4,))
+    ]
     place = jnp.stack([tm, x]).astype(jnp.int32)
     for_last = (final, tile_hot, per_row(one, tile_hot))
     for_filter = (
@@ -372,11 +393,14 @@
     scalars, place, for_last, for_filter, first[5] = lax.optimization_barrier(
         (scalars, place, for_last, for_filter, first[5])
     )
-    second[6], _ = together(second[6], first[5])
-    opposite = [ring(first[5], 1), ring(second[6], -1)]
-
-    total = product(scalars, gathered, [n for pair in zip(*steps) for n in pair])
-    *pieces, to_send = last_product(scalars, gathered, opposite, total, *for_last)
+    pairs = [n for pair in zip(*steps) for n in pair]
+    opposite = [ring(first[5], 1)]
+    total = product(scalars[0], gathered, pairs[:10])
+    second[5], second[6], total = lax.optimization_barrier((second[5], second[6], total))
+    opposite += [ring(second[5][:512], 1), ring(second[6][512:], -1)]
+    opposite[0], total = lax.optimization_barrier((opposite[0], total))
+    total = product(scalars[1], gathered, pairs[10:], total)
+    *pieces, to_send = last_product(scalars[2], gathered, opposite, total, *for_last)
     excitation = [pieces[0]] + [round_x(pieces[d], d) for d in (1, 2, 3)]
     own_ends = lax.all_to_all(to_send, ("y", "c", "x"), 0, 0, tiled=True)
     return filtered(place, *excitation, own_ends, *for_filter)

time: 155 us -> 159 us (1.026)
  Pallas kernels: 21.9 us -> 26.3 us
    ppermute x14 -> x15, waiting for transfers between devices: 29.8 us -> 23.3 us  [ring(): return lax.ppermute(value, 'z', [(i, (i + by) % NZ) for i in range(NZ)])]
    all_gather x1, waiting for transfers between devices: 0.02 us -> 6.45 us  [body(): gathered = lax.all_gather(share, ('x', 'y', 'c'), tiled=True)]
    pallas_call x1 -> x2, Pallas kernels: 9.77 us -> 14.1 us  [product(): pl.pallas_call(functools.partial(product_kernel, blocks, acc is not None)...]
    ppermute x14 -> x15, starting transfers between devices: 22.3 us -> 22.1 us  [ring(): return lax.ppermute(value, 'z', [(i, (i + by) % NZ) for i in range(NZ)])]
  transfers between devices with their start and end apart: 21 -> 22, of which waited for: 9 -> 9; matrix products, arithmetic and copies ran while one was open for 14% -> 14% of each run, Pallas kernels for 6% -> 9%
where the time goes in v4:
time: 159 us
  waiting for transfers between devices  39.9 us (25%)
  starting transfers between devices  33.2 us (21%)
  Pallas kernels  26.3 us (17%)
  blocking collectives  18.2 us (11%)
  local copies, waits for them, and re-layouts  15.2 us (10%)
  between operations  13.9 us (9%)
  matrix products  6.42 us (4%)
  other arithmetic  5.45 us (3%)
    ppermute x15, waiting for transfers between devices, ring(): return lax.ppermute(value, 'z', [(i, (i + by) % NZ) for i in range(NZ)])  23.3 us
    ppermute x15, starting transfers between devices, ring(): return lax.ppermute(value, 'z', [(i, (i + by) % NZ) for i in range(NZ)])  22.1 us
    all_to_all x1, blocking collectives, body(): own_ends = lax.all_to_all(to_send, ('y', 'c', 'x'), 0, 0, tiled=True)  18.2 us
    pallas_call x2, Pallas kernels, product(): pl.pallas_call(functools.partial(product_kernel, blocks, acc is not None)...  14.1 us
    ppermute x6, starting transfers between devices, round_x(): return lax.ppermute(value, 'x', [(i, (i + by) % NX) for i in range(NX)])  11.1 us
    ppermute x6, waiting for transfers between devices, round_x(): return lax.ppermute(value, 'x', [(i, (i + by) % NX) for i in range(NX)])  10.1 us
    all_gather x1, waiting for transfers between devices, body(): gathered = lax.all_gather(share, ('x', 'y', 'c'), tiled=True)  6.45 us
    pallas_call x1, Pallas kernels, filtered(): pl.pallas_call(filter_kernel, grid_spec=pltpu.PrefetchScalarGridSpec(num_...  6.26 us
  transfers between devices with their start and end apart: 22, of which 9 were waited for; matrix products, arithmetic and copies ran while one was open for 14% of the time, Pallas kernels for 9%

profile of v4, /device:TPU:1, one launch (start us, length us, event | category | flops | bytes accessed | tf_op | source)
XLA Modules:
  0.0 158.6 jit_solution(10990902530225525605)
XLA Ops:
  6.5 2.0 %constant_dynamic-slice_fusion.1 = bf16[32,8192]{1,0:T(8,128)(2,1)} fusion(bf16[256,8192]{1,0:T(8,128)(2,1)} %param.6, s32[]{:T(128)S(6)} %select_n.71), kind=kLoop, calls=%fused_computation.62 | loop fusion | bytes 1048580 | tf_op jit(solution)/shard_map/dynamic_slice | solution.py:352
  8.6 2.1 %collective-permute-start = (bf16[256,512]{1,0:T(8,128)(2,1)S(1)}, bf16[256,512]{1,0:T(8,128)(2,1)S(1)}, u32[]{:S(2)}, u32[]{:S(2)}) collective-permute-start(bf16[256,512]{1,0:T(8,128)(2,1)S(1)} %get-tuple-element.112), channel_id=1, source_target_pairs={{0,64},{64,128},{128,192},{192,0},{1,65},{65,129},{129,193},{193,1... | collective-permute-start | bytes 786440 | tf_op jit(solution)/shard_map/ppermute | solution.py:340
  10.8 2.5 %collective-permute-start.1 = (bf16[256,512]{1,0:T(8,128)(2,1)S(1)}, bf16[256,512]{1,0:T(8,128)(2,1)S(1)}, u32[]{:S(2)}, u32[]{:S(2)}) collective-permute-start(bf16[256,512]{1,0:T(8,128)(2,1)S(1)} %get-tuple-element.114), channel_id=1, source_target_pairs={{0,128},{64,192},{128,0},{192,64},{1,129},{65,193},{129,1},{193,65... | collective-permute-start | bytes 786440 | tf_op jit(solution)/shard_map/ppermute | solution.py:340
  13.2 1.2 collective-permute-start.2
  14.4 1.4 collective-permute-done
  15.8 8.7 %collective-permute-done.1 = bf16[256,512]{1,0:T(8,128)(2,1)S(1)} collective-permute-done((bf16[256,512]{1,0:T(8,128)(2,1)S(1)}, bf16[256,512]{1,0:T(8,128)(2,1)S(1)}, u32[]{:S(2)}, u32[]{:S(2)}) %collective-permute-start.1) | collective-permute-done | bytes 262176 | tf_op jit(solution)/shard_map/ppermute | solution.py:340
  24.6 1.7 %collective-permute-start.3 = (bf16[1024,256]{1,0:T(8,128)(2,1)S(1)}, bf16[1024,256]{1,0:T(8,128)(2,1)}, u32[]{:S(2)}, u32[]{:S(2)}) collective-permute-start(bf16[1024,256]{1,0:T(8,128)(2,1)S(1)} %pad_maximum_fusion.refs_0_), channel_id=1, source_target_pairs={{0,8},{8,16},{16,24},{24,32},{32,40},{40,48},{48,56},{56,0},{1,9},... | collective-permute-start | bytes 1572872 | tf_op jit(solution)/shard_map/ppermute | solution.py:336
  26.4 4.0 %collective-permute-start.4 = (bf16[1024,256]{1,0:T(8,128)(2,1)S(1)}, bf16[1024,256]{1,0:T(8,128)(2,1)}, u32[]{:S(2)}, u32[]{:S(2)}) collective-permute-start(bf16[1024,256]{1,0:T(8,128)(2,1)S(1)} %pad_maximum_fusion.refs_0_), channel_id=1, source_target_pairs={{0,56},{8,0},{16,8},{24,16},{32,24},{40,32},{48,40},{56,48},{1,57}... | collective-permute-start | bytes 1572872 | tf_op jit(solution)/shard_map/ppermute | solution.py:336
  30.4 0.7 stack.97.zs
  31.1 0.6 pad_add_fusion.1.zs
  31.7 0.7 pad_add_fusion.2.place
  32.3 0.6 pad_add_fusion.zs
  33.1 2.7 %collective-permute-start.8 = (bf16[1024,256]{1,0:T(8,128)(2,1)S(1)}, bf16[1024,256]{1,0:T(8,128)(2,1)}, u32[]{:S(2)}, u32[]{:S(2)}) collective-permute-start(bf16[1024,256]{1,0:T(8,128)(2,1)S(1)} %pad_maximum_fusion.1.refs_1_), channel_id=1, source_target_pairs={{0,56},{8,0},{16,8},{24,16},{32,24},{40,32},{48,40},{56,48},{1,57}... | collective-permute-start | bytes 1572872 | tf_op jit(solution)/shard_map/ppermute | solution.py:336
  35.7 5.4 %collective-permute-done.3.refs_2_ = bf16[1024,256]{1,0:T(8,128)(2,1)} collective-permute-done((bf16[1024,256]{1,0:T(8,128)(2,1)S(1)}, bf16[1024,256]{1,0:T(8,128)(2,1)}, u32[]{:S(2)}, u32[]{:S(2)}) %collective-permute-start.3) | collective-permute-done | bytes 524320 | tf_op jit(solution)/shard_map/ppermute | solution.py:336
  43.7 1.0 convolution_bitcast_fusion.4
  47.9 2.7 %collective-permute-start.6 = (bf16[1024,256]{1,0:T(8,128)(2,1)}, bf16[1024,256]{1,0:T(8,128)(2,1)}, u32[]{:S(2)}, u32[]{:S(2)}) collective-permute-start(bf16[1024,256]{1,0:T(8,128)(2,1)} %collective-permute-done.4.refs_4_), channel_id=1, source_target_pairs={{0,56},{8,0},{16,8},{24,16},{32,24},{40,32},{48,40},{56,48},{1,57}... | collective-permute-start | bytes 1572872 | tf_op jit(solution)/shard_map/ppermute | solution.py:336
  50.6 1.8 %collective-permute-done.7.refs_3_ = bf16[1024,256]{1,0:T(8,128)(2,1)} collective-permute-done((bf16[1024,256]{1,0:T(8,128)(2,1)S(1)}, bf16[1024,256]{1,0:T(8,128)(2,1)}, u32[]{:S(2)}, u32[]{:S(2)}) %collective-permute-start.7) | collective-permute-done | bytes 524320 | tf_op jit(solution)/shard_map/ppermute | solution.py:336
  52.3 2.7 %collective-permute-start.12 = (bf16[1024,256]{1,0:T(8,128)(2,1)}, bf16[1024,256]{1,0:T(8,128)(2,1)}, u32[]{:S(2)}, u32[]{:S(2)}) collective-permute-start(bf16[1024,256]{1,0:T(8,128)(2,1)} %collective-permute-done.8.refs_5_), channel_id=1, source_target_pairs={{0,56},{8,0},{16,8},{24,16},{32,24},{40,32},{48,40},{56,48},{1,57}... | collective-permute-start | bytes 1572872 | tf_op jit(solution)/shard_map/ppermute | solution.py:336
  55.0 3.4 %fusion.42 = f32[4,1,256,4]{1,2,3,0:T(8,128)S(1)} fusion(f32[256,4,4,4]{0,2,3,1:T(4,128)S(1)} %concatenate.57, f32[4,4,1,1]{1,2,3,0:T(1,128)S(1)} %bitcast.198), kind=kOutput, calls=%fused_computation.103 | convolution fusion | flops 196608 | bytes 81984 | tf_op jit(solution)/shard_map/ka,jkab->kbj/dot_general | solution.py:56
  58.5 0.6 copy.182
  60.5 0.7 fusion.mask_ref
  61.3 0.6 pad_maximum_fusion.3.gain_ref
  62.1 0.9 multiply_reduce_fusion.power_ref
  62.9 2.3 %collective-permute-start.10 = (bf16[1024,256]{1,0:T(8,128)(2,1)}, bf16[1024,256]{1,0:T(8,128)(2,1)}, u32[]{:S(2)}, u32[]{:S(2)}) collective-permute-start(bf16[1024,256]{1,0:T(8,128)(2,1)} %collective-permute-done.6.refs_8_), channel_id=1, source_target_pairs={{0,56},{8,0},{16,8},{24,16},{32,24},{40,32},{48,40},{56,48},{1,57}... | collective-permute-start | bytes 1572872 | tf_op jit(solution)/shard_map/ppermute | solution.py:336
  65.6 8.5 %collective-permute-done.11.refs_7_ = bf16[1024,256]{1,0:T(8,128)(2,1)} collective-permute-done((bf16[1024,256]{1,0:T(8,128)(2,1)}, bf16[1024,256]{1,0:T(8,128)(2,1)}, u32[]{:S(2)}, u32[]{:S(2)}) %collective-permute-start.11) | collective-permute-done | bytes 524320 | tf_op jit(solution)/shard_map/ppermute | solution.py:336
  74.0 2.7 %collective-permute-start.15 = (bf16[1024,256]{1,0:T(8,128)(2,1)}, bf16[1024,256]{1,0:T(8,128)(2,1)S(1)}, u32[]{:S(2)}, u32[]{:S(2)}) collective-permute-start(bf16[1024,256]{1,0:T(8,128)(2,1)} %collective-permute-done.12.refs_9_), channel_id=1, source_target_pairs={{0,56},{8,0},{16,8},{24,16},{32,24},{40,32},{48,40},{56,48},{1,57}... | collective-permute-start | bytes 1572872 | tf_op jit(solution)/shard_map/ppermute | solution.py:336
  76.7 0.6 pad_bitcast_fusion.final_ref
  77.3 0.8 copy.191
  78.1 0.4 slice.140
  78.5 1.8 %reshape.340 = bf16[4,256,511]{2,1,0:T(8,128)(2,1)S(1)} reshape(bf16[4,130816]{1,0:T(4,128)(2,1)S(1)} %slice.140) | data formatting | bytes 2093056 | tf_op jit(solution)/shard_map/reshape | solution.py:63
  80.3 0.8 slice.141
  81.3 0.8 multiply_reduce_fusion.1
  82.1 2.2 %collective-permute-done.10.refs_2_ = bf16[1024,256]{1,0:T(8,128)(2,1)} collective-permute-done((bf16[1024,256]{1,0:T(8,128)(2,1)}, bf16[1024,256]{1,0:T(8,128)(2,1)}, u32[]{:S(2)}, u32[]{:S(2)}) %collective-permute-start.10) | collective-permute-done | bytes 524320 | tf_op jit(solution)/shard_map/ppermute | solution.py:336
  84.3 0.9 collective-permute-done.9.refs_0_
  85.3 6.5 %all-gather.2.cloned.1.call-done = bf16[1024,8192]{1,0:T(8,128)(2,1)} async-done(((bf16[32,8192]{1,0:T(8,128)(2,1)}), bf16[1024,8192]{1,0:T(8,128)(2,1)}) %all-gather.2.cloned.1.call-update) | async-done | bytes 16777232 | tf_op jit(solution)/shard_map/all_gather | solution.py:353
  91.7 8.1 %shard_map.64.refs_4_ = f32[1024,512]{1,0:T(8,128)} custom-call(s32[6]{0:T(128)} %stack.97.zs, bf16[4,256,8192]{2,1,0:T(8,128)(2,1)} %bitcast.181, bf16[1024,256]{1,0:T(8,128)(2,1)} %copy-done, bf16[1024,256]{1,0:T(8,128)(2,1)} %copy-done.1, bf16[1024,256]{1,0:T(8,128)(2,1)} %collective-permute-done.3.refs_2_, ...), custom_call_target="tpu_custom_call" | custom-call | flops 3355443200 | bytes 17825792 | tf_op jit(solution)/shard_map/pallas_call | solution.py:169
  99.9 1.4 collective-permute-start.16
  101.3 1.8 %collective-permute-start.17 = (bf16[512,256]{1,0:T(8,128)(2,1)S(1)}, bf16[512,256]{1,0:T(8,128)(2,1)S(1)}, u32[]{:S(2)}, u32[]{:S(2)}) collective-permute-start(bf16[512,256]{1,0:T(8,128)(2,1)S(1)} %slice.128), channel_id=1, source_target_pairs={{0,56},{8,0},{16,8},{24,16},{32,24},{40,32},{48,40},{56,48},{1,57}... | collective-permute-start | bytes 786440 | tf_op jit(solution)/shard_map/ppermute | solution.py:336
  103.1 4.5 %collective-permute-done.13.first_ref = bf16[1024,256]{1,0:T(8,128)(2,1)S(1)} collective-permute-done((bf16[1024,256]{1,0:T(8,128)(2,1)}, bf16[1024,256]{1,0:T(8,128)(2,1)S(1)}, u32[]{:S(2)}, u32[]{:S(2)}) %collective-permute-start.13) | collective-permute-done | bytes 524320 | tf_op jit(solution)/shard_map/ppermute | solution.py:336
  107.6 6.1 %shard_map.65.total_ref = f32[1024,512]{1,0:T(8,128)} custom-call(s32[3]{0:T(128)} %pad_add_fusion.zs, bf16[4,256,8192]{2,1,0:T(8,128)(2,1)} %bitcast.182, bf16[1024,256]{1,0:T(8,128)(2,1)} %collective-permute-done.9.refs_0_, bf16[1024,256]{1,0:T(8,128)(2,1)} %copy-done.2, bf16[1024,256]{1,0:T(8,128)(2,1)} %collective-permute-done.10.refs_2_, ...), custom_call_target="tpu_custom_call" | custom-call | flops 1342177280 | bytes 8388608 | tf_op jit(solution)/shard_map/pallas_call | solution.py:169
  113.7 0.7 copy-done.6
  114.4 0.7 copy-done.7
  115.1 5.9 %shard_map.66 = (bf16[256,512]{1,0:T(8,128)(2,1)}, bf16[256,512]{1,0:T(8,128)(2,1)}, bf16[256,512]{1,0:T(8,128)(2,1)}, bf16[256,512]{1,0:T(8,128)(2,1)}, f32[32,4,256]{2,1,0:T(4,128)}) custom-call(s32[2]{0:T(128)} %pad_add_fusion.1.zs, bf16[4,256,8192]{2,1,0:T(8,128)(2,1)} %bitcast.183, bf16[1024,256]{1,0:T(8,128)(2,1)} %copy-done.5, ...), custom_call_target="tpu_custom_call" | custom-call | flops 738197504 | bytes 6291456 | tf_op jit(solution)/shard_map/pallas_call | solution.py:242
  121.0 1.7 %collective-permute-start.18 = (bf16[256,512]{1,0:T(8,128)(2,1)}, bf16[256,512]{1,0:T(8,128)(2,1)S(1)}, u32[]{:S(2)}, u32[]{:S(2)}) collective-permute-start(bf16[256,512]{1,0:T(8,128)(2,1)} %get-tuple-element.89), channel_id=1, source_target_pairs={{0,64},{64,128},{128,192},{192,0},{1,65},{65,129},{129,193},{193,1... | collective-permute-start | bytes 786440 | tf_op jit(solution)/shard_map/ppermute | solution.py:340
  122.8 3.7 %collective-permute-start.19 = (bf16[256,512]{1,0:T(8,128)(2,1)}, bf16[256,512]{1,0:T(8,128)(2,1)S(1)}, u32[]{:S(2)}, u32[]{:S(2)}) collective-permute-start(bf16[256,512]{1,0:T(8,128)(2,1)} %get-tuple-element.90), channel_id=1, source_target_pairs={{0,128},{64,192},{128,0},{192,64},{1,129},{65,193},{129,1},{193,65... | collective-permute-start | bytes 786440 | tf_op jit(solution)/shard_map/ppermute | solution.py:340
  126.4 18.2 %all_to_all.5.slabs_ref = f32[32,4,256]{2,1,0:T(4,128)} all-to-all(f32[32,4,256]{2,1,0:T(4,128)} %get-tuple-element.92), channel_id=1, replica_groups=mesh['x'=4,'z'=8,'y'=4,'c'=2] {'y','c','x'}, dimensions={0} | all-to-all | bytes 262144 | tf_op jit(solution)/shard_map/all_to_all | solution.py:405
  144.7 0.7 copy-done.14
  145.5 6.3 %shard_map.67 = f32[256,2048]{1,0:T(8,128)} custom-call(s32[2]{0:T(128)} %pad_add_fusion.2.place, bf16[256,512]{1,0:T(8,128)(2,1)} %get-tuple-element.88.own_ref, bf16[256,512]{1,0:T(8,128)(2,1)} %copy-done.14, bf16[256,512]{1,0:T(8,128)(2,1)} %copy-done.15, bf16[256,512]{1,0:T(8,128)(2,1)} %copy-done.16, f32[32,4,256]{2,1,0:T(4,128)} %all_to_all.5.slabs_ref, ...), custom_call_target="tpu_custom_call" | custom-call | flops 1153433600 | bytes 4194304 | tf_op jit(solution)/shard_map/pallas_call | solution.py:314
  (132 shorter events, 8.4 us)
Async XLA Ops:
  6.5 2.0 %copy-start.4 = (bf16[256,2048]{1,0:T(8,128)(2,1)S(1)}, bf16[256,2048]{1,0:T(8,128)(2,1)}, u32[]{:S(2)}) copy-start(bf16[256,2048]{1,0:T(8,128)(2,1)} %param.7) | copy-start | bytes 3145732
  6.5 85.2 %all-gather.2.cloned.1.call-start = ((), (), s32[]{:S(2)}) async-start(), calls=%async_computation.1 | async-start | bytes 17301504 | tf_op jit(solution)/shard_map/all_gather | solution.py:353
  8.6 7.1 %collective-permute-start = (bf16[256,512]{1,0:T(8,128)(2,1)S(1)}, bf16[256,512]{1,0:T(8,128)(2,1)S(1)}, u32[]{:S(2)}, u32[]{:S(2)}) collective-permute-start(bf16[256,512]{1,0:T(8,128)(2,1)S(1)} %get-tuple-element.112), channel_id=1, source_target_pairs={{0,64},{64,128},{128,192},{192,0},{1,65},{65,129},{129,193},{193,1... | collective-permute-start | bytes 786440 | tf_op jit(solution)/shard_map/ppermute | solution.py:340
  10.8 13.8 %collective-permute-start.1 = (bf16[256,512]{1,0:T(8,128)(2,1)S(1)}, bf16[256,512]{1,0:T(8,128)(2,1)S(1)}, u32[]{:S(2)}, u32[]{:S(2)}) collective-permute-start(bf16[256,512]{1,0:T(8,128)(2,1)S(1)} %get-tuple-element.114), channel_id=1, source_target_pairs={{0,128},{64,192},{128,0},{192,64},{1,129},{65,193},{129,1},{193,65... | collective-permute-start | bytes 786440 | tf_op jit(solution)/shard_map/ppermute | solution.py:340
  13.2 11.3 %collective-permute-start.2 = (bf16[256,512]{1,0:T(8,128)(2,1)S(1)}, bf16[256,512]{1,0:T(8,128)(2,1)S(1)}, u32[]{:S(2)}, u32[]{:S(2)}) collective-permute-start(bf16[256,512]{1,0:T(8,128)(2,1)S(1)} %get-tuple-element.113), channel_id=1, source_target_pairs={{0,192},{64,0},{128,64},{192,128},{1,193},{65,1},{129,65},{193,129... | collective-permute-start | bytes 786440 | tf_op jit(solution)/shard_map/ppermute | solution.py:340
  14.4 26.7 %copy-start.13 = (f32[2,4]{1,0:T(2,128)S(1)}, f32[2,4]{1,0:T(2,128)}, u32[]{:S(2)}) copy-start(f32[2,4]{1,0:T(2,128)} %param.9) | copy-start | bytes 100
  14.4 26.8 %copy-start.12 = (f32[2,4]{1,0:T(2,128)S(1)}, f32[2,4]{1,0:T(2,128)}, u32[]{:S(2)}) copy-start(f32[2,4]{1,0:T(2,128)} %param.10) | copy-start | bytes 100
  14.4 26.9 %copy-start.11 = (f32[4,4]{1,0:T(4,128)S(1)}, f32[4,4]{1,0:T(4,128)}, u32[]{:S(2)}) copy-start(f32[4,4]{1,0:T(4,128)} %param.11) | copy-start | bytes 196
  24.6 33.8 %copy-start = (bf16[1024,256]{1,0:T(8,128)(2,1)}, bf16[1024,256]{1,0:T(8,128)(2,1)S(1)}, u32[]{:S(2)}) copy-start(bf16[1024,256]{1,0:T(8,128)(2,1)S(1)} %pad_maximum_fusion.refs_0_) | copy-start | bytes 1572868
  24.6 16.4 %collective-permute-start.3 = (bf16[1024,256]{1,0:T(8,128)(2,1)S(1)}, bf16[1024,256]{1,0:T(8,128)(2,1)}, u32[]{:S(2)}, u32[]{:S(2)}) collective-permute-start(bf16[1024,256]{1,0:T(8,128)(2,1)S(1)} %pad_maximum_fusion.refs_0_), channel_id=1, source_target_pairs={{0,8},{8,16},{16,24},{24,32},{32,40},{40,48},{48,56},{56,0},{1,9},... | collective-permute-start | bytes 1572872 | tf_op jit(solution)/shard_map/ppermute | solution.py:336
  26.4 14.7 %collective-permute-start.4 = (bf16[1024,256]{1,0:T(8,128)(2,1)S(1)}, bf16[1024,256]{1,0:T(8,128)(2,1)}, u32[]{:S(2)}, u32[]{:S(2)}) collective-permute-start(bf16[1024,256]{1,0:T(8,128)(2,1)S(1)} %pad_maximum_fusion.refs_0_), channel_id=1, source_target_pairs={{0,56},{8,0},{16,8},{24,16},{32,24},{40,32},{48,40},{56,48},{1,57}... | collective-permute-start | bytes 1572872 | tf_op jit(solution)/shard_map/ppermute | solution.py:336
  32.9 25.5 %copy-start.1 = (bf16[1024,256]{1,0:T(8,128)(2,1)}, bf16[1024,256]{1,0:T(8,128)(2,1)S(1)}, u32[]{:S(2)}) copy-start(bf16[1024,256]{1,0:T(8,128)(2,1)S(1)} %pad_maximum_fusion.1.refs_1_) | copy-start | bytes 1572868
  33.0 19.4 %collective-permute-start.7 = (bf16[1024,256]{1,0:T(8,128)(2,1)S(1)}, bf16[1024,256]{1,0:T(8,128)(2,1)}, u32[]{:S(2)}, u32[]{:S(2)}) collective-permute-start(bf16[1024,256]{1,0:T(8,128)(2,1)S(1)} %pad_maximum_fusion.1.refs_1_), channel_id=1, source_target_pairs={{0,8},{8,16},{16,24},{24,32},{32,40},{40,48},{48,56},{56,0},{1,9},... | collective-permute-start | bytes 1572872 | tf_op jit(solution)/shard_map/ppermute | solution.py:336
  33.1 19.3 %collective-permute-start.8 = (bf16[1024,256]{1,0:T(8,128)(2,1)S(1)}, bf16[1024,256]{1,0:T(8,128)(2,1)}, u32[]{:S(2)}, u32[]{:S(2)}) collective-permute-start(bf16[1024,256]{1,0:T(8,128)(2,1)S(1)} %pad_maximum_fusion.1.refs_1_), channel_id=1, source_target_pairs={{0,56},{8,0},{16,8},{24,16},{32,24},{40,32},{48,40},{56,48},{1,57}... | collective-permute-start | bytes 1572872 | tf_op jit(solution)/shard_map/ppermute | solution.py:336
  47.8 15.1 %collective-permute-start.5 = (bf16[1024,256]{1,0:T(8,128)(2,1)}, bf16[1024,256]{1,0:T(8,128)(2,1)}, u32[]{:S(2)}, u32[]{:S(2)}) collective-permute-start(bf16[1024,256]{1,0:T(8,128)(2,1)} %collective-permute-done.3.refs_2_), channel_id=1, source_target_pairs={{0,8},{8,16},{16,24},{24,32},{32,40},{40,48},{48,56},{56,0},{1,9},... | collective-permute-start | bytes 1572872 | tf_op jit(solution)/shard_map/ppermute | solution.py:336
  47.9 15.0 %collective-permute-start.6 = (bf16[1024,256]{1,0:T(8,128)(2,1)}, bf16[1024,256]{1,0:T(8,128)(2,1)}, u32[]{:S(2)}, u32[]{:S(2)}) collective-permute-start(bf16[1024,256]{1,0:T(8,128)(2,1)} %collective-permute-done.4.refs_4_), channel_id=1, source_target_pairs={{0,56},{8,0},{16,8},{24,16},{32,24},{40,32},{48,40},{56,48},{1,57}... | collective-permute-start | bytes 1572872 | tf_op jit(solution)/shard_map/ppermute | solution.py:336
  52.3 21.7 %collective-permute-start.11 = (bf16[1024,256]{1,0:T(8,128)(2,1)}, bf16[1024,256]{1,0:T(8,128)(2,1)}, u32[]{:S(2)}, u32[]{:S(2)}) collective-permute-start(bf16[1024,256]{1,0:T(8,128)(2,1)} %collective-permute-done.7.refs_3_), channel_id=1, source_target_pairs={{0,8},{8,16},{16,24},{24,32},{32,40},{40,48},{48,56},{56,0},{1,9},... | collective-permute-start | bytes 1572872 | tf_op jit(solution)/shard_map/ppermute | solution.py:336
  52.3 21.7 %collective-permute-start.12 = (bf16[1024,256]{1,0:T(8,128)(2,1)}, bf16[1024,256]{1,0:T(8,128)(2,1)}, u32[]{:S(2)}, u32[]{:S(2)}) collective-permute-start(bf16[1024,256]{1,0:T(8,128)(2,1)} %collective-permute-done.8.refs_5_), channel_id=1, source_target_pairs={{0,56},{8,0},{16,8},{24,16},{32,24},{40,32},{48,40},{56,48},{1,57}... | collective-permute-start | bytes 1572872 | tf_op jit(solution)/shard_map/ppermute | solution.py:336
  55.0 4.6 %copy-start.9 = (s32[8192]{0:T(1024)S(1)}, s32[8192]{0:T(1024)}, u32[]{:S(2)}) copy-start(s32[8192]{0:T(1024)} %param.8) | copy-start | bytes 98308
  60.0 18.5 %copy-start.8 = (f32[4,1024]{1,0:T(4,128)}, f32[4,1024]{1,0:T(4,128)S(1)}, u32[]{:S(2)}) copy-start(f32[4,1024]{1,0:T(4,128)S(1)} %fusion.13.onehot_ref) | copy-start | bytes 49156
  60.5 20.8 %copy-start.10 = (f32[4,256]{1,0:T(4,128)}, f32[4,256]{1,0:T(4,128)S(1)}, u32[]{:S(2)}) copy-start(f32[4,256]{1,0:T(4,128)S(1)} %fusion.21.onehot_ref) | copy-start | bytes 12292
  62.9 21.4 %collective-permute-start.10 = (bf16[1024,256]{1,0:T(8,128)(2,1)}, bf16[1024,256]{1,0:T(8,128)(2,1)}, u32[]{:S(2)}, u32[]{:S(2)}) collective-permute-start(bf16[1024,256]{1,0:T(8,128)(2,1)} %collective-permute-done.6.refs_8_), channel_id=1, source_target_pairs={{0,56},{8,0},{16,8},{24,16},{32,24},{40,32},{48,40},{56,48},{1,57}... | collective-permute-start | bytes 1572872 | tf_op jit(solution)/shard_map/ppermute | solution.py:336
  65.3 20.0 %collective-permute-start.9 = (bf16[1024,256]{1,0:T(8,128)(2,1)}, bf16[1024,256]{1,0:T(8,128)(2,1)}, u32[]{:S(2)}, u32[]{:S(2)}) collective-permute-start(bf16[1024,256]{1,0:T(8,128)(2,1)} %collective-permute-done.5.refs_6_), channel_id=1, source_target_pairs={{0,8},{8,16},{16,24},{24,32},{32,40},{40,48},{48,56},{56,0},{1,9},... | collective-permute-start | bytes 1572872 | tf_op jit(solution)/shard_map/ppermute | solution.py:336
  74.0 25.8 %collective-permute-start.14 = (bf16[1024,256]{1,0:T(8,128)(2,1)}, bf16[1024,256]{1,0:T(8,128)(2,1)S(1)}, u32[]{:S(2)}, u32[]{:S(2)}) collective-permute-start(bf16[1024,256]{1,0:T(8,128)(2,1)} %collective-permute-done.11.refs_7_), channel_id=1, source_target_pairs={{0,8},{8,16},{16,24},{24,32},{32,40},{40,48},{48,56},{56,0},{1,9},... | collective-permute-start | bytes 1572872 | tf_op jit(solution)/shard_map/ppermute | solution.py:336
  74.0 25.8 %collective-permute-start.15 = (bf16[1024,256]{1,0:T(8,128)(2,1)}, bf16[1024,256]{1,0:T(8,128)(2,1)S(1)}, u32[]{:S(2)}, u32[]{:S(2)}) collective-permute-start(bf16[1024,256]{1,0:T(8,128)(2,1)} %collective-permute-done.12.refs_9_), channel_id=1, source_target_pairs={{0,56},{8,0},{16,8},{24,16},{32,24},{40,32},{48,40},{56,48},{1,57}... | collective-permute-start | bytes 1572872 | tf_op jit(solution)/shard_map/ppermute | solution.py:336
  85.2 22.4 %collective-permute-start.13 = (bf16[1024,256]{1,0:T(8,128)(2,1)}, bf16[1024,256]{1,0:T(8,128)(2,1)S(1)}, u32[]{:S(2)}, u32[]{:S(2)}) collective-permute-start(bf16[1024,256]{1,0:T(8,128)(2,1)} %collective-permute-done.9.refs_0_), channel_id=1, source_target_pairs={{0,8},{8,16},{16,24},{24,32},{32,40},{40,48},{48,56},{56,0},{1,9},... | collective-permute-start | bytes 1572872 | tf_op jit(solution)/shard_map/ppermute | solution.py:336
  99.8 7.8 %copy-start.2 = (bf16[1024,256]{1,0:T(8,128)(2,1)}, bf16[1024,256]{1,0:T(8,128)(2,1)S(1)}, u32[]{:S(2)}) copy-start(bf16[1024,256]{1,0:T(8,128)(2,1)S(1)} %collective-permute-done.14.refs_1_) | copy-start | bytes 1572868
  99.8 7.8 %copy-start.3 = (bf16[1024,256]{1,0:T(8,128)(2,1)}, bf16[1024,256]{1,0:T(8,128)(2,1)S(1)}, u32[]{:S(2)}) copy-start(bf16[1024,256]{1,0:T(8,128)(2,1)S(1)} %collective-permute-done.15.refs_3_) | copy-start | bytes 1572868
  99.9 13.8 %collective-permute-start.16 = (bf16[512,256]{1,0:T(8,128)(2,1)S(1)}, bf16[512,256]{1,0:T(8,128)(2,1)S(1)}, u32[]{:S(2)}, u32[]{:S(2)}) collective-permute-start(bf16[512,256]{1,0:T(8,128)(2,1)S(1)} %slice.127), channel_id=1, source_target_pairs={{0,8},{8,16},{16,24},{24,32},{32,40},{40,48},{48,56},{56,0},{1,9},... | collective-permute-start | bytes 786440 | tf_op jit(solution)/shard_map/ppermute | solution.py:336
  101.3 12.5 %collective-permute-start.17 = (bf16[512,256]{1,0:T(8,128)(2,1)S(1)}, bf16[512,256]{1,0:T(8,128)(2,1)S(1)}, u32[]{:S(2)}, u32[]{:S(2)}) collective-permute-start(bf16[512,256]{1,0:T(8,128)(2,1)S(1)} %slice.128), channel_id=1, source_target_pairs={{0,56},{8,0},{16,8},{24,16},{32,24},{40,32},{48,40},{56,48},{1,57}... | collective-permute-start | bytes 786440 | tf_op jit(solution)/shard_map/ppermute | solution.py:336
  107.6 6.1 %copy-start.5 = (bf16[1024,256]{1,0:T(8,128)(2,1)}, bf16[1024,256]{1,0:T(8,128)(2,1)S(1)}, u32[]{:S(2)}) copy-start(bf16[1024,256]{1,0:T(8,128)(2,1)S(1)} %collective-permute-done.13.first_ref) | copy-start | bytes 1572868
  113.7 0.7 copy-start.6
  114.4 0.7 copy-start.7
  121.0 23.6 %collective-permute-start.18 = (bf16[256,512]{1,0:T(8,128)(2,1)}, bf16[256,512]{1,0:T(8,128)(2,1)S(1)}, u32[]{:S(2)}, u32[]{:S(2)}) collective-permute-start(bf16[256,512]{1,0:T(8,128)(2,1)} %get-tuple-element.89), channel_id=1, source_target_pairs={{0,64},{64,128},{128,192},{192,0},{1,65},{65,129},{129,193},{193,1... | collective-permute-start | bytes 786440 | tf_op jit(solution)/shard_map/ppermute | solution.py:340
  122.8 21.9 %collective-permute-start.19 = (bf16[256,512]{1,0:T(8,128)(2,1)}, bf16[256,512]{1,0:T(8,128)(2,1)S(1)}, u32[]{:S(2)}, u32[]{:S(2)}) collective-permute-start(bf16[256,512]{1,0:T(8,128)(2,1)} %get-tuple-element.90), channel_id=1, source_target_pairs={{0,128},{64,192},{128,0},{192,64},{1,129},{65,193},{129,1},{193,65... | collective-permute-start | bytes 786440 | tf_op jit(solution)/shard_map/ppermute | solution.py:340
  126.4 18.2 %collective-permute-start.20 = (bf16[256,512]{1,0:T(8,128)(2,1)}, bf16[256,512]{1,0:T(8,128)(2,1)S(1)}, u32[]{:S(2)}, u32[]{:S(2)}) collective-permute-start(bf16[256,512]{1,0:T(8,128)(2,1)} %get-tuple-element.91), channel_id=1, source_target_pairs={{0,192},{64,0},{128,64},{192,128},{1,193},{65,1},{129,65},{193,129... | collective-permute-start | bytes 786440 | tf_op jit(solution)/shard_map/ppermute | solution.py:340
  144.6 0.7 copy-start.14
  144.6 0.8 copy-start.15
  144.6 0.8 copy-start.16
Sparse Core Ops, SparseCore 0:
  9.9 81.7 all-gather.1

commit v5 on v3

--- a/solution.py
+++ b/solution.py
@@ -13,7 +13,7 @@
 SLAB = 512
 AWAY = (0, 7, 1, 6, 2, 5, 3)
 AHEAD = 3
-VMEM_LIMIT = 58 * 1024 * 1024
+VMEM_LIMIT = 44 * 1024 * 1024
 F32 = jnp.float32
 BF16 = jnp.bfloat16
 PRECISE = lax.Precision.HIGHEST

time: 155 us -> 150 us (0.968)
  local copies, waits for them, and re-layouts: 16.2 us -> 22.4 us
  Pallas kernels: 21.9 us -> 16.2 us
  waiting for transfers between devices: 40 us -> 36.2 us
  matrix products: 6.45 us -> 9.1 us
  starting transfers between devices: 33.8 us -> 31.6 us
    ppermute x14, waiting for transfers between devices: 29.8 us -> 26 us  [ring(): return lax.ppermute(value, 'z', [(i, (i + by) % NZ) for i in range(NZ)])]
    reshape x1, local copies, waits for them, and re-layouts: 1.76 us -> 4.07 us  [tables(): toeplitz = tiled.reshape(classes, CH, padded_len - 1)[:, :, :CH]]
    pallas_call x1, Pallas kernels: 5.88 us -> 3.68 us  [last_product(): pl.pallas_call(last_kernel, grid_spec=pltpu.PrefetchScalarGridSpec(num_sc...]
    dot_general x1, matrix products: 3.45 us -> 5.44 us  [tables(): gains = jnp.einsum('ka,jkab->kbj', readout, powers, precision=PRECISE)]
    pallas_call x1, Pallas kernels: 9.77 us -> 7.91 us  [product(): pl.pallas_call(product_kernel, grid_spec=pltpu.PrefetchScalarGridSpec(num...]
    pallas_call x1, Pallas kernels: 6.26 us -> 4.6 us  [filtered(): pl.pallas_call(filter_kernel, grid_spec=pltpu.PrefetchScalarGridSpec(num_...]
    dot_general x1, local copies, waits for them, and re-layouts: 0.61 us -> 2.2 us  [tables(): gains = jnp.einsum('ka,jkab->kbj', readout, powers, precision=PRECISE)]
    unnamed x37 -> x19, local copies, waits for them, and re-layouts: 4.3 us -> 5.11 us
  transfers between devices with their start and end apart: 21 -> 21, of which waited for: 9 -> 7; matrix products, arithmetic and copies ran while one was open for 14% -> 21% of each run, Pallas kernels for 6% -> 5%
where the time goes in v5:
time: 150 us; the launch traced here: 149 us
  waiting for transfers between devices  36.2 us (24%)
  starting transfers between devices  31.6 us (21%)
  local copies, waits for them, and re-layouts  22.4 us (15%)
  blocking collectives  17 us (11%)
  Pallas kernels  16.2 us (11%)
  between operations  13.8 us (9%)
  matrix products  9.1 us (6%)
  other arithmetic  3.03 us (2%)
    ppermute x14, waiting for transfers between devices, ring(): return lax.ppermute(value, 'z', [(i, (i + by) % NZ) for i in range(NZ)])  26 us
    ppermute x14, starting transfers between devices, ring(): return lax.ppermute(value, 'z', [(i, (i + by) % NZ) for i in range(NZ)])  21.3 us
    all_to_all x1, blocking collectives, body(): own_ends = lax.all_to_all(to_send, ('y', 'c', 'x'), 0, 0, tiled=True)  17 us
    ppermute x6, starting transfers between devices, round_x(): return lax.ppermute(value, 'x', [(i, (i + by) % NX) for i in range(NX)])  10.4 us
    ppermute x6, waiting for transfers between devices, round_x(): return lax.ppermute(value, 'x', [(i, (i + by) % NX) for i in range(NX)])  10.1 us
    pallas_call x1, Pallas kernels, product(): pl.pallas_call(product_kernel, grid_spec=pltpu.PrefetchScalarGridSpec(num...  7.91 us
    dot_general x1, matrix products, tables(): gains = jnp.einsum('ka,jkab->kbj', readout, powers, precision=PRECISE)  5.44 us
    unnamed x19, local copies, waits for them, and re-layouts  5.11 us
  transfers between devices with their start and end apart: 21, of which 7 were waited for; matrix products, arithmetic and copies ran while one was open for 21% of the time, Pallas kernels for 5%

profile of v5, /device:TPU:1, one launch (start us, length us, event | category | flops | bytes accessed | tf_op | source)
XLA Modules:
  0.0 149.3 jit_solution(16062700398797682683)
XLA Ops:
  6.5 2.0 %constant_dynamic-slice_fusion.1 = bf16[32,8192]{1,0:T(8,128)(2,1)} fusion(bf16[256,8192]{1,0:T(8,128)(2,1)} %param.6, s32[]{:T(128)S(6)} %select_n.71), kind=kLoop, calls=%fused_computation.62 | loop fusion | bytes 1048580 | tf_op jit(solution)/shard_map/dynamic_slice | solution.py:334
  8.7 2.1 %collective-permute-start = (bf16[256,512]{1,0:T(8,128)(2,1)S(1)}, bf16[256,512]{1,0:T(8,128)(2,1)S(1)}, u32[]{:S(2)}, u32[]{:S(2)}) collective-permute-start(bf16[256,512]{1,0:T(8,128)(2,1)S(1)} %get-tuple-element.100), channel_id=1, source_target_pairs={{0,64},{64,128},{128,192},{192,0},{1,65},{65,129},{129,193},{193,1... | collective-permute-start | bytes 786440 | tf_op jit(solution)/shard_map/ppermute | solution.py:322
  10.8 2.5 %collective-permute-start.1 = (bf16[256,512]{1,0:T(8,128)(2,1)S(1)}, bf16[256,512]{1,0:T(8,128)(2,1)S(1)}, u32[]{:S(2)}, u32[]{:S(2)}) collective-permute-start(bf16[256,512]{1,0:T(8,128)(2,1)S(1)} %get-tuple-element.102), channel_id=1, source_target_pairs={{0,128},{64,192},{128,0},{192,64},{1,129},{65,193},{129,1},{193,65... | collective-permute-start | bytes 786440 | tf_op jit(solution)/shard_map/ppermute | solution.py:322
  13.2 1.2 collective-permute-start.2
  14.4 1.4 collective-permute-done
  15.8 8.7 %collective-permute-done.1 = bf16[256,512]{1,0:T(8,128)(2,1)S(1)} collective-permute-done((bf16[256,512]{1,0:T(8,128)(2,1)S(1)}, bf16[256,512]{1,0:T(8,128)(2,1)S(1)}, u32[]{:S(2)}, u32[]{:S(2)}) %collective-permute-start.1) | collective-permute-done | bytes 262176 | tf_op jit(solution)/shard_map/ppermute | solution.py:322
  24.7 1.7 %collective-permute-start.3 = (bf16[1024,256]{1,0:T(8,128)(2,1)S(1)}, bf16[1024,256]{1,0:T(8,128)(2,1)S(1)}, u32[]{:S(2)}, u32[]{:S(2)}) collective-permute-start(bf16[1024,256]{1,0:T(8,128)(2,1)S(1)} %pad_maximum_fusion.refs_0_), channel_id=1, source_target_pairs={{0,8},{8,16},{16,24},{24,32},{32,40},{40,48},{48,56},{56,0},{1,9},... | collective-permute-start | bytes 1572872 | tf_op jit(solution)/shard_map/ppermute | solution.py:318
  26.4 4.0 %collective-permute-start.4 = (bf16[1024,256]{1,0:T(8,128)(2,1)S(1)}, bf16[1024,256]{1,0:T(8,128)(2,1)S(1)}, u32[]{:S(2)}, u32[]{:S(2)}) collective-permute-start(bf16[1024,256]{1,0:T(8,128)(2,1)S(1)} %pad_maximum_fusion.refs_0_), channel_id=1, source_target_pairs={{0,56},{8,0},{16,8},{24,16},{32,24},{40,32},{48,40},{56,48},{1,57}... | collective-permute-start | bytes 1572872 | tf_op jit(solution)/shard_map/ppermute | solution.py:318
  30.4 0.6 pad.40.clone
  31.3 2.7 %collective-permute-start.8 = (bf16[1024,256]{1,0:T(8,128)(2,1)S(1)}, bf16[1024,256]{1,0:T(8,128)(2,1)S(1)}, u32[]{:S(2)}, u32[]{:S(2)}) collective-permute-start(bf16[1024,256]{1,0:T(8,128)(2,1)S(1)} %pad_maximum_fusion.1.refs_1_), channel_id=1, source_target_pairs={{0,56},{8,0},{16,8},{24,16},{32,24},{40,32},{48,40},{56,48},{1,57}... | collective-permute-start | bytes 1572872 | tf_op jit(solution)/shard_map/ppermute | solution.py:318
  34.0 7.0 %collective-permute-done.3.refs_2_ = bf16[1024,256]{1,0:T(8,128)(2,1)S(1)} collective-permute-done((bf16[1024,256]{1,0:T(8,128)(2,1)S(1)}, bf16[1024,256]{1,0:T(8,128)(2,1)S(1)}, u32[]{:S(2)}, u32[]{:S(2)}) %collective-permute-start.3) | collective-permute-done | bytes 524320 | tf_op jit(solution)/shard_map/ppermute | solution.py:318
  41.5 0.5 bitcast_multiply_fusion.4
  42.5 0.7 fusion.23
  43.5 0.2 fusion.24
  44.7 1.0 convolution_bitcast_fusion.4
  45.8 0.2 copy.138
  47.2 0.2 concatenate.55
  47.9 0.2 concatenate.56
  48.5 0.2 concatenate.57
  49.3 2.7 %collective-permute-start.6 = (bf16[1024,256]{1,0:T(8,128)(2,1)S(1)}, bf16[1024,256]{1,0:T(8,128)(2,1)}, u32[]{:S(2)}, u32[]{:S(2)}) collective-permute-start(bf16[1024,256]{1,0:T(8,128)(2,1)S(1)} %collective-permute-done.4.refs_4_), channel_id=1, source_target_pairs={{0,56},{8,0},{16,8},{24,16},{32,24},{40,32},{48,40},{56,48},{1,57}... | collective-permute-start | bytes 1572872 | tf_op jit(solution)/shard_map/ppermute | solution.py:318
  52.0 0.3 collective-permute-done.7.refs_3_
  52.3 2.7 %collective-permute-start.12 = (bf16[1024,256]{1,0:T(8,128)(2,1)S(1)}, bf16[1024,256]{1,0:T(8,128)(2,1)}, u32[]{:S(2)}, u32[]{:S(2)}) collective-permute-start(bf16[1024,256]{1,0:T(8,128)(2,1)S(1)} %collective-permute-done.8.refs_5_), channel_id=1, source_target_pairs={{0,56},{8,0},{16,8},{24,16},{32,24},{40,32},{48,40},{56,48},{1,57}... | collective-permute-start | bytes 1572872 | tf_op jit(solution)/shard_map/ppermute | solution.py:318
  54.9 0.8 fusion.34
  56.1 0.8 fusion.41
  57.0 0.2 multiply_reduce_fusion.power_ref
  57.8 5.4 %fusion.42 = f32[4,1,256,4]{1,2,3,0:T(8,128)} fusion(f32[256,4,4,4]{0,2,3,1:T(4,128)S(1)} %concatenate.57, f32[4,4,1,1]{1,2,3,0:T(1,128)} %bitcast.198), kind=kOutput, calls=%fused_computation.101 | convolution fusion | flops 196608 | bytes 81984 | tf_op jit(solution)/shard_map/ka,jkab->kbj/dot_general | solution.py:56
  63.2 2.2 %copy.182 = f32[4,1,256,4]{2,3,0,1:T(4,128)S(1)} copy(f32[4,1,256,4]{1,2,3,0:T(8,128)} %fusion.42) | data formatting | bytes 32768 | tf_op jit(solution)/shard_map/ka,jkab->kbj/dot_general | solution.py:56
  65.4 1.1 broadcast_bitcast_fusion
  66.5 1.4 collective-permute-start.10
  68.0 4.9 %collective-permute-done.11.refs_7_ = bf16[1024,256]{1,0:T(8,128)(2,1)} collective-permute-done((bf16[1024,256]{1,0:T(8,128)(2,1)S(1)}, bf16[1024,256]{1,0:T(8,128)(2,1)}, u32[]{:S(2)}, u32[]{:S(2)}) %collective-permute-start.11) | collective-permute-done | bytes 524320 | tf_op jit(solution)/shard_map/ppermute | solution.py:318
  72.8 2.5 %collective-permute-start.14 = (bf16[1024,256]{1,0:T(8,128)(2,1)}, bf16[1024,256]{1,0:T(8,128)(2,1)}, u32[]{:S(2)}, u32[]{:S(2)}) collective-permute-start(bf16[1024,256]{1,0:T(8,128)(2,1)} %collective-permute-done.12.refs_9_), channel_id=1, source_target_pairs={{0,56},{8,0},{16,8},{24,16},{32,24},{40,32},{48,40},{56,48},{1,57}... | collective-permute-start | bytes 1572872 | tf_op jit(solution)/shard_map/ppermute | solution.py:318
  75.5 2.1 %copy.191 = bf16[1,4,256,512]{3,1,2,0:T(4,128)(2,1)S(1)} copy(bf16[1,4,256,512]{3,2,1,0:T(8,128)(2,1)} %broadcast_bitcast_fusion) | data formatting | bytes 2097152
  77.6 1.3 slice.132
  79.0 4.1 %reshape.340 = bf16[4,256,511]{2,1,0:T(8,128)(2,1)} reshape(bf16[4,130816]{1,0:T(4,128)(2,1)} %slice.132) | data formatting | bytes 2093056 | tf_op jit(solution)/shard_map/reshape | solution.py:63
  83.0 1.9 %slice.133 = bf16[4,256,256]{2,1,0:T(8,128)(2,1)} slice(bf16[4,256,511]{2,1,0:T(8,128)(2,1)} %reshape.340), slice={[0:4], [0:256], [0:256]} | slice | bytes 1048576 | tf_op jit(solution)/shard_map/slice | solution.py:63
  85.2 0.2 multiply_reduce_fusion.1
  85.5 8.9 %collective-permute-done.14.refs_13_ = bf16[1024,256]{1,0:T(8,128)(2,1)} collective-permute-done((bf16[1024,256]{1,0:T(8,128)(2,1)}, bf16[1024,256]{1,0:T(8,128)(2,1)}, u32[]{:S(2)}, u32[]{:S(2)}) %collective-permute-start.14) | collective-permute-done | bytes 524320 | tf_op jit(solution)/shard_map/ppermute | solution.py:318
  94.4 3.4 %collective-permute-start.15 = (bf16[1024,256]{1,0:T(8,128)(2,1)}, bf16[1024,256]{1,0:T(8,128)(2,1)}, u32[]{:S(2)}, u32[]{:S(2)}) collective-permute-start(bf16[1024,256]{1,0:T(8,128)(2,1)} %collective-permute-done.14.refs_13_), channel_id=1, source_target_pairs={{0,56},{8,0},{16,8},{24,16},{32,24},{40,32},{48,40},{56,48},{1,57}... | collective-permute-start | bytes 1572872 | tf_op jit(solution)/shard_map/ppermute | solution.py:318
  97.8 0.8 copy-done
  98.6 1.0 copy-done.1
  99.6 7.9 %shard_map.64.total_ref = f32[1024,512]{1,0:T(8,128)S(1)} custom-call(s32[9]{0:T(128)S(1)} %stack.92.zs, bf16[4,256,8192]{2,1,0:T(8,128)(2,1)} %bitcast.182, bf16[1024,256]{1,0:T(8,128)(2,1)S(1)} %pad_maximum_fusion.refs_0_, bf16[1024,256]{1,0:T(8,128)(2,1)S(1)} %pad_maximum_fusion.1.refs_1_, bf16[1024,256]{1,0:T(8,128)(2,1)S(1)} %collective-permute-done.3.refs_2_, ...), custom_call_target="tpu_custom_call" | custom-call | flops 4697620480 | bytes 19922944 | tf_op jit(solution)/shard_map/pallas_call | solution.py:160
  107.6 5.0 %collective-permute-done.13.first_ref = bf16[1024,256]{1,0:T(8,128)(2,1)} collective-permute-done((bf16[1024,256]{1,0:T(8,128)(2,1)}, bf16[1024,256]{1,0:T(8,128)(2,1)}, u32[]{:S(2)}, u32[]{:S(2)}) %collective-permute-start.13) | collective-permute-done | bytes 524320 | tf_op jit(solution)/shard_map/ppermute | solution.py:318
  112.5 3.7 %shard_map.65 = (bf16[256,512]{1,0:T(8,128)(2,1)S(1)}, bf16[256,512]{1,0:T(8,128)(2,1)S(1)}, bf16[256,512]{1,0:T(8,128)(2,1)S(1)}, bf16[256,512]{1,0:T(8,128)(2,1)S(1)}, f32[32,4,256]{2,1,0:T(4,128)S(1)}) custom-call(s32[9]{0:T(128)S(1)} %stack.92.zs, bf16[4,256,8192]{2,1,0:T(8,128)(2,1)} %bitcast.183, bf16[1024,256]{1,0:T(8,128)(2,1)} %collective-permute-done.13.first_ref, ...), custom_call_target="tpu_custom_call" | custom-call | flops 738197504 | bytes 6291456 | tf_op jit(solution)/shard_map/pallas_call | solution.py:224
  116.2 0.8 collective-permute-start.17
  117.0 2.0 %collective-permute-start.18 = (bf16[256,512]{1,0:T(8,128)(2,1)S(1)}, bf16[256,512]{1,0:T(8,128)(2,1)S(1)}, u32[]{:S(2)}, u32[]{:S(2)}) collective-permute-start(bf16[256,512]{1,0:T(8,128)(2,1)S(1)} %get-tuple-element.78), channel_id=1, source_target_pairs={{0,128},{64,192},{128,0},{192,64},{1,129},{65,193},{129,1},{193,65... | collective-permute-start | bytes 786440 | tf_op jit(solution)/shard_map/ppermute | solution.py:322
  119.0 1.8 %collective-permute-start.19 = (bf16[256,512]{1,0:T(8,128)(2,1)S(1)}, bf16[256,512]{1,0:T(8,128)(2,1)S(1)}, u32[]{:S(2)}, u32[]{:S(2)}) collective-permute-start(bf16[256,512]{1,0:T(8,128)(2,1)S(1)} %get-tuple-element.79), channel_id=1, source_target_pairs={{0,192},{64,0},{128,64},{192,128},{1,193},{65,1},{129,65},{193,129... | collective-permute-start | bytes 786440 | tf_op jit(solution)/shard_map/ppermute | solution.py:322
  120.8 17.0 %all_to_all.5.slabs_ref = f32[32,4,256]{2,1,0:T(4,128)S(1)} all-to-all(f32[32,4,256]{2,1,0:T(4,128)S(1)} %get-tuple-element.80), channel_id=1, replica_groups=mesh['x'=4,'z'=8,'y'=4,'c'=2] {'y','c','x'}, dimensions={0} | all-to-all | bytes 262144 | tf_op jit(solution)/shard_map/all_to_all | solution.py:381
  137.9 4.6 %shard_map.66 = f32[256,2048]{1,0:T(8,128)} custom-call(s32[2]{0:T(128)S(1)} %pad_add_fusion.place, bf16[256,512]{1,0:T(8,128)(2,1)S(1)} %get-tuple-element.76.own_ref, bf16[256,512]{1,0:T(8,128)(2,1)S(1)} %collective-permute-done.17.by_one_ref, bf16[256,512]{1,0:T(8,128)(2,1)S(1)} %collective-permute-done.18.by_two_ref, ...), custom_call_target="tpu_custom_call" | custom-call | flops 1153433600 | bytes 4194304 | tf_op jit(solution)/shard_map/pallas_call | solution.py:296
  (107 shorter events, 7.0 us)
Async XLA Ops:
  6.5 2.0 %copy-start.3 = (bf16[256,2048]{1,0:T(8,128)(2,1)S(1)}, bf16[256,2048]{1,0:T(8,128)(2,1)}, u32[]{:S(2)}) copy-start(bf16[256,2048]{1,0:T(8,128)(2,1)} %param.7) | copy-start | bytes 3145732
  6.5 92.0 %all-gather.2.cloned.1.call-start = ((), (), s32[]{:S(2)}) async-start(), calls=%async_computation.1 | async-start | bytes 17301504 | tf_op jit(solution)/shard_map/all_gather | solution.py:335
  8.7 7.1 %collective-permute-start = (bf16[256,512]{1,0:T(8,128)(2,1)S(1)}, bf16[256,512]{1,0:T(8,128)(2,1)S(1)}, u32[]{:S(2)}, u32[]{:S(2)}) collective-permute-start(bf16[256,512]{1,0:T(8,128)(2,1)S(1)} %get-tuple-element.100), channel_id=1, source_target_pairs={{0,64},{64,128},{128,192},{192,0},{1,65},{65,129},{129,193},{193,1... | collective-permute-start | bytes 786440 | tf_op jit(solution)/shard_map/ppermute | solution.py:322
  10.8 13.8 %collective-permute-start.1 = (bf16[256,512]{1,0:T(8,128)(2,1)S(1)}, bf16[256,512]{1,0:T(8,128)(2,1)S(1)}, u32[]{:S(2)}, u32[]{:S(2)}) collective-permute-start(bf16[256,512]{1,0:T(8,128)(2,1)S(1)} %get-tuple-element.102), channel_id=1, source_target_pairs={{0,128},{64,192},{128,0},{192,64},{1,129},{65,193},{129,1},{193,65... | collective-permute-start | bytes 786440 | tf_op jit(solution)/shard_map/ppermute | solution.py:322
  13.2 11.3 %collective-permute-start.2 = (bf16[256,512]{1,0:T(8,128)(2,1)S(1)}, bf16[256,512]{1,0:T(8,128)(2,1)S(1)}, u32[]{:S(2)}, u32[]{:S(2)}) collective-permute-start(bf16[256,512]{1,0:T(8,128)(2,1)S(1)} %get-tuple-element.101), channel_id=1, source_target_pairs={{0,192},{64,0},{128,64},{192,128},{1,193},{65,1},{129,65},{193,129... | collective-permute-start | bytes 786440 | tf_op jit(solution)/shard_map/ppermute | solution.py:322
  14.4 26.6 %copy-start.7 = (f32[2,4]{1,0:T(2,128)S(1)}, f32[2,4]{1,0:T(2,128)}, u32[]{:S(2)}) copy-start(f32[2,4]{1,0:T(2,128)} %param.9) | copy-start | bytes 100
  14.4 26.6 %copy-start.6 = (f32[2,4]{1,0:T(2,128)S(1)}, f32[2,4]{1,0:T(2,128)}, u32[]{:S(2)}) copy-start(f32[2,4]{1,0:T(2,128)} %param.10) | copy-start | bytes 100
  14.4 26.8 %copy-start.5 = (f32[4,4]{1,0:T(4,128)S(1)}, f32[4,4]{1,0:T(4,128)}, u32[]{:S(2)}) copy-start(f32[4,4]{1,0:T(4,128)} %param.11) | copy-start | bytes 196
  24.7 16.3 %collective-permute-start.3 = (bf16[1024,256]{1,0:T(8,128)(2,1)S(1)}, bf16[1024,256]{1,0:T(8,128)(2,1)S(1)}, u32[]{:S(2)}, u32[]{:S(2)}) collective-permute-start(bf16[1024,256]{1,0:T(8,128)(2,1)S(1)} %pad_maximum_fusion.refs_0_), channel_id=1, source_target_pairs={{0,8},{8,16},{16,24},{24,32},{32,40},{40,48},{48,56},{56,0},{1,9},... | collective-permute-start | bytes 1572872 | tf_op jit(solution)/shard_map/ppermute | solution.py:318
  26.4 14.6 %collective-permute-start.4 = (bf16[1024,256]{1,0:T(8,128)(2,1)S(1)}, bf16[1024,256]{1,0:T(8,128)(2,1)S(1)}, u32[]{:S(2)}, u32[]{:S(2)}) collective-permute-start(bf16[1024,256]{1,0:T(8,128)(2,1)S(1)} %pad_maximum_fusion.refs_0_), channel_id=1, source_target_pairs={{0,56},{8,0},{16,8},{24,16},{32,24},{40,32},{48,40},{56,48},{1,57}... | collective-permute-start | bytes 1572872 | tf_op jit(solution)/shard_map/ppermute | solution.py:318
  31.0 25.9 %copy-start.4 = (s32[8192]{0:T(1024)S(1)}, s32[8192]{0:T(1024)}, u32[]{:S(2)}) copy-start(s32[8192]{0:T(1024)} %param.8) | copy-start | bytes 98308
  31.2 21.0 %collective-permute-start.7 = (bf16[1024,256]{1,0:T(8,128)(2,1)S(1)}, bf16[1024,256]{1,0:T(8,128)(2,1)S(1)}, u32[]{:S(2)}, u32[]{:S(2)}) collective-permute-start(bf16[1024,256]{1,0:T(8,128)(2,1)S(1)} %pad_maximum_fusion.1.refs_1_), channel_id=1, source_target_pairs={{0,8},{8,16},{16,24},{24,32},{32,40},{40,48},{48,56},{56,0},{1,9},... | collective-permute-start | bytes 1572872 | tf_op jit(solution)/shard_map/ppermute | solution.py:318
  31.3 20.9 %collective-permute-start.8 = (bf16[1024,256]{1,0:T(8,128)(2,1)S(1)}, bf16[1024,256]{1,0:T(8,128)(2,1)S(1)}, u32[]{:S(2)}, u32[]{:S(2)}) collective-permute-start(bf16[1024,256]{1,0:T(8,128)(2,1)S(1)} %pad_maximum_fusion.1.refs_1_), channel_id=1, source_target_pairs={{0,56},{8,0},{16,8},{24,16},{32,24},{40,32},{48,40},{56,48},{1,57}... | collective-permute-start | bytes 1572872 | tf_op jit(solution)/shard_map/ppermute | solution.py:318
  49.2 17.3 %collective-permute-start.5 = (bf16[1024,256]{1,0:T(8,128)(2,1)S(1)}, bf16[1024,256]{1,0:T(8,128)(2,1)}, u32[]{:S(2)}, u32[]{:S(2)}) collective-permute-start(bf16[1024,256]{1,0:T(8,128)(2,1)S(1)} %collective-permute-done.3.refs_2_), channel_id=1, source_target_pairs={{0,8},{8,16},{16,24},{24,32},{32,40},{40,48},{48,56},{56,0},{1,9},... | collective-permute-start | bytes 1572872 | tf_op jit(solution)/shard_map/ppermute | solution.py:318
  49.3 17.2 %collective-permute-start.6 = (bf16[1024,256]{1,0:T(8,128)(2,1)S(1)}, bf16[1024,256]{1,0:T(8,128)(2,1)}, u32[]{:S(2)}, u32[]{:S(2)}) collective-permute-start(bf16[1024,256]{1,0:T(8,128)(2,1)S(1)} %collective-permute-done.4.refs_4_), channel_id=1, source_target_pairs={{0,56},{8,0},{16,8},{24,16},{32,24},{40,32},{48,40},{56,48},{1,57}... | collective-permute-start | bytes 1572872 | tf_op jit(solution)/shard_map/ppermute | solution.py:318
  52.2 20.6 %collective-permute-start.11 = (bf16[1024,256]{1,0:T(8,128)(2,1)S(1)}, bf16[1024,256]{1,0:T(8,128)(2,1)}, u32[]{:S(2)}, u32[]{:S(2)}) collective-permute-start(bf16[1024,256]{1,0:T(8,128)(2,1)S(1)} %collective-permute-done.7.refs_3_), channel_id=1, source_target_pairs={{0,8},{8,16},{16,24},{24,32},{32,40},{40,48},{48,56},{56,0},{1,9},... | collective-permute-start | bytes 1572872 | tf_op jit(solution)/shard_map/ppermute | solution.py:318
  52.3 20.6 %collective-permute-start.12 = (bf16[1024,256]{1,0:T(8,128)(2,1)S(1)}, bf16[1024,256]{1,0:T(8,128)(2,1)}, u32[]{:S(2)}, u32[]{:S(2)}) collective-permute-start(bf16[1024,256]{1,0:T(8,128)(2,1)S(1)} %collective-permute-done.8.refs_5_), channel_id=1, source_target_pairs={{0,56},{8,0},{16,8},{24,16},{32,24},{40,32},{48,40},{56,48},{1,57}... | collective-permute-start | bytes 1572872 | tf_op jit(solution)/shard_map/ppermute | solution.py:318
  66.5 19.0 %collective-permute-start.10 = (bf16[1024,256]{1,0:T(8,128)(2,1)}, bf16[1024,256]{1,0:T(8,128)(2,1)}, u32[]{:S(2)}, u32[]{:S(2)}) collective-permute-start(bf16[1024,256]{1,0:T(8,128)(2,1)} %collective-permute-done.6.refs_8_), channel_id=1, source_target_pairs={{0,56},{8,0},{16,8},{24,16},{32,24},{40,32},{48,40},{56,48},{1,57}... | collective-permute-start | bytes 1572872 | tf_op jit(solution)/shard_map/ppermute | solution.py:318
  67.9 17.6 %collective-permute-start.9 = (bf16[1024,256]{1,0:T(8,128)(2,1)}, bf16[1024,256]{1,0:T(8,128)(2,1)}, u32[]{:S(2)}, u32[]{:S(2)}) collective-permute-start(bf16[1024,256]{1,0:T(8,128)(2,1)} %collective-permute-done.5.refs_6_), channel_id=1, source_target_pairs={{0,8},{8,16},{16,24},{24,32},{32,40},{40,48},{48,56},{56,0},{1,9},... | collective-permute-start | bytes 1572872 | tf_op jit(solution)/shard_map/ppermute | solution.py:318
  72.8 21.5 %collective-permute-start.14 = (bf16[1024,256]{1,0:T(8,128)(2,1)}, bf16[1024,256]{1,0:T(8,128)(2,1)}, u32[]{:S(2)}, u32[]{:S(2)}) collective-permute-start(bf16[1024,256]{1,0:T(8,128)(2,1)} %collective-permute-done.12.refs_9_), channel_id=1, source_target_pairs={{0,56},{8,0},{16,8},{24,16},{32,24},{40,32},{48,40},{56,48},{1,57}... | collective-permute-start | bytes 1572872 | tf_op jit(solution)/shard_map/ppermute | solution.py:318
  85.1 12.7 %collective-permute-start.16 = (bf16[1024,256]{1,0:T(8,128)(2,1)}, bf16[1024,256]{1,0:T(8,128)(2,1)S(1)}, u32[]{:S(2)}, u32[]{:S(2)}) collective-permute-start(bf16[1024,256]{1,0:T(8,128)(2,1)} %collective-permute-done.11.refs_7_), channel_id=1, source_target_pairs={{0,8},{8,16},{16,24},{24,32},{32,40},{40,48},{48,56},{56,0},{1,9},... | collective-permute-start | bytes 1572872 | tf_op jit(solution)/shard_map/ppermute | solution.py:318
  94.4 13.2 %collective-permute-start.15 = (bf16[1024,256]{1,0:T(8,128)(2,1)}, bf16[1024,256]{1,0:T(8,128)(2,1)}, u32[]{:S(2)}, u32[]{:S(2)}) collective-permute-start(bf16[1024,256]{1,0:T(8,128)(2,1)} %collective-permute-done.14.refs_13_), channel_id=1, source_target_pairs={{0,56},{8,0},{16,8},{24,16},{32,24},{40,32},{48,40},{56,48},{1,57}... | collective-permute-start | bytes 1572872 | tf_op jit(solution)/shard_map/ppermute | solution.py:318
  97.8 14.7 %collective-permute-start.13 = (bf16[1024,256]{1,0:T(8,128)(2,1)}, bf16[1024,256]{1,0:T(8,128)(2,1)}, u32[]{:S(2)}, u32[]{:S(2)}) collective-permute-start(bf16[1024,256]{1,0:T(8,128)(2,1)} %collective-permute-done.9.refs_10_), channel_id=1, source_target_pairs={{0,8},{8,16},{16,24},{24,32},{32,40},{40,48},{48,56},{56,0},{1,9},... | collective-permute-start | bytes 1572872 | tf_op jit(solution)/shard_map/ppermute | solution.py:318
  97.8 0.8 copy-start
  98.6 1.0 copy-start.1
  107.5 30.3 %copy-start.2 = (bf16[4,256,256]{2,1,0:T(8,128)(2,1)S(1)}, bf16[4,256,256]{2,1,0:T(8,128)(2,1)}, u32[]{:S(2)}) copy-start(bf16[4,256,256]{2,1,0:T(8,128)(2,1)} %slice.133) | copy-start | bytes 1572868
  116.2 21.6 %collective-permute-start.17 = (bf16[256,512]{1,0:T(8,128)(2,1)S(1)}, bf16[256,512]{1,0:T(8,128)(2,1)S(1)}, u32[]{:S(2)}, u32[]{:S(2)}) collective-permute-start(bf16[256,512]{1,0:T(8,128)(2,1)S(1)} %get-tuple-element.77), channel_id=1, source_target_pairs={{0,64},{64,128},{128,192},{192,0},{1,65},{65,129},{129,193},{193,1... | collective-permute-start | bytes 786440 | tf_op jit(solution)/shard_map/ppermute | solution.py:322
  117.0 20.8 %collective-permute-start.18 = (bf16[256,512]{1,0:T(8,128)(2,1)S(1)}, bf16[256,512]{1,0:T(8,128)(2,1)S(1)}, u32[]{:S(2)}, u32[]{:S(2)}) collective-permute-start(bf16[256,512]{1,0:T(8,128)(2,1)S(1)} %get-tuple-element.78), channel_id=1, source_target_pairs={{0,128},{64,192},{128,0},{192,64},{1,129},{65,193},{129,1},{193,65... | collective-permute-start | bytes 786440 | tf_op jit(solution)/shard_map/ppermute | solution.py:322
  119.0 18.8 %collective-permute-start.19 = (bf16[256,512]{1,0:T(8,128)(2,1)S(1)}, bf16[256,512]{1,0:T(8,128)(2,1)S(1)}, u32[]{:S(2)}, u32[]{:S(2)}) collective-permute-start(bf16[256,512]{1,0:T(8,128)(2,1)S(1)} %get-tuple-element.79), channel_id=1, source_target_pairs={{0,192},{64,0},{128,64},{192,128},{1,193},{65,1},{129,65},{193,129... | collective-permute-start | bytes 786440 | tf_op jit(solution)/shard_map/ppermute | solution.py:322
Sparse Core Ops, SparseCore 0:
  9.9 81.7 all-gather.1

commit v6 on v5

--- a/solution.py
+++ b/solution.py
@@ -13,7 +13,7 @@
 SLAB = 512
 AWAY = (0, 7, 1, 6, 2, 5, 3)
 AHEAD = 3
-VMEM_LIMIT = 44 * 1024 * 1024
+VMEM_LIMIT = 36 * 1024 * 1024
 F32 = jnp.float32
 BF16 = jnp.bfloat16
 PRECISE = lax.Precision.HIGHEST

time: 150 us -> 150 us (level)
  no operation moved by 1% of the time
where the time goes in v6:
time: 150 us; the launch traced here: 149 us
  waiting for transfers between devices  36.2 us (24%)
  starting transfers between devices  31.6 us (21%)
  local copies, waits for them, and re-layouts  22.4 us (15%)
  blocking collectives  17 us (11%)
  Pallas kernels  16.2 us (11%)
  between operations  13.8 us (9%)
  matrix products  9.1 us (6%)
  other arithmetic  3.03 us (2%)
    ppermute x14, waiting for transfers between devices, ring(): return lax.ppermute(value, 'z', [(i, (i + by) % NZ) for i in range(NZ)])  26 us
    ppermute x14, starting transfers between devices, ring(): return lax.ppermute(value, 'z', [(i, (i + by) % NZ) for i in range(NZ)])  21.3 us
    all_to_all x1, blocking collectives, body(): own_ends = lax.all_to_all(to_send, ('y', 'c', 'x'), 0, 0, tiled=True)  17 us
    ppermute x6, starting transfers between devices, round_x(): return lax.ppermute(value, 'x', [(i, (i + by) % NX) for i in range(NX)])  10.4 us
    ppermute x6, waiting for transfers between devices, round_x(): return lax.ppermute(value, 'x', [(i, (i + by) % NX) for i in range(NX)])  10.1 us
    pallas_call x1, Pallas kernels, product(): pl.pallas_call(product_kernel, grid_spec=pltpu.PrefetchScalarGridSpec(num...  7.91 us
    dot_general x1, matrix products, tables(): gains = jnp.einsum('ka,jkab->kbj', readout, powers, precision=PRECISE)  5.44 us
    unnamed x19, local copies, waits for them, and re-layouts  5.11 us
  transfers between devices with their start and end apart: 21, of which 7 were waited for; matrix products, arithmetic and copies ran while one was open for 21% of the time, Pallas kernels for 5%

profile of v6, /device:TPU:1, one launch (start us, length us, event | category | flops | bytes accessed | tf_op | source)
XLA Modules:
  0.0 149.3 jit_solution(1535153196455175733)
XLA Ops:
  6.5 2.0 %constant_dynamic-slice_fusion.1 = bf16[32,8192]{1,0:T(8,128)(2,1)} fusion(bf16[256,8192]{1,0:T(8,128)(2,1)} %param.6, s32[]{:T(128)S(6)} %select_n.71), kind=kLoop, calls=%fused_computation.62 | loop fusion | bytes 1048580 | tf_op jit(solution)/shard_map/dynamic_slice | solution.py:334
  8.7 2.1 %collective-permute-start = (bf16[256,512]{1,0:T(8,128)(2,1)S(1)}, bf16[256,512]{1,0:T(8,128)(2,1)S(1)}, u32[]{:S(2)}, u32[]{:S(2)}) collective-permute-start(bf16[256,512]{1,0:T(8,128)(2,1)S(1)} %get-tuple-element.100), channel_id=1, source_target_pairs={{0,64},{64,128},{128,192},{192,0},{1,65},{65,129},{129,193},{193,1... | collective-permute-start | bytes 786440 | tf_op jit(solution)/shard_map/ppermute | solution.py:322
  10.8 2.5 %collective-permute-start.1 = (bf16[256,512]{1,0:T(8,128)(2,1)S(1)}, bf16[256,512]{1,0:T(8,128)(2,1)S(1)}, u32[]{:S(2)}, u32[]{:S(2)}) collective-permute-start(bf16[256,512]{1,0:T(8,128)(2,1)S(1)} %get-tuple-element.102), channel_id=1, source_target_pairs={{0,128},{64,192},{128,0},{192,64},{1,129},{65,193},{129,1},{193,65... | collective-permute-start | bytes 786440 | tf_op jit(solution)/shard_map/ppermute | solution.py:322
  13.2 1.2 collective-permute-start.2
  14.4 1.4 collective-permute-done
  15.8 8.7 %collective-permute-done.1 = bf16[256,512]{1,0:T(8,128)(2,1)S(1)} collective-permute-done((bf16[256,512]{1,0:T(8,128)(2,1)S(1)}, bf16[256,512]{1,0:T(8,128)(2,1)S(1)}, u32[]{:S(2)}, u32[]{:S(2)}) %collective-permute-start.1) | collective-permute-done | bytes 262176 | tf_op jit(solution)/shard_map/ppermute | solution.py:322
  24.7 1.7 %collective-permute-start.3 = (bf16[1024,256]{1,0:T(8,128)(2,1)S(1)}, bf16[1024,256]{1,0:T(8,128)(2,1)S(1)}, u32[]{:S(2)}, u32[]{:S(2)}) collective-permute-start(bf16[1024,256]{1,0:T(8,128)(2,1)S(1)} %pad_maximum_fusion.refs_0_), channel_id=1, source_target_pairs={{0,8},{8,16},{16,24},{24,32},{32,40},{40,48},{48,56},{56,0},{1,9},... | collective-permute-start | bytes 1572872 | tf_op jit(solution)/shard_map/ppermute | solution.py:318
  26.4 4.0 %collective-permute-start.4 = (bf16[1024,256]{1,0:T(8,128)(2,1)S(1)}, bf16[1024,256]{1,0:T(8,128)(2,1)S(1)}, u32[]{:S(2)}, u32[]{:S(2)}) collective-permute-start(bf16[1024,256]{1,0:T(8,128)(2,1)S(1)} %pad_maximum_fusion.refs_0_), channel_id=1, source_target_pairs={{0,56},{8,0},{16,8},{24,16},{32,24},{40,32},{48,40},{56,48},{1,57}... | collective-permute-start | bytes 1572872 | tf_op jit(solution)/shard_map/ppermute | solution.py:318
  30.4 0.6 pad.40.clone
  31.3 2.7 %collective-permute-start.8 = (bf16[1024,256]{1,0:T(8,128)(2,1)S(1)}, bf16[1024,256]{1,0:T(8,128)(2,1)S(1)}, u32[]{:S(2)}, u32[]{:S(2)}) collective-permute-start(bf16[1024,256]{1,0:T(8,128)(2,1)S(1)} %pad_maximum_fusion.1.refs_1_), channel_id=1, source_target_pairs={{0,56},{8,0},{16,8},{24,16},{32,24},{40,32},{48,40},{56,48},{1,57}... | collective-permute-start | bytes 1572872 | tf_op jit(solution)/shard_map/ppermute | solution.py:318
  34.0 7.0 %collective-permute-done.3.refs_2_ = bf16[1024,256]{1,0:T(8,128)(2,1)S(1)} collective-permute-done((bf16[1024,256]{1,0:T(8,128)(2,1)S(1)}, bf16[1024,256]{1,0:T(8,128)(2,1)S(1)}, u32[]{:S(2)}, u32[]{:S(2)}) %collective-permute-start.3) | collective-permute-done | bytes 524320 | tf_op jit(solution)/shard_map/ppermute | solution.py:318
  41.5 0.5 bitcast_multiply_fusion.4
  42.5 0.7 fusion.23
  43.5 0.2 fusion.24
  44.7 1.0 convolution_bitcast_fusion.4
  45.8 0.2 copy.138
  47.2 0.2 concatenate.55
  47.9 0.2 concatenate.56
  48.5 0.2 concatenate.57
  49.3 2.7 %collective-permute-start.6 = (bf16[1024,256]{1,0:T(8,128)(2,1)S(1)}, bf16[1024,256]{1,0:T(8,128)(2,1)}, u32[]{:S(2)}, u32[]{:S(2)}) collective-permute-start(bf16[1024,256]{1,0:T(8,128)(2,1)S(1)} %collective-permute-done.4.refs_4_), channel_id=1, source_target_pairs={{0,56},{8,0},{16,8},{24,16},{32,24},{40,32},{48,40},{56,48},{1,57}... | collective-permute-start | bytes 1572872 | tf_op jit(solution)/shard_map/ppermute | solution.py:318
  52.0 0.3 collective-permute-done.7.refs_3_
  52.3 2.7 %collective-permute-start.12 = (bf16[1024,256]{1,0:T(8,128)(2,1)S(1)}, bf16[1024,256]{1,0:T(8,128)(2,1)}, u32[]{:S(2)}, u32[]{:S(2)}) collective-permute-start(bf16[1024,256]{1,0:T(8,128)(2,1)S(1)} %collective-permute-done.8.refs_5_), channel_id=1, source_target_pairs={{0,56},{8,0},{16,8},{24,16},{32,24},{40,32},{48,40},{56,48},{1,57}... | collective-permute-start | bytes 1572872 | tf_op jit(solution)/shard_map/ppermute | solution.py:318
  54.9 0.8 fusion.34
  56.1 0.8 fusion.41
  57.0 0.2 multiply_reduce_fusion.power_ref
  57.8 5.4 %fusion.42 = f32[4,1,256,4]{1,2,3,0:T(8,128)} fusion(f32[256,4,4,4]{0,2,3,1:T(4,128)S(1)} %concatenate.57, f32[4,4,1,1]{1,2,3,0:T(1,128)} %bitcast.198), kind=kOutput, calls=%fused_computation.101 | convolution fusion | flops 196608 | bytes 81984 | tf_op jit(solution)/shard_map/ka,jkab->kbj/dot_general | solution.py:56
  63.2 2.2 %copy.182 = f32[4,1,256,4]{2,3,0,1:T(4,128)S(1)} copy(f32[4,1,256,4]{1,2,3,0:T(8,128)} %fusion.42) | data formatting | bytes 32768 | tf_op jit(solution)/shard_map/ka,jkab->kbj/dot_general | solution.py:56
  65.4 1.1 broadcast_bitcast_fusion
  66.5 1.4 collective-permute-start.10
  68.0 4.9 %collective-permute-done.11.refs_7_ = bf16[1024,256]{1,0:T(8,128)(2,1)} collective-permute-done((bf16[1024,256]{1,0:T(8,128)(2,1)S(1)}, bf16[1024,256]{1,0:T(8,128)(2,1)}, u32[]{:S(2)}, u32[]{:S(2)}) %collective-permute-start.11) | collective-permute-done | bytes 524320 | tf_op jit(solution)/shard_map/ppermute | solution.py:318
  72.8 2.5 %collective-permute-start.14 = (bf16[1024,256]{1,0:T(8,128)(2,1)}, bf16[1024,256]{1,0:T(8,128)(2,1)}, u32[]{:S(2)}, u32[]{:S(2)}) collective-permute-start(bf16[1024,256]{1,0:T(8,128)(2,1)} %collective-permute-done.12.refs_9_), channel_id=1, source_target_pairs={{0,56},{8,0},{16,8},{24,16},{32,24},{40,32},{48,40},{56,48},{1,57}... | collective-permute-start | bytes 1572872 | tf_op jit(solution)/shard_map/ppermute | solution.py:318
  75.5 2.1 %copy.191 = bf16[1,4,256,512]{3,1,2,0:T(4,128)(2,1)S(1)} copy(bf16[1,4,256,512]{3,2,1,0:T(8,128)(2,1)} %broadcast_bitcast_fusion) | data formatting | bytes 2097152
  77.6 1.3 slice.132
  79.0 4.1 %reshape.340 = bf16[4,256,511]{2,1,0:T(8,128)(2,1)} reshape(bf16[4,130816]{1,0:T(4,128)(2,1)} %slice.132) | data formatting | bytes 2093056 | tf_op jit(solution)/shard_map/reshape | solution.py:63
  83.0 1.9 %slice.133 = bf16[4,256,256]{2,1,0:T(8,128)(2,1)} slice(bf16[4,256,511]{2,1,0:T(8,128)(2,1)} %reshape.340), slice={[0:4], [0:256], [0:256]} | slice | bytes 1048576 | tf_op jit(solution)/shard_map/slice | solution.py:63
  85.2 0.2 multiply_reduce_fusion.1
  85.5 8.9 %collective-permute-done.14.refs_13_ = bf16[1024,256]{1,0:T(8,128)(2,1)} collective-permute-done((bf16[1024,256]{1,0:T(8,128)(2,1)}, bf16[1024,256]{1,0:T(8,128)(2,1)}, u32[]{:S(2)}, u32[]{:S(2)}) %collective-permute-start.14) | collective-permute-done | bytes 524320 | tf_op jit(solution)/shard_map/ppermute | solution.py:318
  94.4 3.4 %collective-permute-start.15 = (bf16[1024,256]{1,0:T(8,128)(2,1)}, bf16[1024,256]{1,0:T(8,128)(2,1)}, u32[]{:S(2)}, u32[]{:S(2)}) collective-permute-start(bf16[1024,256]{1,0:T(8,128)(2,1)} %collective-permute-done.14.refs_13_), channel_id=1, source_target_pairs={{0,56},{8,0},{16,8},{24,16},{32,24},{40,32},{48,40},{56,48},{1,57}... | collective-permute-start | bytes 1572872 | tf_op jit(solution)/shard_map/ppermute | solution.py:318
  97.8 0.8 copy-done
  98.6 1.0 copy-done.1
  99.6 7.9 %shard_map.64.total_ref = f32[1024,512]{1,0:T(8,128)S(1)} custom-call(s32[9]{0:T(128)S(1)} %stack.92.zs, bf16[4,256,8192]{2,1,0:T(8,128)(2,1)} %bitcast.182, bf16[1024,256]{1,0:T(8,128)(2,1)S(1)} %pad_maximum_fusion.refs_0_, bf16[1024,256]{1,0:T(8,128)(2,1)S(1)} %pad_maximum_fusion.1.refs_1_, bf16[1024,256]{1,0:T(8,128)(2,1)S(1)} %collective-permute-done.3.refs_2_, ...), custom_call_target="tpu_custom_call" | custom-call | flops 4697620480 | bytes 19922944 | tf_op jit(solution)/shard_map/pallas_call | solution.py:160
  107.6 5.0 %collective-permute-done.13.first_ref = bf16[1024,256]{1,0:T(8,128)(2,1)} collective-permute-done((bf16[1024,256]{1,0:T(8,128)(2,1)}, bf16[1024,256]{1,0:T(8,128)(2,1)}, u32[]{:S(2)}, u32[]{:S(2)}) %collective-permute-start.13) | collective-permute-done | bytes 524320 | tf_op jit(solution)/shard_map/ppermute | solution.py:318
  112.5 3.7 %shard_map.65 = (bf16[256,512]{1,0:T(8,128)(2,1)S(1)}, bf16[256,512]{1,0:T(8,128)(2,1)S(1)}, bf16[256,512]{1,0:T(8,128)(2,1)S(1)}, bf16[256,512]{1,0:T(8,128)(2,1)S(1)}, f32[32,4,256]{2,1,0:T(4,128)S(1)}) custom-call(s32[9]{0:T(128)S(1)} %stack.92.zs, bf16[4,256,8192]{2,1,0:T(8,128)(2,1)} %bitcast.183, bf16[1024,256]{1,0:T(8,128)(2,1)} %collective-permute-done.13.first_ref, ...), custom_call_target="tpu_custom_call" | custom-call | flops 738197504 | bytes 6291456 | tf_op jit(solution)/shard_map/pallas_call | solution.py:224
  116.2 0.8 collective-permute-start.17
  117.0 2.0 %collective-permute-start.18 = (bf16[256,512]{1,0:T(8,128)(2,1)S(1)}, bf16[256,512]{1,0:T(8,128)(2,1)S(1)}, u32[]{:S(2)}, u32[]{:S(2)}) collective-permute-start(bf16[256,512]{1,0:T(8,128)(2,1)S(1)} %get-tuple-element.78), channel_id=1, source_target_pairs={{0,128},{64,192},{128,0},{192,64},{1,129},{65,193},{129,1},{193,65... | collective-permute-start | bytes 786440 | tf_op jit(solution)/shard_map/ppermute | solution.py:322
  119.0 1.8 %collective-permute-start.19 = (bf16[256,512]{1,0:T(8,128)(2,1)S(1)}, bf16[256,512]{1,0:T(8,128)(2,1)S(1)}, u32[]{:S(2)}, u32[]{:S(2)}) collective-permute-start(bf16[256,512]{1,0:T(8,128)(2,1)S(1)} %get-tuple-element.79), channel_id=1, source_target_pairs={{0,192},{64,0},{128,64},{192,128},{1,193},{65,1},{129,65},{193,129... | collective-permute-start | bytes 786440 | tf_op jit(solution)/shard_map/ppermute | solution.py:322
  120.8 17.0 %all_to_all.5.slabs_ref = f32[32,4,256]{2,1,0:T(4,128)S(1)} all-to-all(f32[32,4,256]{2,1,0:T(4,128)S(1)} %get-tuple-element.80), channel_id=1, replica_groups=mesh['x'=4,'z'=8,'y'=4,'c'=2] {'y','c','x'}, dimensions={0} | all-to-all | bytes 262144 | tf_op jit(solution)/shard_map/all_to_all | solution.py:381
  137.9 4.6 %shard_map.66 = f32[256,2048]{1,0:T(8,128)} custom-call(s32[2]{0:T(128)S(1)} %pad_add_fusion.place, bf16[256,512]{1,0:T(8,128)(2,1)S(1)} %get-tuple-element.76.own_ref, bf16[256,512]{1,0:T(8,128)(2,1)S(1)} %collective-permute-done.17.by_one_ref, bf16[256,512]{1,0:T(8,128)(2,1)S(1)} %collective-permute-done.18.by_two_ref, ...), custom_call_target="tpu_custom_call" | custom-call | flops 1153433600 | bytes 4194304 | tf_op jit(solution)/shard_map/pallas_call | solution.py:296
  (107 shorter events, 7.0 us)
Async XLA Ops:
  6.5 2.0 %copy-start.3 = (bf16[256,2048]{1,0:T(8,128)(2,1)S(1)}, bf16[256,2048]{1,0:T(8,128)(2,1)}, u32[]{:S(2)}) copy-start(bf16[256,2048]{1,0:T(8,128)(2,1)} %param.7) | copy-start | bytes 3145732
  6.5 92.0 %all-gather.2.cloned.1.call-start = ((), (), s32[]{:S(2)}) async-start(), calls=%async_computation.1 | async-start | bytes 17301504 | tf_op jit(solution)/shard_map/all_gather | solution.py:335
  8.7 7.1 %collective-permute-start = (bf16[256,512]{1,0:T(8,128)(2,1)S(1)}, bf16[256,512]{1,0:T(8,128)(2,1)S(1)}, u32[]{:S(2)}, u32[]{:S(2)}) collective-permute-start(bf16[256,512]{1,0:T(8,128)(2,1)S(1)} %get-tuple-element.100), channel_id=1, source_target_pairs={{0,64},{64,128},{128,192},{192,0},{1,65},{65,129},{129,193},{193,1... | collective-permute-start | bytes 786440 | tf_op jit(solution)/shard_map/ppermute | solution.py:322
  10.8 13.8 %collective-permute-start.1 = (bf16[256,512]{1,0:T(8,128)(2,1)S(1)}, bf16[256,512]{1,0:T(8,128)(2,1)S(1)}, u32[]{:S(2)}, u32[]{:S(2)}) collective-permute-start(bf16[256,512]{1,0:T(8,128)(2,1)S(1)} %get-tuple-element.102), channel_id=1, source_target_pairs={{0,128},{64,192},{128,0},{192,64},{1,129},{65,193},{129,1},{193,65... | collective-permute-start | bytes 786440 | tf_op jit(solution)/shard_map/ppermute | solution.py:322
  13.2 11.3 %collective-permute-start.2 = (bf16[256,512]{1,0:T(8,128)(2,1)S(1)}, bf16[256,512]{1,0:T(8,128)(2,1)S(1)}, u32[]{:S(2)}, u32[]{:S(2)}) collective-permute-start(bf16[256,512]{1,0:T(8,128)(2,1)S(1)} %get-tuple-element.101), channel_id=1, source_target_pairs={{0,192},{64,0},{128,64},{192,128},{1,193},{65,1},{129,65},{193,129... | collective-permute-start | bytes 786440 | tf_op jit(solution)/shard_map/ppermute | solution.py:322
  14.4 26.6 %copy-start.7 = (f32[2,4]{1,0:T(2,128)S(1)}, f32[2,4]{1,0:T(2,128)}, u32[]{:S(2)}) copy-start(f32[2,4]{1,0:T(2,128)} %param.9) | copy-start | bytes 100
  14.4 26.6 %copy-start.6 = (f32[2,4]{1,0:T(2,128)S(1)}, f32[2,4]{1,0:T(2,128)}, u32[]{:S(2)}) copy-start(f32[2,4]{1,0:T(2,128)} %param.10) | copy-start | bytes 100
  14.4 26.8 %copy-start.5 = (f32[4,4]{1,0:T(4,128)S(1)}, f32[4,4]{1,0:T(4,128)}, u32[]{:S(2)}) copy-start(f32[4,4]{1,0:T(4,128)} %param.11) | copy-start | bytes 196
  24.7 16.3 %collective-permute-start.3 = (bf16[1024,256]{1,0:T(8,128)(2,1)S(1)}, bf16[1024,256]{1,0:T(8,128)(2,1)S(1)}, u32[]{:S(2)}, u32[]{:S(2)}) collective-permute-start(bf16[1024,256]{1,0:T(8,128)(2,1)S(1)} %pad_maximum_fusion.refs_0_), channel_id=1, source_target_pairs={{0,8},{8,16},{16,24},{24,32},{32,40},{40,48},{48,56},{56,0},{1,9},... | collective-permute-start | bytes 1572872 | tf_op jit(solution)/shard_map/ppermute | solution.py:318
  26.4 14.6 %collective-permute-start.4 = (bf16[1024,256]{1,0:T(8,128)(2,1)S(1)}, bf16[1024,256]{1,0:T(8,128)(2,1)S(1)}, u32[]{:S(2)}, u32[]{:S(2)}) collective-permute-start(bf16[1024,256]{1,0:T(8,128)(2,1)S(1)} %pad_maximum_fusion.refs_0_), channel_id=1, source_target_pairs={{0,56},{8,0},{16,8},{24,16},{32,24},{40,32},{48,40},{56,48},{1,57}... | collective-permute-start | bytes 1572872 | tf_op jit(solution)/shard_map/ppermute | solution.py:318
  31.0 25.9 %copy-start.4 = (s32[8192]{0:T(1024)S(1)}, s32[8192]{0:T(1024)}, u32[]{:S(2)}) copy-start(s32[8192]{0:T(1024)} %param.8) | copy-start | bytes 98308
  31.2 21.0 %collective-permute-start.7 = (bf16[1024,256]{1,0:T(8,128)(2,1)S(1)}, bf16[1024,256]{1,0:T(8,128)(2,1)S(1)}, u32[]{:S(2)}, u32[]{:S(2)}) collective-permute-start(bf16[1024,256]{1,0:T(8,128)(2,1)S(1)} %pad_maximum_fusion.1.refs_1_), channel_id=1, source_target_pairs={{0,8},{8,16},{16,24},{24,32},{32,40},{40,48},{48,56},{56,0},{1,9},... | collective-permute-start | bytes 1572872 | tf_op jit(solution)/shard_map/ppermute | solution.py:318
  31.3 20.9 %collective-permute-start.8 = (bf16[1024,256]{1,0:T(8,128)(2,1)S(1)}, bf16[1024,256]{1,0:T(8,128)(2,1)S(1)}, u32[]{:S(2)}, u32[]{:S(2)}) collective-permute-start(bf16[1024,256]{1,0:T(8,128)(2,1)S(1)} %pad_maximum_fusion.1.refs_1_), channel_id=1, source_target_pairs={{0,56},{8,0},{16,8},{24,16},{32,24},{40,32},{48,40},{56,48},{1,57}... | collective-permute-start | bytes 1572872 | tf_op jit(solution)/shard_map/ppermute | solution.py:318
  49.2 17.3 %collective-permute-start.5 = (bf16[1024,256]{1,0:T(8,128)(2,1)S(1)}, bf16[1024,256]{1,0:T(8,128)(2,1)}, u32[]{:S(2)}, u32[]{:S(2)}) collective-permute-start(bf16[1024,256]{1,0:T(8,128)(2,1)S(1)} %collective-permute-done.3.refs_2_), channel_id=1, source_target_pairs={{0,8},{8,16},{16,24},{24,32},{32,40},{40,48},{48,56},{56,0},{1,9},... | collective-permute-start | bytes 1572872 | tf_op jit(solution)/shard_map/ppermute | solution.py:318
  49.3 17.2 %collective-permute-start.6 = (bf16[1024,256]{1,0:T(8,128)(2,1)S(1)}, bf16[1024,256]{1,0:T(8,128)(2,1)}, u32[]{:S(2)}, u32[]{:S(2)}) collective-permute-start(bf16[1024,256]{1,0:T(8,128)(2,1)S(1)} %collective-permute-done.4.refs_4_), channel_id=1, source_target_pairs={{0,56},{8,0},{16,8},{24,16},{32,24},{40,32},{48,40},{56,48},{1,57}... | collective-permute-start | bytes 1572872 | tf_op jit(solution)/shard_map/ppermute | solution.py:318
  52.2 20.6 %collective-permute-start.11 = (bf16[1024,256]{1,0:T(8,128)(2,1)S(1)}, bf16[1024,256]{1,0:T(8,128)(2,1)}, u32[]{:S(2)}, u32[]{:S(2)}) collective-permute-start(bf16[1024,256]{1,0:T(8,128)(2,1)S(1)} %collective-permute-done.7.refs_3_), channel_id=1, source_target_pairs={{0,8},{8,16},{16,24},{24,32},{32,40},{40,48},{48,56},{56,0},{1,9},... | collective-permute-start | bytes 1572872 | tf_op jit(solution)/shard_map/ppermute | solution.py:318
  52.3 20.6 %collective-permute-start.12 = (bf16[1024,256]{1,0:T(8,128)(2,1)S(1)}, bf16[1024,256]{1,0:T(8,128)(2,1)}, u32[]{:S(2)}, u32[]{:S(2)}) collective-permute-start(bf16[1024,256]{1,0:T(8,128)(2,1)S(1)} %collective-permute-done.8.refs_5_), channel_id=1, source_target_pairs={{0,56},{8,0},{16,8},{24,16},{32,24},{40,32},{48,40},{56,48},{1,57}... | collective-permute-start | bytes 1572872 | tf_op jit(solution)/shard_map/ppermute | solution.py:318
  66.5 19.0 %collective-permute-start.10 = (bf16[1024,256]{1,0:T(8,128)(2,1)}, bf16[1024,256]{1,0:T(8,128)(2,1)}, u32[]{:S(2)}, u32[]{:S(2)}) collective-permute-start(bf16[1024,256]{1,0:T(8,128)(2,1)} %collective-permute-done.6.refs_8_), channel_id=1, source_target_pairs={{0,56},{8,0},{16,8},{24,16},{32,24},{40,32},{48,40},{56,48},{1,57}... | collective-permute-start | bytes 1572872 | tf_op jit(solution)/shard_map/ppermute | solution.py:318
  67.9 17.6 %collective-permute-start.9 = (bf16[1024,256]{1,0:T(8,128)(2,1)}, bf16[1024,256]{1,0:T(8,128)(2,1)}, u32[]{:S(2)}, u32[]{:S(2)}) collective-permute-start(bf16[1024,256]{1,0:T(8,128)(2,1)} %collective-permute-done.5.refs_6_), channel_id=1, source_target_pairs={{0,8},{8,16},{16,24},{24,32},{32,40},{40,48},{48,56},{56,0},{1,9},... | collective-permute-start | bytes 1572872 | tf_op jit(solution)/shard_map/ppermute | solution.py:318
  72.8 21.5 %collective-permute-start.14 = (bf16[1024,256]{1,0:T(8,128)(2,1)}, bf16[1024,256]{1,0:T(8,128)(2,1)}, u32[]{:S(2)}, u32[]{:S(2)}) collective-permute-start(bf16[1024,256]{1,0:T(8,128)(2,1)} %collective-permute-done.12.refs_9_), channel_id=1, source_target_pairs={{0,56},{8,0},{16,8},{24,16},{32,24},{40,32},{48,40},{56,48},{1,57}... | collective-permute-start | bytes 1572872 | tf_op jit(solution)/shard_map/ppermute | solution.py:318
  85.1 12.7 %collective-permute-start.16 = (bf16[1024,256]{1,0:T(8,128)(2,1)}, bf16[1024,256]{1,0:T(8,128)(2,1)S(1)}, u32[]{:S(2)}, u32[]{:S(2)}) collective-permute-start(bf16[1024,256]{1,0:T(8,128)(2,1)} %collective-permute-done.11.refs_7_), channel_id=1, source_target_pairs={{0,8},{8,16},{16,24},{24,32},{32,40},{40,48},{48,56},{56,0},{1,9},... | collective-permute-start | bytes 1572872 | tf_op jit(solution)/shard_map/ppermute | solution.py:318
  94.4 13.2 %collective-permute-start.15 = (bf16[1024,256]{1,0:T(8,128)(2,1)}, bf16[1024,256]{1,0:T(8,128)(2,1)}, u32[]{:S(2)}, u32[]{:S(2)}) collective-permute-start(bf16[1024,256]{1,0:T(8,128)(2,1)} %collective-permute-done.14.refs_13_), channel_id=1, source_target_pairs={{0,56},{8,0},{16,8},{24,16},{32,24},{40,32},{48,40},{56,48},{1,57}... | collective-permute-start | bytes 1572872 | tf_op jit(solution)/shard_map/ppermute | solution.py:318
  97.8 14.7 %collective-permute-start.13 = (bf16[1024,256]{1,0:T(8,128)(2,1)}, bf16[1024,256]{1,0:T(8,128)(2,1)}, u32[]{:S(2)}, u32[]{:S(2)}) collective-permute-start(bf16[1024,256]{1,0:T(8,128)(2,1)} %collective-permute-done.9.refs_10_), channel_id=1, source_target_pairs={{0,8},{8,16},{16,24},{24,32},{32,40},{40,48},{48,56},{56,0},{1,9},... | collective-permute-start | bytes 1572872 | tf_op jit(solution)/shard_map/ppermute | solution.py:318
  97.8 0.8 copy-start
  98.6 1.0 copy-start.1
  107.5 30.3 %copy-start.2 = (bf16[4,256,256]{2,1,0:T(8,128)(2,1)S(1)}, bf16[4,256,256]{2,1,0:T(8,128)(2,1)}, u32[]{:S(2)}) copy-start(bf16[4,256,256]{2,1,0:T(8,128)(2,1)} %slice.133) | copy-start | bytes 1572868
  116.2 21.6 %collective-permute-start.17 = (bf16[256,512]{1,0:T(8,128)(2,1)S(1)}, bf16[256,512]{1,0:T(8,128)(2,1)S(1)}, u32[]{:S(2)}, u32[]{:S(2)}) collective-permute-start(bf16[256,512]{1,0:T(8,128)(2,1)S(1)} %get-tuple-element.77), channel_id=1, source_target_pairs={{0,64},{64,128},{128,192},{192,0},{1,65},{65,129},{129,193},{193,1... | collective-permute-start | bytes 786440 | tf_op jit(solution)/shard_map/ppermute | solution.py:322
  117.0 20.8 %collective-permute-start.18 = (bf16[256,512]{1,0:T(8,128)(2,1)S(1)}, bf16[256,512]{1,0:T(8,128)(2,1)S(1)}, u32[]{:S(2)}, u32[]{:S(2)}) collective-permute-start(bf16[256,512]{1,0:T(8,128)(2,1)S(1)} %get-tuple-element.78), channel_id=1, source_target_pairs={{0,128},{64,192},{128,0},{192,64},{1,129},{65,193},{129,1},{193,65... | collective-permute-start | bytes 786440 | tf_op jit(solution)/shard_map/ppermute | solution.py:322
  119.0 18.8 %collective-permute-start.19 = (bf16[256,512]{1,0:T(8,128)(2,1)S(1)}, bf16[256,512]{1,0:T(8,128)(2,1)S(1)}, u32[]{:S(2)}, u32[]{:S(2)}) collective-permute-start(bf16[256,512]{1,0:T(8,128)(2,1)S(1)} %get-tuple-element.79), channel_id=1, source_target_pairs={{0,192},{64,0},{128,64},{192,128},{1,193},{65,1},{129,65},{193,129... | collective-permute-start | bytes 786440 | tf_op jit(solution)/shard_map/ppermute | solution.py:322
Sparse Core Ops, SparseCore 0:
  9.9 81.7 all-gather.1

commit v7 on v6

--- a/solution.py
+++ b/solution.py
@@ -340,14 +340,14 @@
         return lax.dynamic_slice(white_noise, (0, first), (ROWS, SLAB))
 
     parts = [cut(0)] + [round_x(cut(d), d) for d in (1, 2, 3)]
+    site_class, site_decay, site_angle, site_mix, *parts[1:] = lax.optimization_barrier(
+        (site_class, site_decay, site_angle, site_mix, *parts[1:])
+    )
     steps = []
     for half in range(2):
         start = jnp.concatenate([p[:, half * CH : (half + 1) * CH] for p in parts], axis=0)
         steps.append([start, ring(start, 1), ring(start, -1)])
     first, second = steps
-    site_class, site_decay, site_angle, site_mix, *first[1:] = lax.optimization_barrier(
-        (site_class, site_decay, site_angle, site_mix, *first[1:])
-    )
     for _ in range(2):
         first += [ring(first[-2], 1), ring(first[-1], -1)]
         second[-2:], first[-4:-2] = together(second[-2:], first[-4:-2])

time: 150 us -> 155 us (1.033)
  starting transfers between devices: 31.6 us -> 35.3 us
  blocking collectives: 17 us -> 18.7 us
    ppermute x6, starting transfers between devices: 10.4 us -> 13 us  [round_x(): return lax.ppermute(value, 'x', [(i, (i + by) % NX) for i in range(NX)])]
    all_to_all x1, blocking collectives: 17 us -> 18.7 us  [body(): own_ends = lax.all_to_all(to_send, ('y', 'c', 'x'), 0, 0, tiled=True)]
  transfers between devices with their start and end apart: 21 -> 21, of which waited for: 7 -> 7; matrix products, arithmetic and copies ran while one was open for 21% -> 20% of each run, Pallas kernels for 5% -> 5%
where the time goes in v7:
time: 155 us; the launch traced here: 154 us
  waiting for transfers between devices  36.2 us (23%)
  starting transfers between devices  35.3 us (23%)
  local copies, waits for them, and re-layouts  22.2 us (14%)
  blocking collectives  18.7 us (12%)
  Pallas kernels  16.2 us (10%)
  between operations  13.8 us (9%)
  matrix products  9.07 us (6%)
  other arithmetic  3 us (2%)
    ppermute x14, waiting for transfers between devices, ring(): return lax.ppermute(value, 'z', [(i, (i + by) % NZ) for i in range(NZ)])  26.7 us
    ppermute x14, starting transfers between devices, ring(): return lax.ppermute(value, 'z', [(i, (i + by) % NZ) for i in range(NZ)])  22.3 us
    all_to_all x1, blocking collectives, body(): own_ends = lax.all_to_all(to_send, ('y', 'c', 'x'), 0, 0, tiled=True)  18.7 us
    ppermute x6, starting transfers between devices, round_x(): return lax.ppermute(value, 'x', [(i, (i + by) % NX) for i in range(NX)])  13 us
    ppermute x6, waiting for transfers between devices, round_x(): return lax.ppermute(value, 'x', [(i, (i + by) % NX) for i in range(NX)])  9.47 us
    pallas_call x1, Pallas kernels, product(): pl.pallas_call(product_kernel, grid_spec=pltpu.PrefetchScalarGridSpec(num...  7.91 us
    dot_general x1, matrix products, tables(): gains = jnp.einsum('ka,jkab->kbj', readout, powers, precision=PRECISE)  5.44 us
    unnamed x19, local copies, waits for them, and re-layouts  5.06 us
  transfers between devices with their start and end apart: 21, of which 7 were waited for; matrix products, arithmetic and copies ran while one was open for 20% of the time, Pallas kernels for 5%

profile of v7, /device:TPU:1, one launch (start us, length us, event | category | flops | bytes accessed | tf_op | source)
XLA Modules:
  0.0 154.5 jit_solution(15548522222529445542)
XLA Ops:
  6.5 2.0 %constant_dynamic-slice_fusion.1 = bf16[32,8192]{1,0:T(8,128)(2,1)} fusion(bf16[256,8192]{1,0:T(8,128)(2,1)} %param.6, s32[]{:T(128)S(6)} %select_n.71), kind=kLoop, calls=%fused_computation.62 | loop fusion | bytes 1048580 | tf_op jit(solution)/shard_map/dynamic_slice | solution.py:334
  8.7 2.1 %collective-permute-start = (bf16[256,512]{1,0:T(8,128)(2,1)S(1)}, bf16[256,512]{1,0:T(8,128)(2,1)S(1)}, u32[]{:S(2)}, u32[]{:S(2)}) collective-permute-start(bf16[256,512]{1,0:T(8,128)(2,1)S(1)} %get-tuple-element.104), channel_id=1, source_target_pairs={{0,64},{64,128},{128,192},{192,0},{1,65},{65,129},{129,193},{193,1... | collective-permute-start | bytes 786440 | tf_op jit(solution)/shard_map/ppermute | solution.py:322
  10.8 2.5 %collective-permute-start.1 = (bf16[256,512]{1,0:T(8,128)(2,1)S(1)}, bf16[256,512]{1,0:T(8,128)(2,1)S(1)}, u32[]{:S(2)}, u32[]{:S(2)}) collective-permute-start(bf16[256,512]{1,0:T(8,128)(2,1)S(1)} %get-tuple-element.103), channel_id=1, source_target_pairs={{0,128},{64,192},{128,0},{192,64},{1,129},{65,193},{129,1},{193,65... | collective-permute-start | bytes 786440 | tf_op jit(solution)/shard_map/ppermute | solution.py:322
  13.2 1.2 collective-permute-start.2
  14.4 0.5 pad.44.clone
  15.1 0.7 collective-permute-done
  15.8 8.7 %collective-permute-done.1 = bf16[256,512]{1,0:T(8,128)(2,1)S(1)} collective-permute-done((bf16[256,512]{1,0:T(8,128)(2,1)S(1)}, bf16[256,512]{1,0:T(8,128)(2,1)S(1)}, u32[]{:S(2)}, u32[]{:S(2)}) %collective-permute-start.1) | collective-permute-done | bytes 262176 | tf_op jit(solution)/shard_map/ppermute | solution.py:322
  24.7 1.7 %collective-permute-start.3 = (bf16[1024,256]{1,0:T(8,128)(2,1)S(1)}, bf16[1024,256]{1,0:T(8,128)(2,1)S(1)}, u32[]{:S(2)}, u32[]{:S(2)}) collective-permute-start(bf16[1024,256]{1,0:T(8,128)(2,1)S(1)} %pad_maximum_fusion.refs_0_), channel_id=1, source_target_pairs={{0,8},{8,16},{16,24},{24,32},{32,40},{40,48},{48,56},{56,0},{1,9},... | collective-permute-start | bytes 1572872 | tf_op jit(solution)/shard_map/ppermute | solution.py:318
  26.4 4.0 %collective-permute-start.5 = (bf16[1024,256]{1,0:T(8,128)(2,1)S(1)}, bf16[1024,256]{1,0:T(8,128)(2,1)S(1)}, u32[]{:S(2)}, u32[]{:S(2)}) collective-permute-start(bf16[1024,256]{1,0:T(8,128)(2,1)S(1)} %pad_maximum_fusion.refs_0_), channel_id=1, source_target_pairs={{0,56},{8,0},{16,8},{24,16},{32,24},{40,32},{48,40},{56,48},{1,57}... | collective-permute-start | bytes 1572872 | tf_op jit(solution)/shard_map/ppermute | solution.py:318
  30.6 2.7 %collective-permute-start.8 = (bf16[1024,256]{1,0:T(8,128)(2,1)S(1)}, bf16[1024,256]{1,0:T(8,128)(2,1)S(1)}, u32[]{:S(2)}, u32[]{:S(2)}) collective-permute-start(bf16[1024,256]{1,0:T(8,128)(2,1)S(1)} %pad_maximum_fusion.1.refs_1_), channel_id=1, source_target_pairs={{0,56},{8,0},{16,8},{24,16},{32,24},{40,32},{48,40},{56,48},{1,57}... | collective-permute-start | bytes 1572872 | tf_op jit(solution)/shard_map/ppermute | solution.py:318
  33.7 0.5 bitcast_multiply_fusion.4
  34.7 0.7 fusion.23
  35.7 0.2 fusion.24
  35.9 0.2 copy.155
  36.9 1.0 convolution_bitcast_fusion.4
  38.0 0.2 copy.138
  39.4 0.2 concatenate.54
  40.1 0.2 concatenate.55
  40.7 0.2 concatenate.56
  41.5 0.7 fusion.34
  42.8 0.8 fusion.41
  43.8 0.2 multiply_reduce_fusion.power_ref
  44.2 5.4 %fusion.42 = f32[4,1,256,4]{1,2,3,0:T(8,128)} fusion(f32[256,4,4,4]{0,2,3,1:T(4,128)S(1)} %concatenate.56, f32[4,4,1,1]{1,2,3,0:T(1,128)} %bitcast.198), kind=kOutput, calls=%fused_computation.101 | convolution fusion | flops 196608 | bytes 81984 | tf_op jit(solution)/shard_map/ka,jkab->kbj/dot_general | solution.py:56
  49.7 2.6 %collective-permute-done.7.refs_3_ = bf16[1024,256]{1,0:T(8,128)(2,1)S(1)} collective-permute-done((bf16[1024,256]{1,0:T(8,128)(2,1)S(1)}, bf16[1024,256]{1,0:T(8,128)(2,1)S(1)}, u32[]{:S(2)}, u32[]{:S(2)}) %collective-permute-start.7) | collective-permute-done | bytes 524320 | tf_op jit(solution)/shard_map/ppermute | solution.py:318
  52.3 2.7 %collective-permute-start.12 = (bf16[1024,256]{1,0:T(8,128)(2,1)S(1)}, bf16[1024,256]{1,0:T(8,128)(2,1)}, u32[]{:S(2)}, u32[]{:S(2)}) collective-permute-start(bf16[1024,256]{1,0:T(8,128)(2,1)S(1)} %collective-permute-done.8.refs_5_), channel_id=1, source_target_pairs={{0,56},{8,0},{16,8},{24,16},{32,24},{40,32},{48,40},{56,48},{1,57}... | collective-permute-start | bytes 1572872 | tf_op jit(solution)/shard_map/ppermute | solution.py:318
  55.0 2.7 %collective-permute-start.6 = (bf16[1024,256]{1,0:T(8,128)(2,1)S(1)}, bf16[1024,256]{1,0:T(8,128)(2,1)}, u32[]{:S(2)}, u32[]{:S(2)}) collective-permute-start(bf16[1024,256]{1,0:T(8,128)(2,1)S(1)} %collective-permute-done.5.refs_4_), channel_id=1, source_target_pairs={{0,56},{8,0},{16,8},{24,16},{32,24},{40,32},{48,40},{56,48},{1,57}... | collective-permute-start | bytes 1572872 | tf_op jit(solution)/shard_map/ppermute | solution.py:318
  57.6 2.2 %copy.182 = f32[4,1,256,4]{2,3,0,1:T(4,128)S(1)} copy(f32[4,1,256,4]{1,2,3,0:T(8,128)} %fusion.42) | data formatting | bytes 32768 | tf_op jit(solution)/shard_map/ka,jkab->kbj/dot_general | solution.py:56
  59.9 1.1 broadcast_bitcast_fusion
  60.9 15.1 %collective-permute-done.4.refs_6_ = bf16[1024,256]{1,0:T(8,128)(2,1)} collective-permute-done((bf16[1024,256]{1,0:T(8,128)(2,1)S(1)}, bf16[1024,256]{1,0:T(8,128)(2,1)}, u32[]{:S(2)}, u32[]{:S(2)}) %collective-permute-start.4) | collective-permute-done | bytes 524320 | tf_op jit(solution)/shard_map/ppermute | solution.py:318
  76.1 2.4 %collective-permute-start.10 = (bf16[1024,256]{1,0:T(8,128)(2,1)}, bf16[1024,256]{1,0:T(8,128)(2,1)}, u32[]{:S(2)}, u32[]{:S(2)}) collective-permute-start(bf16[1024,256]{1,0:T(8,128)(2,1)} %collective-permute-done.6.refs_8_), channel_id=1, source_target_pairs={{0,56},{8,0},{16,8},{24,16},{32,24},{40,32},{48,40},{56,48},{1,57}... | collective-permute-start | bytes 1572872 | tf_op jit(solution)/shard_map/ppermute | solution.py:318
  78.5 2.7 %collective-permute-start.14 = (bf16[1024,256]{1,0:T(8,128)(2,1)}, bf16[1024,256]{1,0:T(8,128)(2,1)}, u32[]{:S(2)}, u32[]{:S(2)}) collective-permute-start(bf16[1024,256]{1,0:T(8,128)(2,1)} %collective-permute-done.12.refs_9_), channel_id=1, source_target_pairs={{0,56},{8,0},{16,8},{24,16},{32,24},{40,32},{48,40},{56,48},{1,57}... | collective-permute-start | bytes 1572872 | tf_op jit(solution)/shard_map/ppermute | solution.py:318
  81.3 2.0 %copy.191 = bf16[1,4,256,512]{3,1,2,0:T(4,128)(2,1)S(1)} copy(bf16[1,4,256,512]{3,2,1,0:T(8,128)(2,1)} %broadcast_bitcast_fusion) | data formatting | bytes 2097152
  83.4 1.4 slice.129
  84.7 4.0 %reshape.340 = bf16[4,256,511]{2,1,0:T(8,128)(2,1)} reshape(bf16[4,130816]{1,0:T(4,128)(2,1)} %slice.129) | data formatting | bytes 2093056 | tf_op jit(solution)/shard_map/reshape | solution.py:63
  88.8 1.9 %slice.130 = bf16[4,256,256]{2,1,0:T(8,128)(2,1)} slice(bf16[4,256,511]{2,1,0:T(8,128)(2,1)} %reshape.340), slice={[0:4], [0:256], [0:256]} | slice | bytes 1048576 | tf_op jit(solution)/shard_map/slice | solution.py:63
  90.9 0.2 multiply_reduce_fusion.1
  91.2 6.6 %collective-permute-done.14.refs_13_ = bf16[1024,256]{1,0:T(8,128)(2,1)} collective-permute-done((bf16[1024,256]{1,0:T(8,128)(2,1)}, bf16[1024,256]{1,0:T(8,128)(2,1)}, u32[]{:S(2)}, u32[]{:S(2)}) %collective-permute-start.14) | collective-permute-done | bytes 524320 | tf_op jit(solution)/shard_map/ppermute | solution.py:318
  97.9 3.4 %collective-permute-start.15 = (bf16[1024,256]{1,0:T(8,128)(2,1)}, bf16[1024,256]{1,0:T(8,128)(2,1)}, u32[]{:S(2)}, u32[]{:S(2)}) collective-permute-start(bf16[1024,256]{1,0:T(8,128)(2,1)} %collective-permute-done.14.refs_13_), channel_id=1, source_target_pairs={{0,56},{8,0},{16,8},{24,16},{32,24},{40,32},{48,40},{56,48},{1,57}... | collective-permute-start | bytes 1572872 | tf_op jit(solution)/shard_map/ppermute | solution.py:318
  101.2 0.3 collective-permute-done.16.refs_11_
  101.5 0.8 copy-done
  102.3 1.0 copy-done.1
  103.3 7.9 %shard_map.64.total_ref = f32[1024,512]{1,0:T(8,128)S(1)} custom-call(s32[9]{0:T(128)S(1)} %stack.92.zs, bf16[4,256,8192]{2,1,0:T(8,128)(2,1)} %bitcast.182, bf16[1024,256]{1,0:T(8,128)(2,1)S(1)} %pad_maximum_fusion.refs_0_, bf16[1024,256]{1,0:T(8,128)(2,1)S(1)} %pad_maximum_fusion.1.refs_1_, bf16[1024,256]{1,0:T(8,128)(2,1)S(1)} %collective-permute-done.3.refs_2_, ...), custom_call_target="tpu_custom_call" | custom-call | flops 4697620480 | bytes 19922944 | tf_op jit(solution)/shard_map/pallas_call | solution.py:160
  111.3 2.1 %collective-permute-done.13.first_ref = bf16[1024,256]{1,0:T(8,128)(2,1)} collective-permute-done((bf16[1024,256]{1,0:T(8,128)(2,1)}, bf16[1024,256]{1,0:T(8,128)(2,1)}, u32[]{:S(2)}, u32[]{:S(2)}) %collective-permute-start.13) | collective-permute-done | bytes 524320 | tf_op jit(solution)/shard_map/ppermute | solution.py:318
  113.3 3.7 %shard_map.65 = (bf16[256,512]{1,0:T(8,128)(2,1)S(1)}, bf16[256,512]{1,0:T(8,128)(2,1)S(1)}, bf16[256,512]{1,0:T(8,128)(2,1)S(1)}, bf16[256,512]{1,0:T(8,128)(2,1)S(1)}, f32[32,4,256]{2,1,0:T(4,128)S(1)}) custom-call(s32[9]{0:T(128)S(1)} %stack.92.zs, bf16[4,256,8192]{2,1,0:T(8,128)(2,1)} %bitcast.183, bf16[1024,256]{1,0:T(8,128)(2,1)} %collective-permute-done.13.first_ref, ...), custom_call_target="tpu_custom_call" | custom-call | flops 738197504 | bytes 6291456 | tf_op jit(solution)/shard_map/pallas_call | solution.py:224
  117.0 2.3 %collective-permute-start.17 = (bf16[256,512]{1,0:T(8,128)(2,1)S(1)}, bf16[256,512]{1,0:T(8,128)(2,1)S(1)}, u32[]{:S(2)}, u32[]{:S(2)}) collective-permute-start(bf16[256,512]{1,0:T(8,128)(2,1)S(1)} %get-tuple-element.79), channel_id=1, source_target_pairs={{0,64},{64,128},{128,192},{192,0},{1,65},{65,129},{129,193},{193,1... | collective-permute-start | bytes 786440 | tf_op jit(solution)/shard_map/ppermute | solution.py:322
  119.3 4.9 %collective-permute-start.18 = (bf16[256,512]{1,0:T(8,128)(2,1)S(1)}, bf16[256,512]{1,0:T(8,128)(2,1)S(1)}, u32[]{:S(2)}, u32[]{:S(2)}) collective-permute-start(bf16[256,512]{1,0:T(8,128)(2,1)S(1)} %get-tuple-element.80), channel_id=1, source_target_pairs={{0,128},{64,192},{128,0},{192,64},{1,129},{65,193},{129,1},{193,65... | collective-permute-start | bytes 786440 | tf_op jit(solution)/shard_map/ppermute | solution.py:322
  124.3 18.7 %all_to_all.5.slabs_ref = f32[32,4,256]{2,1,0:T(4,128)S(1)} all-to-all(f32[32,4,256]{2,1,0:T(4,128)S(1)} %get-tuple-element.82), channel_id=1, replica_groups=mesh['x'=4,'z'=8,'y'=4,'c'=2] {'y','c','x'}, dimensions={0} | all-to-all | bytes 262144 | tf_op jit(solution)/shard_map/all_to_all | solution.py:381
  143.0 4.6 %shard_map.66 = f32[256,2048]{1,0:T(8,128)} custom-call(s32[2]{0:T(128)S(1)} %pad_add_fusion.place, bf16[256,512]{1,0:T(8,128)(2,1)S(1)} %get-tuple-element.78.own_ref, bf16[256,512]{1,0:T(8,128)(2,1)S(1)} %collective-permute-done.17.by_one_ref, bf16[256,512]{1,0:T(8,128)(2,1)S(1)} %collective-permute-done.18.by_two_ref, ...), custom_call_target="tpu_custom_call" | custom-call | flops 1153433600 | bytes 4194304 | tf_op jit(solution)/shard_map/pallas_call | solution.py:296
  (106 shorter events, 6.6 us)
Async XLA Ops:
  6.5 2.0 %copy-start.3 = (bf16[256,2048]{1,0:T(8,128)(2,1)S(1)}, bf16[256,2048]{1,0:T(8,128)(2,1)}, u32[]{:S(2)}) copy-start(bf16[256,2048]{1,0:T(8,128)(2,1)} %param.7) | copy-start | bytes 3145732
  6.5 95.8 %all-gather.2.cloned.1.call-start = ((), (), s32[]{:S(2)}) async-start(), calls=%async_computation.1 | async-start | bytes 17301504 | tf_op jit(solution)/shard_map/all_gather | solution.py:335
  8.7 7.1 %collective-permute-start = (bf16[256,512]{1,0:T(8,128)(2,1)S(1)}, bf16[256,512]{1,0:T(8,128)(2,1)S(1)}, u32[]{:S(2)}, u32[]{:S(2)}) collective-permute-start(bf16[256,512]{1,0:T(8,128)(2,1)S(1)} %get-tuple-element.104), channel_id=1, source_target_pairs={{0,64},{64,128},{128,192},{192,0},{1,65},{65,129},{129,193},{193,1... | collective-permute-start | bytes 786440 | tf_op jit(solution)/shard_map/ppermute | solution.py:322
  10.8 13.8 %collective-permute-start.1 = (bf16[256,512]{1,0:T(8,128)(2,1)S(1)}, bf16[256,512]{1,0:T(8,128)(2,1)S(1)}, u32[]{:S(2)}, u32[]{:S(2)}) collective-permute-start(bf16[256,512]{1,0:T(8,128)(2,1)S(1)} %get-tuple-element.103), channel_id=1, source_target_pairs={{0,128},{64,192},{128,0},{192,64},{1,129},{65,193},{129,1},{193,65... | collective-permute-start | bytes 786440 | tf_op jit(solution)/shard_map/ppermute | solution.py:322
  13.2 11.3 %collective-permute-start.2 = (bf16[256,512]{1,0:T(8,128)(2,1)S(1)}, bf16[256,512]{1,0:T(8,128)(2,1)S(1)}, u32[]{:S(2)}, u32[]{:S(2)}) collective-permute-start(bf16[256,512]{1,0:T(8,128)(2,1)S(1)} %get-tuple-element.102), channel_id=1, source_target_pairs={{0,192},{64,0},{128,64},{192,128},{1,193},{65,1},{129,65},{193,129... | collective-permute-start | bytes 786440 | tf_op jit(solution)/shard_map/ppermute | solution.py:322
  15.1 18.2 %copy-start.7 = (f32[2,4]{1,0:T(2,128)S(1)}, f32[2,4]{1,0:T(2,128)}, u32[]{:S(2)}) copy-start(f32[2,4]{1,0:T(2,128)} %param.9) | copy-start | bytes 100
  15.1 18.2 %copy-start.6 = (f32[2,4]{1,0:T(2,128)S(1)}, f32[2,4]{1,0:T(2,128)}, u32[]{:S(2)}) copy-start(f32[2,4]{1,0:T(2,128)} %param.10) | copy-start | bytes 100
  15.1 18.3 %copy-start.5 = (f32[4,4]{1,0:T(4,128)S(1)}, f32[4,4]{1,0:T(4,128)}, u32[]{:S(2)}) copy-start(f32[4,4]{1,0:T(4,128)} %param.11) | copy-start | bytes 196
  24.7 17.7 %copy-start.4 = (s32[8192]{0:T(1024)S(1)}, s32[8192]{0:T(1024)}, u32[]{:S(2)}) copy-start(s32[8192]{0:T(1024)} %param.8) | copy-start | bytes 98308
  24.7 25.0 %collective-permute-start.3 = (bf16[1024,256]{1,0:T(8,128)(2,1)S(1)}, bf16[1024,256]{1,0:T(8,128)(2,1)S(1)}, u32[]{:S(2)}, u32[]{:S(2)}) collective-permute-start(bf16[1024,256]{1,0:T(8,128)(2,1)S(1)} %pad_maximum_fusion.refs_0_), channel_id=1, source_target_pairs={{0,8},{8,16},{16,24},{24,32},{32,40},{40,48},{48,56},{56,0},{1,9},... | collective-permute-start | bytes 1572872 | tf_op jit(solution)/shard_map/ppermute | solution.py:318
  26.4 23.2 %collective-permute-start.5 = (bf16[1024,256]{1,0:T(8,128)(2,1)S(1)}, bf16[1024,256]{1,0:T(8,128)(2,1)S(1)}, u32[]{:S(2)}, u32[]{:S(2)}) collective-permute-start(bf16[1024,256]{1,0:T(8,128)(2,1)S(1)} %pad_maximum_fusion.refs_0_), channel_id=1, source_target_pairs={{0,56},{8,0},{16,8},{24,16},{32,24},{40,32},{48,40},{56,48},{1,57}... | collective-permute-start | bytes 1572872 | tf_op jit(solution)/shard_map/ppermute | solution.py:318
  30.5 21.8 %collective-permute-start.7 = (bf16[1024,256]{1,0:T(8,128)(2,1)S(1)}, bf16[1024,256]{1,0:T(8,128)(2,1)S(1)}, u32[]{:S(2)}, u32[]{:S(2)}) collective-permute-start(bf16[1024,256]{1,0:T(8,128)(2,1)S(1)} %pad_maximum_fusion.1.refs_1_), channel_id=1, source_target_pairs={{0,8},{8,16},{16,24},{24,32},{32,40},{40,48},{48,56},{56,0},{1,9},... | collective-permute-start | bytes 1572872 | tf_op jit(solution)/shard_map/ppermute | solution.py:318
  30.6 21.7 %collective-permute-start.8 = (bf16[1024,256]{1,0:T(8,128)(2,1)S(1)}, bf16[1024,256]{1,0:T(8,128)(2,1)S(1)}, u32[]{:S(2)}, u32[]{:S(2)}) collective-permute-start(bf16[1024,256]{1,0:T(8,128)(2,1)S(1)} %pad_maximum_fusion.1.refs_1_), channel_id=1, source_target_pairs={{0,56},{8,0},{16,8},{24,16},{32,24},{40,32},{48,40},{56,48},{1,57}... | collective-permute-start | bytes 1572872 | tf_op jit(solution)/shard_map/ppermute | solution.py:318
  52.3 26.2 %collective-permute-start.11 = (bf16[1024,256]{1,0:T(8,128)(2,1)S(1)}, bf16[1024,256]{1,0:T(8,128)(2,1)}, u32[]{:S(2)}, u32[]{:S(2)}) collective-permute-start(bf16[1024,256]{1,0:T(8,128)(2,1)S(1)} %collective-permute-done.7.refs_3_), channel_id=1, source_target_pairs={{0,8},{8,16},{16,24},{24,32},{32,40},{40,48},{48,56},{56,0},{1,9},... | collective-permute-start | bytes 1572872 | tf_op jit(solution)/shard_map/ppermute | solution.py:318
  52.3 26.2 %collective-permute-start.12 = (bf16[1024,256]{1,0:T(8,128)(2,1)S(1)}, bf16[1024,256]{1,0:T(8,128)(2,1)}, u32[]{:S(2)}, u32[]{:S(2)}) collective-permute-start(bf16[1024,256]{1,0:T(8,128)(2,1)S(1)} %collective-permute-done.8.refs_5_), channel_id=1, source_target_pairs={{0,56},{8,0},{16,8},{24,16},{32,24},{40,32},{48,40},{56,48},{1,57}... | collective-permute-start | bytes 1572872 | tf_op jit(solution)/shard_map/ppermute | solution.py:318
  55.0 21.1 %collective-permute-start.4 = (bf16[1024,256]{1,0:T(8,128)(2,1)S(1)}, bf16[1024,256]{1,0:T(8,128)(2,1)}, u32[]{:S(2)}, u32[]{:S(2)}) collective-permute-start(bf16[1024,256]{1,0:T(8,128)(2,1)S(1)} %collective-permute-done.3.refs_2_), channel_id=1, source_target_pairs={{0,8},{8,16},{16,24},{24,32},{32,40},{40,48},{48,56},{56,0},{1,9},... | collective-permute-start | bytes 1572872 | tf_op jit(solution)/shard_map/ppermute | solution.py:318
  55.0 21.1 %collective-permute-start.6 = (bf16[1024,256]{1,0:T(8,128)(2,1)S(1)}, bf16[1024,256]{1,0:T(8,128)(2,1)}, u32[]{:S(2)}, u32[]{:S(2)}) collective-permute-start(bf16[1024,256]{1,0:T(8,128)(2,1)S(1)} %collective-permute-done.5.refs_4_), channel_id=1, source_target_pairs={{0,56},{8,0},{16,8},{24,16},{32,24},{40,32},{48,40},{56,48},{1,57}... | collective-permute-start | bytes 1572872 | tf_op jit(solution)/shard_map/ppermute | solution.py:318
  76.1 15.2 %collective-permute-start.10 = (bf16[1024,256]{1,0:T(8,128)(2,1)}, bf16[1024,256]{1,0:T(8,128)(2,1)}, u32[]{:S(2)}, u32[]{:S(2)}) collective-permute-start(bf16[1024,256]{1,0:T(8,128)(2,1)} %collective-permute-done.6.refs_8_), channel_id=1, source_target_pairs={{0,56},{8,0},{16,8},{24,16},{32,24},{40,32},{48,40},{56,48},{1,57}... | collective-permute-start | bytes 1572872 | tf_op jit(solution)/shard_map/ppermute | solution.py:318
  78.5 12.8 %collective-permute-start.9 = (bf16[1024,256]{1,0:T(8,128)(2,1)}, bf16[1024,256]{1,0:T(8,128)(2,1)}, u32[]{:S(2)}, u32[]{:S(2)}) collective-permute-start(bf16[1024,256]{1,0:T(8,128)(2,1)} %collective-permute-done.4.refs_6_), channel_id=1, source_target_pairs={{0,8},{8,16},{16,24},{24,32},{32,40},{40,48},{48,56},{56,0},{1,9},... | collective-permute-start | bytes 1572872 | tf_op jit(solution)/shard_map/ppermute | solution.py:318
  78.5 19.4 %collective-permute-start.14 = (bf16[1024,256]{1,0:T(8,128)(2,1)}, bf16[1024,256]{1,0:T(8,128)(2,1)}, u32[]{:S(2)}, u32[]{:S(2)}) collective-permute-start(bf16[1024,256]{1,0:T(8,128)(2,1)} %collective-permute-done.12.refs_9_), channel_id=1, source_target_pairs={{0,56},{8,0},{16,8},{24,16},{32,24},{40,32},{48,40},{56,48},{1,57}... | collective-permute-start | bytes 1572872 | tf_op jit(solution)/shard_map/ppermute | solution.py:318
  90.9 10.6 %collective-permute-start.16 = (bf16[1024,256]{1,0:T(8,128)(2,1)}, bf16[1024,256]{1,0:T(8,128)(2,1)S(1)}, u32[]{:S(2)}, u32[]{:S(2)}) collective-permute-start(bf16[1024,256]{1,0:T(8,128)(2,1)} %collective-permute-done.11.refs_7_), channel_id=1, source_target_pairs={{0,8},{8,16},{16,24},{24,32},{32,40},{40,48},{48,56},{56,0},{1,9},... | collective-permute-start | bytes 1572872 | tf_op jit(solution)/shard_map/ppermute | solution.py:318
  97.9 13.4 %collective-permute-start.15 = (bf16[1024,256]{1,0:T(8,128)(2,1)}, bf16[1024,256]{1,0:T(8,128)(2,1)}, u32[]{:S(2)}, u32[]{:S(2)}) collective-permute-start(bf16[1024,256]{1,0:T(8,128)(2,1)} %collective-permute-done.14.refs_13_), channel_id=1, source_target_pairs={{0,56},{8,0},{16,8},{24,16},{32,24},{40,32},{48,40},{56,48},{1,57}... | collective-permute-start | bytes 1572872 | tf_op jit(solution)/shard_map/ppermute | solution.py:318
  101.2 12.1 %collective-permute-start.13 = (bf16[1024,256]{1,0:T(8,128)(2,1)}, bf16[1024,256]{1,0:T(8,128)(2,1)}, u32[]{:S(2)}, u32[]{:S(2)}) collective-permute-start(bf16[1024,256]{1,0:T(8,128)(2,1)} %collective-permute-done.9.refs_10_), channel_id=1, source_target_pairs={{0,8},{8,16},{16,24},{24,32},{32,40},{40,48},{48,56},{56,0},{1,9},... | collective-permute-start | bytes 1572872 | tf_op jit(solution)/shard_map/ppermute | solution.py:318
  101.5 0.8 copy-start
  102.3 1.0 copy-start.1
  111.3 31.7 %copy-start.2 = (bf16[4,256,256]{2,1,0:T(8,128)(2,1)S(1)}, bf16[4,256,256]{2,1,0:T(8,128)(2,1)}, u32[]{:S(2)}) copy-start(bf16[4,256,256]{2,1,0:T(8,128)(2,1)} %slice.130) | copy-start | bytes 1572868
  117.0 25.9 %collective-permute-start.17 = (bf16[256,512]{1,0:T(8,128)(2,1)S(1)}, bf16[256,512]{1,0:T(8,128)(2,1)S(1)}, u32[]{:S(2)}, u32[]{:S(2)}) collective-permute-start(bf16[256,512]{1,0:T(8,128)(2,1)S(1)} %get-tuple-element.79), channel_id=1, source_target_pairs={{0,64},{64,128},{128,192},{192,0},{1,65},{65,129},{129,193},{193,1... | collective-permute-start | bytes 786440 | tf_op jit(solution)/shard_map/ppermute | solution.py:322
  119.3 23.6 %collective-permute-start.18 = (bf16[256,512]{1,0:T(8,128)(2,1)S(1)}, bf16[256,512]{1,0:T(8,128)(2,1)S(1)}, u32[]{:S(2)}, u32[]{:S(2)}) collective-permute-start(bf16[256,512]{1,0:T(8,128)(2,1)S(1)} %get-tuple-element.80), channel_id=1, source_target_pairs={{0,128},{64,192},{128,0},{192,64},{1,129},{65,193},{129,1},{193,65... | collective-permute-start | bytes 786440 | tf_op jit(solution)/shard_map/ppermute | solution.py:322
  124.3 18.7 %collective-permute-start.19 = (bf16[256,512]{1,0:T(8,128)(2,1)S(1)}, bf16[256,512]{1,0:T(8,128)(2,1)S(1)}, u32[]{:S(2)}, u32[]{:S(2)}) collective-permute-start(bf16[256,512]{1,0:T(8,128)(2,1)S(1)} %get-tuple-element.81), channel_id=1, source_target_pairs={{0,192},{64,0},{128,64},{192,128},{1,193},{65,1},{129,65},{193,129... | collective-permute-start | bytes 786440 | tf_op jit(solution)/shard_map/ppermute | solution.py:322
Sparse Core Ops, SparseCore 0:
  9.9 81.7 all-gather.1

commit v8 on v6

--- a/solution.py
+++ b/solution.py
@@ -12,7 +12,7 @@
 ROWS = 256
 SLAB = 512
 AWAY = (0, 7, 1, 6, 2, 5, 3)
-AHEAD = 3
+AHEAD = 5
 VMEM_LIMIT = 36 * 1024 * 1024
 F32 = jnp.float32
 BF16 = jnp.bfloat16

time: 150 us -> 150 us (level)
  no operation moved by 1% of the time
where the time goes in v8:
time: 150 us; the launch traced here: 149 us
  waiting for transfers between devices  36.2 us (24%)
  starting transfers between devices  31.6 us (21%)
  local copies, waits for them, and re-layouts  22.4 us (15%)
  blocking collectives  17 us (11%)
  Pallas kernels  16.2 us (11%)
  between operations  13.8 us (9%)
  matrix products  9.1 us (6%)
  other arithmetic  3.03 us (2%)
    ppermute x14, waiting for transfers between devices, ring(): return lax.ppermute(value, 'z', [(i, (i + by) % NZ) for i in range(NZ)])  26 us
    ppermute x14, starting transfers between devices, ring(): return lax.ppermute(value, 'z', [(i, (i + by) % NZ) for i in range(NZ)])  21.3 us
    all_to_all x1, blocking collectives, body(): own_ends = lax.all_to_all(to_send, ('y', 'c', 'x'), 0, 0, tiled=True)  17 us
    ppermute x6, starting transfers between devices, round_x(): return lax.ppermute(value, 'x', [(i, (i + by) % NX) for i in range(NX)])  10.4 us
    ppermute x6, waiting for transfers between devices, round_x(): return lax.ppermute(value, 'x', [(i, (i + by) % NX) for i in range(NX)])  10.1 us
    pallas_call x1, Pallas kernels, product(): pl.pallas_call(product_kernel, grid_spec=pltpu.PrefetchScalarGridSpec(num...  7.89 us
    dot_general x1, matrix products, tables(): gains = jnp.einsum('ka,jkab->kbj', readout, powers, precision=PRECISE)  5.44 us
    unnamed x19, local copies, waits for them, and re-layouts  5.11 us
  transfers between devices with their start and end apart: 21, of which 7 were waited for; matrix products, arithmetic and copies ran while one was open for 21% of the time, Pallas kernels for 5%

profile of v8, /device:TPU:1, one launch (start us, length us, event | category | flops | bytes accessed | tf_op | source)
XLA Modules:
  0.0 149.3 jit_solution(11330438923175905783)
XLA Ops:
  6.5 2.0 %constant_dynamic-slice_fusion.1 = bf16[32,8192]{1,0:T(8,128)(2,1)} fusion(bf16[256,8192]{1,0:T(8,128)(2,1)} %param.6, s32[]{:T(128)S(6)} %select_n.71), kind=kLoop, calls=%fused_computation.62 | loop fusion | bytes 1048580 | tf_op jit(solution)/shard_map/dynamic_slice | solution.py:334
  8.7 2.1 %collective-permute-start = (bf16[256,512]{1,0:T(8,128)(2,1)S(1)}, bf16[256,512]{1,0:T(8,128)(2,1)S(1)}, u32[]{:S(2)}, u32[]{:S(2)}) collective-permute-start(bf16[256,512]{1,0:T(8,128)(2,1)S(1)} %get-tuple-element.100), channel_id=1, source_target_pairs={{0,64},{64,128},{128,192},{192,0},{1,65},{65,129},{129,193},{193,1... | collective-permute-start | bytes 786440 | tf_op jit(solution)/shard_map/ppermute | solution.py:322
  10.8 2.5 %collective-permute-start.1 = (bf16[256,512]{1,0:T(8,128)(2,1)S(1)}, bf16[256,512]{1,0:T(8,128)(2,1)S(1)}, u32[]{:S(2)}, u32[]{:S(2)}) collective-permute-start(bf16[256,512]{1,0:T(8,128)(2,1)S(1)} %get-tuple-element.102), channel_id=1, source_target_pairs={{0,128},{64,192},{128,0},{192,64},{1,129},{65,193},{129,1},{193,65... | collective-permute-start | bytes 786440 | tf_op jit(solution)/shard_map/ppermute | solution.py:322
  13.2 1.2 collective-permute-start.2
  14.4 1.4 collective-permute-done
  15.8 8.7 %collective-permute-done.1 = bf16[256,512]{1,0:T(8,128)(2,1)S(1)} collective-permute-done((bf16[256,512]{1,0:T(8,128)(2,1)S(1)}, bf16[256,512]{1,0:T(8,128)(2,1)S(1)}, u32[]{:S(2)}, u32[]{:S(2)}) %collective-permute-start.1) | collective-permute-done | bytes 262176 | tf_op jit(solution)/shard_map/ppermute | solution.py:322
  24.7 1.7 %collective-permute-start.3 = (bf16[1024,256]{1,0:T(8,128)(2,1)S(1)}, bf16[1024,256]{1,0:T(8,128)(2,1)S(1)}, u32[]{:S(2)}, u32[]{:S(2)}) collective-permute-start(bf16[1024,256]{1,0:T(8,128)(2,1)S(1)} %pad_maximum_fusion.refs_0_), channel_id=1, source_target_pairs={{0,8},{8,16},{16,24},{24,32},{32,40},{40,48},{48,56},{56,0},{1,9},... | collective-permute-start | bytes 1572872 | tf_op jit(solution)/shard_map/ppermute | solution.py:318
  26.4 4.0 %collective-permute-start.4 = (bf16[1024,256]{1,0:T(8,128)(2,1)S(1)}, bf16[1024,256]{1,0:T(8,128)(2,1)S(1)}, u32[]{:S(2)}, u32[]{:S(2)}) collective-permute-start(bf16[1024,256]{1,0:T(8,128)(2,1)S(1)} %pad_maximum_fusion.refs_0_), channel_id=1, source_target_pairs={{0,56},{8,0},{16,8},{24,16},{32,24},{40,32},{48,40},{56,48},{1,57}... | collective-permute-start | bytes 1572872 | tf_op jit(solution)/shard_map/ppermute | solution.py:318
  30.4 0.6 pad.40.clone
  31.3 2.7 %collective-permute-start.8 = (bf16[1024,256]{1,0:T(8,128)(2,1)S(1)}, bf16[1024,256]{1,0:T(8,128)(2,1)S(1)}, u32[]{:S(2)}, u32[]{:S(2)}) collective-permute-start(bf16[1024,256]{1,0:T(8,128)(2,1)S(1)} %pad_maximum_fusion.1.refs_1_), channel_id=1, source_target_pairs={{0,56},{8,0},{16,8},{24,16},{32,24},{40,32},{48,40},{56,48},{1,57}... | collective-permute-start | bytes 1572872 | tf_op jit(solution)/shard_map/ppermute | solution.py:318
  34.0 7.0 %collective-permute-done.3.refs_2_ = bf16[1024,256]{1,0:T(8,128)(2,1)S(1)} collective-permute-done((bf16[1024,256]{1,0:T(8,128)(2,1)S(1)}, bf16[1024,256]{1,0:T(8,128)(2,1)S(1)}, u32[]{:S(2)}, u32[]{:S(2)}) %collective-permute-start.3) | collective-permute-done | bytes 524320 | tf_op jit(solution)/shard_map/ppermute | solution.py:318
  41.5 0.5 bitcast_multiply_fusion.4
  42.5 0.7 fusion.23
  43.5 0.2 fusion.24
  44.7 1.0 convolution_bitcast_fusion.4
  45.8 0.2 copy.138
  47.2 0.2 concatenate.55
  47.9 0.2 concatenate.56
  48.5 0.2 concatenate.57
  49.3 2.7 %collective-permute-start.6 = (bf16[1024,256]{1,0:T(8,128)(2,1)S(1)}, bf16[1024,256]{1,0:T(8,128)(2,1)}, u32[]{:S(2)}, u32[]{:S(2)}) collective-permute-start(bf16[1024,256]{1,0:T(8,128)(2,1)S(1)} %collective-permute-done.4.refs_4_), channel_id=1, source_target_pairs={{0,56},{8,0},{16,8},{24,16},{32,24},{40,32},{48,40},{56,48},{1,57}... | collective-permute-start | bytes 1572872 | tf_op jit(solution)/shard_map/ppermute | solution.py:318
  52.0 0.3 collective-permute-done.7.refs_3_
  52.3 2.7 %collective-permute-start.12 = (bf16[1024,256]{1,0:T(8,128)(2,1)S(1)}, bf16[1024,256]{1,0:T(8,128)(2,1)}, u32[]{:S(2)}, u32[]{:S(2)}) collective-permute-start(bf16[1024,256]{1,0:T(8,128)(2,1)S(1)} %collective-permute-done.8.refs_5_), channel_id=1, source_target_pairs={{0,56},{8,0},{16,8},{24,16},{32,24},{40,32},{48,40},{56,48},{1,57}... | collective-permute-start | bytes 1572872 | tf_op jit(solution)/shard_map/ppermute | solution.py:318
  54.9 0.8 fusion.34
  56.1 0.8 fusion.41
  57.0 0.2 multiply_reduce_fusion.power_ref
  57.8 5.4 %fusion.42 = f32[4,1,256,4]{1,2,3,0:T(8,128)} fusion(f32[256,4,4,4]{0,2,3,1:T(4,128)S(1)} %concatenate.57, f32[4,4,1,1]{1,2,3,0:T(1,128)} %bitcast.198), kind=kOutput, calls=%fused_computation.101 | convolution fusion | flops 196608 | bytes 81984 | tf_op jit(solution)/shard_map/ka,jkab->kbj/dot_general | solution.py:56
  63.2 2.2 %copy.182 = f32[4,1,256,4]{2,3,0,1:T(4,128)S(1)} copy(f32[4,1,256,4]{1,2,3,0:T(8,128)} %fusion.42) | data formatting | bytes 32768 | tf_op jit(solution)/shard_map/ka,jkab->kbj/dot_general | solution.py:56
  65.4 1.1 broadcast_bitcast_fusion
  66.5 1.4 collective-permute-start.10
  68.0 4.9 %collective-permute-done.11.refs_7_ = bf16[1024,256]{1,0:T(8,128)(2,1)} collective-permute-done((bf16[1024,256]{1,0:T(8,128)(2,1)S(1)}, bf16[1024,256]{1,0:T(8,128)(2,1)}, u32[]{:S(2)}, u32[]{:S(2)}) %collective-permute-start.11) | collective-permute-done | bytes 524320 | tf_op jit(solution)/shard_map/ppermute | solution.py:318
  72.8 2.5 %collective-permute-start.14 = (bf16[1024,256]{1,0:T(8,128)(2,1)}, bf16[1024,256]{1,0:T(8,128)(2,1)}, u32[]{:S(2)}, u32[]{:S(2)}) collective-permute-start(bf16[1024,256]{1,0:T(8,128)(2,1)} %collective-permute-done.12.refs_9_), channel_id=1, source_target_pairs={{0,56},{8,0},{16,8},{24,16},{32,24},{40,32},{48,40},{56,48},{1,57}... | collective-permute-start | bytes 1572872 | tf_op jit(solution)/shard_map/ppermute | solution.py:318
  75.5 2.1 %copy.191 = bf16[1,4,256,512]{3,1,2,0:T(4,128)(2,1)S(1)} copy(bf16[1,4,256,512]{3,2,1,0:T(8,128)(2,1)} %broadcast_bitcast_fusion) | data formatting | bytes 2097152
  77.6 1.3 slice.132
  79.0 4.1 %reshape.340 = bf16[4,256,511]{2,1,0:T(8,128)(2,1)} reshape(bf16[4,130816]{1,0:T(4,128)(2,1)} %slice.132) | data formatting | bytes 2093056 | tf_op jit(solution)/shard_map/reshape | solution.py:63
  83.0 1.9 %slice.133 = bf16[4,256,256]{2,1,0:T(8,128)(2,1)} slice(bf16[4,256,511]{2,1,0:T(8,128)(2,1)} %reshape.340), slice={[0:4], [0:256], [0:256]} | slice | bytes 1048576 | tf_op jit(solution)/shard_map/slice | solution.py:63
  85.2 0.2 multiply_reduce_fusion.1
  85.5 8.9 %collective-permute-done.14.refs_13_ = bf16[1024,256]{1,0:T(8,128)(2,1)} collective-permute-done((bf16[1024,256]{1,0:T(8,128)(2,1)}, bf16[1024,256]{1,0:T(8,128)(2,1)}, u32[]{:S(2)}, u32[]{:S(2)}) %collective-permute-start.14) | collective-permute-done | bytes 524320 | tf_op jit(solution)/shard_map/ppermute | solution.py:318
  94.4 3.4 %collective-permute-start.15 = (bf16[1024,256]{1,0:T(8,128)(2,1)}, bf16[1024,256]{1,0:T(8,128)(2,1)}, u32[]{:S(2)}, u32[]{:S(2)}) collective-permute-start(bf16[1024,256]{1,0:T(8,128)(2,1)} %collective-permute-done.14.refs_13_), channel_id=1, source_target_pairs={{0,56},{8,0},{16,8},{24,16},{32,24},{40,32},{48,40},{56,48},{1,57}... | collective-permute-start | bytes 1572872 | tf_op jit(solution)/shard_map/ppermute | solution.py:318
  97.8 0.8 copy-done
  98.6 1.0 copy-done.1
  99.6 7.9 %shard_map.64.total_ref = f32[1024,512]{1,0:T(8,128)S(1)} custom-call(s32[9]{0:T(128)S(1)} %stack.92.zs, bf16[4,256,8192]{2,1,0:T(8,128)(2,1)} %bitcast.182, bf16[1024,256]{1,0:T(8,128)(2,1)S(1)} %pad_maximum_fusion.refs_0_, bf16[1024,256]{1,0:T(8,128)(2,1)S(1)} %pad_maximum_fusion.1.refs_1_, bf16[1024,256]{1,0:T(8,128)(2,1)S(1)} %collective-permute-done.3.refs_2_, ...), custom_call_target="tpu_custom_call" | custom-call | flops 4697620480 | bytes 19922944 | tf_op jit(solution)/shard_map/pallas_call | solution.py:160
  107.5 5.0 %collective-permute-done.13.first_ref = bf16[1024,256]{1,0:T(8,128)(2,1)} collective-permute-done((bf16[1024,256]{1,0:T(8,128)(2,1)}, bf16[1024,256]{1,0:T(8,128)(2,1)}, u32[]{:S(2)}, u32[]{:S(2)}) %collective-permute-start.13) | collective-permute-done | bytes 524320 | tf_op jit(solution)/shard_map/ppermute | solution.py:318
  112.5 3.7 %shard_map.65 = (bf16[256,512]{1,0:T(8,128)(2,1)S(1)}, bf16[256,512]{1,0:T(8,128)(2,1)S(1)}, bf16[256,512]{1,0:T(8,128)(2,1)S(1)}, bf16[256,512]{1,0:T(8,128)(2,1)S(1)}, f32[32,4,256]{2,1,0:T(4,128)S(1)}) custom-call(s32[9]{0:T(128)S(1)} %stack.92.zs, bf16[4,256,8192]{2,1,0:T(8,128)(2,1)} %bitcast.183, bf16[1024,256]{1,0:T(8,128)(2,1)} %collective-permute-done.13.first_ref, ...), custom_call_target="tpu_custom_call" | custom-call | flops 738197504 | bytes 6291456 | tf_op jit(solution)/shard_map/pallas_call | solution.py:224
  116.2 0.8 collective-permute-start.17
  117.0 2.0 %collective-permute-start.18 = (bf16[256,512]{1,0:T(8,128)(2,1)S(1)}, bf16[256,512]{1,0:T(8,128)(2,1)S(1)}, u32[]{:S(2)}, u32[]{:S(2)}) collective-permute-start(bf16[256,512]{1,0:T(8,128)(2,1)S(1)} %get-tuple-element.78), channel_id=1, source_target_pairs={{0,128},{64,192},{128,0},{192,64},{1,129},{65,193},{129,1},{193,65... | collective-permute-start | bytes 786440 | tf_op jit(solution)/shard_map/ppermute | solution.py:322
  119.0 1.8 %collective-permute-start.19 = (bf16[256,512]{1,0:T(8,128)(2,1)S(1)}, bf16[256,512]{1,0:T(8,128)(2,1)S(1)}, u32[]{:S(2)}, u32[]{:S(2)}) collective-permute-start(bf16[256,512]{1,0:T(8,128)(2,1)S(1)} %get-tuple-element.79), channel_id=1, source_target_pairs={{0,192},{64,0},{128,64},{192,128},{1,193},{65,1},{129,65},{193,129... | collective-permute-start | bytes 786440 | tf_op jit(solution)/shard_map/ppermute | solution.py:322
  120.8 17.0 %all_to_all.5.slabs_ref = f32[32,4,256]{2,1,0:T(4,128)S(1)} all-to-all(f32[32,4,256]{2,1,0:T(4,128)S(1)} %get-tuple-element.80), channel_id=1, replica_groups=mesh['x'=4,'z'=8,'y'=4,'c'=2] {'y','c','x'}, dimensions={0} | all-to-all | bytes 262144 | tf_op jit(solution)/shard_map/all_to_all | solution.py:381
  137.9 4.6 %shard_map.66 = f32[256,2048]{1,0:T(8,128)} custom-call(s32[2]{0:T(128)S(1)} %pad_add_fusion.place, bf16[256,512]{1,0:T(8,128)(2,1)S(1)} %get-tuple-element.76.own_ref, bf16[256,512]{1,0:T(8,128)(2,1)S(1)} %collective-permute-done.17.by_one_ref, bf16[256,512]{1,0:T(8,128)(2,1)S(1)} %collective-permute-done.18.by_two_ref, ...), custom_call_target="tpu_custom_call" | custom-call | flops 1153433600 | bytes 4194304 | tf_op jit(solution)/shard_map/pallas_call | solution.py:296
  (107 shorter events, 7.0 us)
Async XLA Ops:
  6.5 2.0 %copy-start.3 = (bf16[256,2048]{1,0:T(8,128)(2,1)S(1)}, bf16[256,2048]{1,0:T(8,128)(2,1)}, u32[]{:S(2)}) copy-start(bf16[256,2048]{1,0:T(8,128)(2,1)} %param.7) | copy-start | bytes 3145732
  6.5 92.0 %all-gather.2.cloned.1.call-start = ((), (), s32[]{:S(2)}) async-start(), calls=%async_computation.1 | async-start | bytes 17301504 | tf_op jit(solution)/shard_map/all_gather | solution.py:335
  8.7 7.1 %collective-permute-start = (bf16[256,512]{1,0:T(8,128)(2,1)S(1)}, bf16[256,512]{1,0:T(8,128)(2,1)S(1)}, u32[]{:S(2)}, u32[]{:S(2)}) collective-permute-start(bf16[256,512]{1,0:T(8,128)(2,1)S(1)} %get-tuple-element.100), channel_id=1, source_target_pairs={{0,64},{64,128},{128,192},{192,0},{1,65},{65,129},{129,193},{193,1... | collective-permute-start | bytes 786440 | tf_op jit(solution)/shard_map/ppermute | solution.py:322
  10.8 13.8 %collective-permute-start.1 = (bf16[256,512]{1,0:T(8,128)(2,1)S(1)}, bf16[256,512]{1,0:T(8,128)(2,1)S(1)}, u32[]{:S(2)}, u32[]{:S(2)}) collective-permute-start(bf16[256,512]{1,0:T(8,128)(2,1)S(1)} %get-tuple-element.102), channel_id=1, source_target_pairs={{0,128},{64,192},{128,0},{192,64},{1,129},{65,193},{129,1},{193,65... | collective-permute-start | bytes 786440 | tf_op jit(solution)/shard_map/ppermute | solution.py:322
  13.2 11.3 %collective-permute-start.2 = (bf16[256,512]{1,0:T(8,128)(2,1)S(1)}, bf16[256,512]{1,0:T(8,128)(2,1)S(1)}, u32[]{:S(2)}, u32[]{:S(2)}) collective-permute-start(bf16[256,512]{1,0:T(8,128)(2,1)S(1)} %get-tuple-element.101), channel_id=1, source_target_pairs={{0,192},{64,0},{128,64},{192,128},{1,193},{65,1},{129,65},{193,129... | collective-permute-start | bytes 786440 | tf_op jit(solution)/shard_map/ppermute | solution.py:322
  14.4 26.6 %copy-start.7 = (f32[2,4]{1,0:T(2,128)S(1)}, f32[2,4]{1,0:T(2,128)}, u32[]{:S(2)}) copy-start(f32[2,4]{1,0:T(2,128)} %param.9) | copy-start | bytes 100
  14.4 26.6 %copy-start.6 = (f32[2,4]{1,0:T(2,128)S(1)}, f32[2,4]{1,0:T(2,128)}, u32[]{:S(2)}) copy-start(f32[2,4]{1,0:T(2,128)} %param.10) | copy-start | bytes 100
  14.4 26.8 %copy-start.5 = (f32[4,4]{1,0:T(4,128)S(1)}, f32[4,4]{1,0:T(4,128)}, u32[]{:S(2)}) copy-start(f32[4,4]{1,0:T(4,128)} %param.11) | copy-start | bytes 196
  24.7 16.3 %collective-permute-start.3 = (bf16[1024,256]{1,0:T(8,128)(2,1)S(1)}, bf16[1024,256]{1,0:T(8,128)(2,1)S(1)}, u32[]{:S(2)}, u32[]{:S(2)}) collective-permute-start(bf16[1024,256]{1,0:T(8,128)(2,1)S(1)} %pad_maximum_fusion.refs_0_), channel_id=1, source_target_pairs={{0,8},{8,16},{16,24},{24,32},{32,40},{40,48},{48,56},{56,0},{1,9},... | collective-permute-start | bytes 1572872 | tf_op jit(solution)/shard_map/ppermute | solution.py:318
  26.4 14.6 %collective-permute-start.4 = (bf16[1024,256]{1,0:T(8,128)(2,1)S(1)}, bf16[1024,256]{1,0:T(8,128)(2,1)S(1)}, u32[]{:S(2)}, u32[]{:S(2)}) collective-permute-start(bf16[1024,256]{1,0:T(8,128)(2,1)S(1)} %pad_maximum_fusion.refs_0_), channel_id=1, source_target_pairs={{0,56},{8,0},{16,8},{24,16},{32,24},{40,32},{48,40},{56,48},{1,57}... | collective-permute-start | bytes 1572872 | tf_op jit(solution)/shard_map/ppermute | solution.py:318
  31.0 25.9 %copy-start.4 = (s32[8192]{0:T(1024)S(1)}, s32[8192]{0:T(1024)}, u32[]{:S(2)}) copy-start(s32[8192]{0:T(1024)} %param.8) | copy-start | bytes 98308
  31.2 21.0 %collective-permute-start.7 = (bf16[1024,256]{1,0:T(8,128)(2,1)S(1)}, bf16[1024,256]{1,0:T(8,128)(2,1)S(1)}, u32[]{:S(2)}, u32[]{:S(2)}) collective-permute-start(bf16[1024,256]{1,0:T(8,128)(2,1)S(1)} %pad_maximum_fusion.1.refs_1_), channel_id=1, source_target_pairs={{0,8},{8,16},{16,24},{24,32},{32,40},{40,48},{48,56},{56,0},{1,9},... | collective-permute-start | bytes 1572872 | tf_op jit(solution)/shard_map/ppermute | solution.py:318
  31.3 20.9 %collective-permute-start.8 = (bf16[1024,256]{1,0:T(8,128)(2,1)S(1)}, bf16[1024,256]{1,0:T(8,128)(2,1)S(1)}, u32[]{:S(2)}, u32[]{:S(2)}) collective-permute-start(bf16[1024,256]{1,0:T(8,128)(2,1)S(1)} %pad_maximum_fusion.1.refs_1_), channel_id=1, source_target_pairs={{0,56},{8,0},{16,8},{24,16},{32,24},{40,32},{48,40},{56,48},{1,57}... | collective-permute-start | bytes 1572872 | tf_op jit(solution)/shard_map/ppermute | solution.py:318
  49.2 17.3 %collective-permute-start.5 = (bf16[1024,256]{1,0:T(8,128)(2,1)S(1)}, bf16[1024,256]{1,0:T(8,128)(2,1)}, u32[]{:S(2)}, u32[]{:S(2)}) collective-permute-start(bf16[1024,256]{1,0:T(8,128)(2,1)S(1)} %collective-permute-done.3.refs_2_), channel_id=1, source_target_pairs={{0,8},{8,16},{16,24},{24,32},{32,40},{40,48},{48,56},{56,0},{1,9},... | collective-permute-start | bytes 1572872 | tf_op jit(solution)/shard_map/ppermute | solution.py:318
  49.3 17.2 %collective-permute-start.6 = (bf16[1024,256]{1,0:T(8,128)(2,1)S(1)}, bf16[1024,256]{1,0:T(8,128)(2,1)}, u32[]{:S(2)}, u32[]{:S(2)}) collective-permute-start(bf16[1024,256]{1,0:T(8,128)(2,1)S(1)} %collective-permute-done.4.refs_4_), channel_id=1, source_target_pairs={{0,56},{8,0},{16,8},{24,16},{32,24},{40,32},{48,40},{56,48},{1,57}... | collective-permute-start | bytes 1572872 | tf_op jit(solution)/shard_map/ppermute | solution.py:318
  52.2 20.6 %collective-permute-start.11 = (bf16[1024,256]{1,0:T(8,128)(2,1)S(1)}, bf16[1024,256]{1,0:T(8,128)(2,1)}, u32[]{:S(2)}, u32[]{:S(2)}) collective-permute-start(bf16[1024,256]{1,0:T(8,128)(2,1)S(1)} %collective-permute-done.7.refs_3_), channel_id=1, source_target_pairs={{0,8},{8,16},{16,24},{24,32},{32,40},{40,48},{48,56},{56,0},{1,9},... | collective-permute-start | bytes 1572872 | tf_op jit(solution)/shard_map/ppermute | solution.py:318
  52.3 20.6 %collective-permute-start.12 = (bf16[1024,256]{1,0:T(8,128)(2,1)S(1)}, bf16[1024,256]{1,0:T(8,128)(2,1)}, u32[]{:S(2)}, u32[]{:S(2)}) collective-permute-start(bf16[1024,256]{1,0:T(8,128)(2,1)S(1)} %collective-permute-done.8.refs_5_), channel_id=1, source_target_pairs={{0,56},{8,0},{16,8},{24,16},{32,24},{40,32},{48,40},{56,48},{1,57}... | collective-permute-start | bytes 1572872 | tf_op jit(solution)/shard_map/ppermute | solution.py:318
  66.5 19.0 %collective-permute-start.10 = (bf16[1024,256]{1,0:T(8,128)(2,1)}, bf16[1024,256]{1,0:T(8,128)(2,1)}, u32[]{:S(2)}, u32[]{:S(2)}) collective-permute-start(bf16[1024,256]{1,0:T(8,128)(2,1)} %collective-permute-done.6.refs_8_), channel_id=1, source_target_pairs={{0,56},{8,0},{16,8},{24,16},{32,24},{40,32},{48,40},{56,48},{1,57}... | collective-permute-start | bytes 1572872 | tf_op jit(solution)/shard_map/ppermute | solution.py:318
  67.9 17.6 %collective-permute-start.9 = (bf16[1024,256]{1,0:T(8,128)(2,1)}, bf16[1024,256]{1,0:T(8,128)(2,1)}, u32[]{:S(2)}, u32[]{:S(2)}) collective-permute-start(bf16[1024,256]{1,0:T(8,128)(2,1)} %collective-permute-done.5.refs_6_), channel_id=1, source_target_pairs={{0,8},{8,16},{16,24},{24,32},{32,40},{40,48},{48,56},{56,0},{1,9},... | collective-permute-start | bytes 1572872 | tf_op jit(solution)/shard_map/ppermute | solution.py:318
  72.8 21.5 %collective-permute-start.14 = (bf16[1024,256]{1,0:T(8,128)(2,1)}, bf16[1024,256]{1,0:T(8,128)(2,1)}, u32[]{:S(2)}, u32[]{:S(2)}) collective-permute-start(bf16[1024,256]{1,0:T(8,128)(2,1)} %collective-permute-done.12.refs_9_), channel_id=1, source_target_pairs={{0,56},{8,0},{16,8},{24,16},{32,24},{40,32},{48,40},{56,48},{1,57}... | collective-permute-start | bytes 1572872 | tf_op jit(solution)/shard_map/ppermute | solution.py:318
  85.1 12.7 %collective-permute-start.16 = (bf16[1024,256]{1,0:T(8,128)(2,1)}, bf16[1024,256]{1,0:T(8,128)(2,1)S(1)}, u32[]{:S(2)}, u32[]{:S(2)}) collective-permute-start(bf16[1024,256]{1,0:T(8,128)(2,1)} %collective-permute-done.11.refs_7_), channel_id=1, source_target_pairs={{0,8},{8,16},{16,24},{24,32},{32,40},{40,48},{48,56},{56,0},{1,9},... | collective-permute-start | bytes 1572872 | tf_op jit(solution)/shard_map/ppermute | solution.py:318
  94.4 13.2 %collective-permute-start.15 = (bf16[1024,256]{1,0:T(8,128)(2,1)}, bf16[1024,256]{1,0:T(8,128)(2,1)}, u32[]{:S(2)}, u32[]{:S(2)}) collective-permute-start(bf16[1024,256]{1,0:T(8,128)(2,1)} %collective-permute-done.14.refs_13_), channel_id=1, source_target_pairs={{0,56},{8,0},{16,8},{24,16},{32,24},{40,32},{48,40},{56,48},{1,57}... | collective-permute-start | bytes 1572872 | tf_op jit(solution)/shard_map/ppermute | solution.py:318
  97.8 14.7 %collective-permute-start.13 = (bf16[1024,256]{1,0:T(8,128)(2,1)}, bf16[1024,256]{1,0:T(8,128)(2,1)}, u32[]{:S(2)}, u32[]{:S(2)}) collective-permute-start(bf16[1024,256]{1,0:T(8,128)(2,1)} %collective-permute-done.9.refs_10_), channel_id=1, source_target_pairs={{0,8},{8,16},{16,24},{24,32},{32,40},{40,48},{48,56},{56,0},{1,9},... | collective-permute-start | bytes 1572872 | tf_op jit(solution)/shard_map/ppermute | solution.py:318
  97.8 0.8 copy-start
  98.6 1.0 copy-start.1
  107.5 30.3 %copy-start.2 = (bf16[4,256,256]{2,1,0:T(8,128)(2,1)S(1)}, bf16[4,256,256]{2,1,0:T(8,128)(2,1)}, u32[]{:S(2)}) copy-start(bf16[4,256,256]{2,1,0:T(8,128)(2,1)} %slice.133) | copy-start | bytes 1572868
  116.2 21.6 %collective-permute-start.17 = (bf16[256,512]{1,0:T(8,128)(2,1)S(1)}, bf16[256,512]{1,0:T(8,128)(2,1)S(1)}, u32[]{:S(2)}, u32[]{:S(2)}) collective-permute-start(bf16[256,512]{1,0:T(8,128)(2,1)S(1)} %get-tuple-element.77), channel_id=1, source_target_pairs={{0,64},{64,128},{128,192},{192,0},{1,65},{65,129},{129,193},{193,1... | collective-permute-start | bytes 786440 | tf_op jit(solution)/shard_map/ppermute | solution.py:322
  117.0 20.8 %collective-permute-start.18 = (bf16[256,512]{1,0:T(8,128)(2,1)S(1)}, bf16[256,512]{1,0:T(8,128)(2,1)S(1)}, u32[]{:S(2)}, u32[]{:S(2)}) collective-permute-start(bf16[256,512]{1,0:T(8,128)(2,1)S(1)} %get-tuple-element.78), channel_id=1, source_target_pairs={{0,128},{64,192},{128,0},{192,64},{1,129},{65,193},{129,1},{193,65... | collective-permute-start | bytes 786440 | tf_op jit(solution)/shard_map/ppermute | solution.py:322
  119.0 18.8 %collective-permute-start.19 = (bf16[256,512]{1,0:T(8,128)(2,1)S(1)}, bf16[256,512]{1,0:T(8,128)(2,1)S(1)}, u32[]{:S(2)}, u32[]{:S(2)}) collective-permute-start(bf16[256,512]{1,0:T(8,128)(2,1)S(1)} %get-tuple-element.79), channel_id=1, source_target_pairs={{0,192},{64,0},{128,64},{192,128},{1,193},{65,1},{129,65},{193,129... | collective-permute-start | bytes 786440 | tf_op jit(solution)/shard_map/ppermute | solution.py:322
Sparse Core Ops, SparseCore 0:
  9.9 81.7 all-gather.1
